TPU v7x, 256 devices: a whole 4x4x8 slice. The times are simulated.
256 devices in a mesh: sub: 64 (over z, y, x_hi), dom: 4 (over x_lo, core).
Axes of the slice: x: 4 (x_hi: 2, x_lo: 2; x = x_hi * 2 + x_lo), y: 4, z: 8, core: 2. Of those that a mesh axis runs over, the one named last changes fastest.
Arguments:
- multipliers: bfloat16 [256, 2048, 128], P('sub', 'dom'), may hold values from -6 to 6
- schur_inverse: bfloat16 [256, 2048, 2048], P('sub', 'dom'), may hold values from -0.125 to 0.125
- corner_coupling: bfloat16 [256, 24, 2048], P('sub', None, 'dom'), may hold values from -0.26367188 to 0.26367188
- coarse_inverse: float32 [4096, 4096], P('dom', 'sub'), may hold values from -0.09375 to 0.09375
- partner: int32 [256, 16], P('sub'), may hold values from 0 to 255, as said below
- corner_map: int32 [256, 24], P('sub'), may hold values from 0 to 4095, as said below
Outputs:
- twice: bfloat16 [256, 2048, 128], P('sub', 'dom')
Inputs may be any that keep to these rules, and one draw needn't show every extreme that they name: partner[partner[s, t], t] = s and partner[s, t] != s; the partner lies on the same sub index s // 4, the next or the previous one (cyclically); for each tile slot and sub index at most 2 tiles have a partner on the next sub index and at most 2 on the previous, and both are reached in every draw. `corner_map`: the corners of subdomain s lie in coarse rows (s // 4) * 64 to (s // 4 + 1) * 64 - 1.
All inputs are finite; a program needn't handle non-finite values.
Results may differ from a plain program's by a relative error of at most 0.0055.
Values may be sent and summed in bfloat16 or wider, within the bound.
No kernel may reach another device: no remote copies, remote signals or barrier semaphores. Data moves between devices by JAX's collectives and lax.ppermute only.
A program may use at most 64 MiB of HBM per device.

v0:
```python
import jax
import jax.numpy as jnp
from jax import lax
from jax.sharding import PartitionSpec as P

TILE = 128


def from_root(value, axis, source):
    kept = jnp.where(lax.axis_index(axis) == source, value, 0).astype(value.dtype)
    return lax.psum(kept, axis)


def passed_along(block, axis, distance):
    devices = range(lax.axis_size(axis))
    route = [((i - distance) % len(devices), i) for i in devices]
    return lax.ppermute(block, axis, route)


def body(multipliers, schur_inverse, corner_coupling, coarse_inverse, partner, corner_map):
    n_sub = lax.axis_size("sub")
    sub_index = lax.axis_index("sub")
    dom_index = lax.axis_index("dom")
    sub_dev, block_rows, rhs_cols = multipliers.shape
    tiles_block = block_rows // TILE
    local_tiles = sub_dev * tiles_block
    coarse_block, coarse_dev = coarse_inverse.shape
    partner_block = lax.dynamic_slice_in_dim(partner, dom_index * tiles_block, tiles_block, 1)
    global_ids = sub_index * sub_dev + jnp.arange(sub_dev, dtype=jnp.int32)
    signs = jnp.where(global_ids[:, None] < partner_block, 1.0, -1.0).astype(jnp.float32)
    sign_rows = jnp.repeat(signs, TILE, axis=1)[:, :, None]
    partner_local = partner_block % sub_dev
    relation = ((partner_block // sub_dev - sub_index) % n_sub).reshape(-1)
    slot_grid = jnp.broadcast_to(
        jnp.arange(tiles_block, dtype=jnp.int32)[None, :], (sub_dev, tiles_block)
    )
    tile_source = (partner_local * tiles_block + slot_grid).reshape(-1)
    corner_local = (corner_map - sub_index * coarse_dev).reshape(-1)
    corner_table = (
        corner_local[:, None] == jnp.arange(coarse_dev, dtype=jnp.int32)[None, :]
    ).astype(jnp.float32)
    source = jnp.where(
        relation == 0,
        tile_source,
        jnp.where(relation == 1, 2 * local_tiles + tile_source, local_tiles + tile_source),
    )
    candidate_count = 3 * local_tiles
    selector = (source[:, None] == jnp.arange(candidate_count, dtype=jnp.int32)[None, :]).astype(
        jnp.bfloat16
    )
    coupling_wide = corner_coupling.astype(jnp.float32)

    def apply_once(values):
        signed = (values.astype(jnp.float32) * sign_rows).astype(jnp.bfloat16)
        direct = jnp.einsum(
            "snk,skr->snr",
            schur_inverse,
            lax.all_gather(signed, "dom", axis=1, tiled=True),
            preferred_element_type=jnp.float32,
        )
        local_corner = jnp.einsum(
            "sjk,skr->sjr", corner_coupling, signed, preferred_element_type=jnp.float32
        )
        corner_part = lax.psum(local_corner, "dom")
        coarse_load = jnp.dot(
            corner_table.T, corner_part.reshape(-1, rhs_cols), precision=lax.Precision.HIGHEST
        )
        coarse_term = jnp.dot(coarse_inverse, coarse_load, precision=lax.Precision.HIGHEST)
        coarse_total = lax.psum(coarse_term, "sub")
        root_dom = sub_index * coarse_dev // coarse_block
        offset = jnp.clip(
            sub_index * coarse_dev - dom_index * coarse_block, 0, coarse_block - coarse_dev
        )
        own_rows = lax.dynamic_slice_in_dim(coarse_total, offset, coarse_dev, 0)
        coarse_own = from_root(own_rows, "dom", root_dom)
        corner_values = jnp.dot(corner_table, coarse_own, precision=lax.Precision.HIGHEST).reshape(
            sub_dev, -1, rhs_cols
        )
        back = jnp.einsum(
            "sjn,sjr->snr", coupling_wide, corner_values, precision=lax.Precision.HIGHEST
        )
        solved = (direct + back).astype(jnp.bfloat16)
        solved_tiles = solved.reshape(local_tiles, TILE, rhs_cols)
        arrived_previous = passed_along(solved_tiles, "sub", 1)
        arrived_next = passed_along(solved_tiles, "sub", -1)
        candidates = jnp.concatenate([solved_tiles, arrived_previous, arrived_next], axis=0)
        partner_tiles = jnp.einsum(
            "pq,qtr->ptr", selector, candidates, preferred_element_type=jnp.float32
        )
        result = signs.reshape(-1)[:, None, None] * (
            solved_tiles.astype(jnp.float32) - partner_tiles
        )
        return result.astype(jnp.bfloat16).reshape(sub_dev, block_rows, rhs_cols)

    return apply_once(apply_once(multipliers))


def solution(mesh):
    placed = (
        P("sub", "dom", None),
        P("sub", "dom", None),
        P("sub", None, "dom"),
        P("dom", "sub"),
        P("sub", None),
        P("sub", None),
    )
    return jax.shard_map(
        body, mesh=mesh, in_specs=placed, out_specs=P("sub", "dom", None), check_vma=False
    )
```

profile of v0, /device:TPU:1, one launch (start us, length us, event | category | flops | bytes accessed | tf_op | source)
XLA Modules:
  0.0 1536.8 jit_solution(11752515576676951363)
XLA Ops:
  7.4 0.0 copy-start
  7.4 0.0 all-reduce.3.cloned.1.call-start
  7.4 0.8 compare_select_fusion
  8.2 0.1 broadcast_bitcast_fusion
  8.3 1.2 copy.10
  9.5 0.0 copy-start.4
  9.6 0.1 multiply_convert_fusion.1
  9.7 0.0 copy-start.2
  9.7 0.0 copy-done.3
  9.7 0.2 fusion.58
  9.9 12.9 psum.42
  22.9 0.1 eq.55
  23.0 0.3 fusion.40
  23.3 1.8 convolution_bitcast_fusion.1
  25.1 0.0 all-reduce.3.cloned.1.call-update
  25.1 0.0 all-gather.3.cloned.1.call-start
  25.2 0.5 all-gather.3.cloned.1.call-update
  25.7 0.0 all-reduce.5.cloned.1.call-start
  25.7 0.1 mul.54
  25.8 0.1 broadcast_compare_fusion.2
  25.9 655.5 %all-reduce.3.cloned.1.call-done = f32[1024,128]{1,0:T(8,128)} async-done(((f32[1024,128]{1,0:T(8,128)}), f32[1024,128]{1,0:T(8,128)}) %all-reduce.3.cloned.1.call-update) | async-done | bytes 524304 | tf_op jit(solution)/shard_map/psum | solution.py:69
  681.4 0.8 dynamic-slice_select_fusion.1
  682.1 55.2 %psum.44 = f32[64,128]{1,0:T(8,128)S(1)} all-reduce(f32[64,128]{1,0:T(8,128)S(1)} %dynamic-slice_select_fusion.1), channel_id=1, replica_groups=mesh['sub'=64,'dom'=4] {'dom'}, use_global_device_ids=true, to_apply=%region_2.3 | all-reduce | flops 8192 | bytes 65536 | tf_op jit(solution)/shard_map/psum | solution.py:11
  737.3 0.2 fusion.39
  737.5 0.0 all-gather.3.cloned.1.call-done
  737.6 6.9 fusion.57
  744.5 0.7 fusion.36
  745.2 0.3 copy.12
  745.5 0.3 copy.13
  745.8 0.8 collective-permute-start
  746.7 6.4 collective-permute-start.1
  753.1 0.1 eq.61
  753.2 0.1 eq.63
  753.3 0.1 fusion.53
  753.4 0.1 reshape.65
  753.4 13.7 collective-permute-done
  767.1 4.6 collective-permute-done.1
  771.8 0.4 fusion.32
  772.2 0.3 copy.17
  772.5 0.3 copy.18
  772.9 0.1 multiply_convert_fusion
  773.0 0.0 copy-start.1
  773.0 0.2 fusion.60
  773.2 11.5 psum.45
  784.8 0.3 fusion.38
  785.1 1.8 convolution_bitcast_fusion
  786.9 0.0 all-reduce.5.cloned.1.call-update
  786.9 0.0 all-gather.5.cloned.1.call-start
  787.0 0.5 all-gather.5.cloned.1.call-update
  787.5 650.2 %all-reduce.5.cloned.1.call-done = f32[1024,128]{1,0:T(8,128)} async-done(((f32[1024,128]{1,0:T(8,128)}), f32[1024,128]{1,0:T(8,128)}) %all-reduce.5.cloned.1.call-update) | async-done | bytes 524304 | tf_op jit(solution)/shard_map/psum | solution.py:69
  1437.7 0.8 dynamic-slice_select_fusion
  1438.5 55.2 %psum.47 = f32[64,128]{1,0:T(8,128)S(1)} all-reduce(f32[64,128]{1,0:T(8,128)S(1)} %dynamic-slice_select_fusion), channel_id=1, replica_groups=mesh['sub'=64,'dom'=4] {'dom'}, use_global_device_ids=true, to_apply=%region_5.6 | all-reduce | flops 8192 | bytes 65536 | tf_op jit(solution)/shard_map/psum | solution.py:11
  1493.6 0.2 fusion.37
  1493.9 0.0 all-gather.5.cloned.1.call-done
  1493.9 6.9 fusion.59
  1500.8 0.7 fusion.35
  1501.5 0.3 copy.20
  1501.8 0.3 copy.21
  1502.1 1.0 collective-permute-start.2
  1503.2 6.3 collective-permute-start.3
  1509.4 14.0 collective-permute-done.2
  1523.4 4.6 collective-permute-done.3
  1528.0 0.4 fusion.29
  1528.4 0.9 copy.25
  (12 shorter events, 0.0 us)
Async XLA Ops:
  7.4 15.9 %copy-start = (f32[1024,64]{0,1:T(8,128)S(1)}, f32[1024,64]{0,1:T(8,128)}, u32[]{:S(2)}) copy-start(f32[1024,64]{0,1:T(8,128)} %param.9) | copy-start | bytes 786436
  7.4 2.3 copy-start.3
  7.4 15.5 %copy-start.5 = (s32[4,24]{1,0:T(4,128)S(1)}, s32[4,24]{1,0:T(4,128)}, u32[]{:S(2)}) copy-start(s32[4,24]{1,0:T(4,128)} %param.11) | copy-start | bytes 1156
  7.4 674.0 %all-reduce.3.cloned.1.call-start = ((), (), s32[]{:S(2)}) async-start(), calls=%async_computation.1 | async-start | bytes 1048576 | tf_op jit(solution)/shard_map/psum | solution.py:69
  9.5 16.3 %copy-start.4 = (s32[4,16]{1,0:T(4,128)S(1)}, s32[4,16]{1,0:T(4,128)}, u32[]{:S(2)}) copy-start(s32[4,16]{1,0:T(4,128)} %param.10) | copy-start | bytes 772
  9.7 15.5 %copy-start.2 = (bf16[4,512,128]{1,2,0:T(8,128)(2,1)}, bf16[4,512,128]{1,2,0:T(8,128)(2,1)S(1)}, u32[]{:S(2)}) copy-start(bf16[4,512,128]{1,2,0:T(8,128)(2,1)S(1)} %multiply_convert_fusion.1) | copy-start | bytes 1572868
  25.1 712.5 %all-gather.3.cloned.1.call-start = ((), (), s32[]{:S(2)}) async-start(), calls=%async_computation | async-start | bytes 2621440 | tf_op jit(solution)/shard_map/all_gather | solution.py:58
  25.7 1412.0 %all-reduce.5.cloned.1.call-start = ((), (), s32[]{:S(2)}) async-start(), calls=%async_computation.3 | async-start | bytes 1048576 | tf_op jit(solution)/shard_map/psum | solution.py:69
  745.8 21.3 %collective-permute-start = (bf16[16,128,128]{2,0,1:T(8,128)(2,1)S(1)}, bf16[16,128,128]{2,0,1:T(8,128)(2,1)S(1)}, u32[]{:S(2)}, u32[]{:S(2)}) collective-permute-start(bf16[16,128,128]{2,0,1:T(8,128)(2,1)S(1)} %copy.13), channel_id=1, source_target_pairs={{252,0},{0,4},{4,8},{8,12},{12,16},{16,20},{20,24},{24,28},{28,32}... | collective-permute-start | bytes 1572872 | tf_op jit(solution)/shard_map/ppermute | solution.py:17
  746.7 25.1 %collective-permute-start.1 = (bf16[16,128,128]{2,0,1:T(8,128)(2,1)S(1)}, bf16[16,128,128]{2,0,1:T(8,128)(2,1)S(1)}, u32[]{:S(2)}, u32[]{:S(2)}) collective-permute-start(bf16[16,128,128]{2,0,1:T(8,128)(2,1)S(1)} %copy.13), channel_id=1, source_target_pairs={{4,0},{8,4},{12,8},{16,12},{20,16},{24,20},{28,24},{32,28},{36,32}... | collective-permute-start | bytes 1572872 | tf_op jit(solution)/shard_map/ppermute | solution.py:17
  773.0 14.0 copy-start.1
  786.9 707.0 %all-gather.5.cloned.1.call-start = ((), (), s32[]{:S(2)}) async-start(), calls=%async_computation.2 | async-start | bytes 2621440 | tf_op jit(solution)/shard_map/all_gather | solution.py:58
  1502.1 21.3 %collective-permute-start.2 = (bf16[16,128,128]{2,0,1:T(8,128)(2,1)S(1)}, bf16[16,128,128]{2,0,1:T(8,128)(2,1)S(1)}, u32[]{:S(2)}, u32[]{:S(2)}) collective-permute-start(bf16[16,128,128]{2,0,1:T(8,128)(2,1)S(1)} %copy.21), channel_id=1, source_target_pairs={{252,0},{0,4},{4,8},{8,12},{12,16},{16,20},{20,24},{24,28},{28,32}... | collective-permute-start | bytes 1572872 | tf_op jit(solution)/shard_map/ppermute | solution.py:17
  1503.2 24.9 %collective-permute-start.3 = (bf16[16,128,128]{2,0,1:T(8,128)(2,1)S(1)}, bf16[16,128,128]{2,0,1:T(8,128)(2,1)S(1)}, u32[]{:S(2)}, u32[]{:S(2)}) collective-permute-start(bf16[16,128,128]{2,0,1:T(8,128)(2,1)S(1)} %copy.21), channel_id=1, source_target_pairs={{4,0},{8,4},{12,8},{16,12},{20,16},{24,20},{28,24},{32,28},{36,32}... | collective-permute-start | bytes 1572872 | tf_op jit(solution)/shard_map/ppermute | solution.py:17
Sparse Core Ops, SparseCore 0:
  25.2 656.1 all-reduce.2
  787.0 650.6 all-reduce.4
Sparse Core Ops, SparseCore 1:
  27.4 35.0 all-gather.2
  789.3 29.5 all-gather.4
where the time goes:
time: 1540 us
  waiting for transfers between devices  1340 us (87%)
  blocking collectives  135 us (9%)
  matrix products  21.1 us (1%)
    psum x2, waiting for transfers between devices, apply_once(): coarse_total = lax.psum(coarse_term, 'sub')  1310 us
    psum x2, blocking collectives, from_root(): return lax.psum(kept, axis)  110 us
    ppermute x4, waiting for transfers between devices, passed_along(): return lax.ppermute(block, axis, route)  36.9 us
  transfers between devices with their start and end apart: 8, of which 6 were waited for; matrix products, arithmetic and copies ran while one was open for 0% of the time, Pallas kernels for 0%

commit v1 on v0

v1 whole, which is shorter than its diff:
```python
import functools

import jax
import jax.numpy as jnp
from jax import lax
from jax.experimental import pallas as pl
from jax.experimental.pallas import tpu as pltpu
from jax.sharding import PartitionSpec as P

TILE = 128
F32 = jnp.float32
BF16 = jnp.bfloat16
SMEM = pltpu.SMEM
VMEM_BYTES = 40 * 1024 * 1024


def shifted(block, axis, distance):
    n = lax.axis_size(axis)
    return lax.ppermute(block, axis, [(i, (i + distance) % n) for i in range(n)])


def swapped(block, axis, mask):
    n = lax.axis_size(axis)
    return lax.ppermute(block, axis, [(i, i ^ mask) for i in range(n)])


def halves(x):
    high = lax.reduce_precision(x, 8, 7)
    return high.astype(BF16), (x - high).astype(BF16)


def dot(a, b, dims=((1,), (0,)), precision=None):
    return lax.dot_general(a, b, (dims, ((), ())), precision=precision, preferred_element_type=F32)


def product_kernel(slots, with_coupling, order, after, before, s_ref, u0, u1, u2, u3, *refs):
    if with_coupling:
        coupling, direct_ref, to_after, to_before = refs
    else:
        direct_ref, to_after, to_before = refs
    step = pl.program_id(0)
    depth = u0.shape[1]

    @pl.when(step == 0)
    def _():
        to_after[...] = jnp.zeros_like(to_after)
        to_before[...] = jnp.zeros_like(to_before)

    total = None
    for place, piece in enumerate((u0, u1, u2, u3)):
        columns = pl.ds(pl.multiple_of(order[place] * depth, depth), depth)
        term = dot(s_ref[0, :, columns], piece[0])
        total = term if total is None else total + term
    direct_ref[...] = total.reshape(direct_ref.shape)
    for t in range(slots):
        for index, target in ((after, to_after), (before, to_before)):
            place = index[step * slots + t]

            @pl.when(place >= 0)
            def _(t=t, place=place, target=target):
                tile = total[t * TILE : (t + 1) * TILE]
                target[pl.ds(place, 1), :TILE] = tile.astype(BF16)[None]
                if with_coupling:
                    target[pl.ds(place, 1), TILE:] = coupling[pl.ds(t, 1)]


def product(schur_inverse, pieces, order, after, before, coupling_tiles):
    sub_dev, rows, cols = schur_inverse.shape
    depth, rhs = pieces[0].shape[1:]
    slots = rows // TILE
    extra = 0 if coupling_tiles is None else coupling_tiles.shape[1]
    packed = jax.ShapeDtypeStruct((2 * slots, TILE + extra, rhs), BF16)
    whole = pl.BlockSpec(packed.shape, lambda i: (0, 0, 0))
    operands = [order, after, before, schur_inverse, *pieces]
    in_specs = [pl.BlockSpec(memory_space=SMEM)] * 3
    in_specs += [pl.BlockSpec((1, rows, cols), lambda i: (i, 0, 0))]
    in_specs += [pl.BlockSpec((1, depth, rhs), lambda i: (i, 0, 0))] * 4
    if extra:
        operands.append(coupling_tiles)
        in_specs.append(pl.BlockSpec((slots, extra, TILE), lambda i: (i, 0, 0)))
    return pl.pallas_call(
        functools.partial(product_kernel, slots, bool(extra)),
        grid=(sub_dev,),
        in_specs=in_specs,
        out_specs=[pl.BlockSpec((slots, TILE, rhs), lambda i: (i, 0, 0)), whole, whole],
        out_shape=[jax.ShapeDtypeStruct((sub_dev * slots, TILE, rhs), F32), packed, packed],
        compiler_params=pltpu.CompilerParams(vmem_limit_bytes=VMEM_BYTES),
        cost_estimate=pl.CostEstimate(
            flops=2 * sub_dev * rows * cols * rhs, bytes_accessed=2 * sub_dev * rows * cols, transcendentals=0
        ),
    )(*operands)


def difference_kernel(kind, index, direct, from_before, from_after, coupling, delta, spread, load):
    n_tiles, dofs = coupling.shape[:2]
    rhs = direct.shape[2]
    total = None
    for p in range(n_tiles):
        mine = coupling[p].astype(F32)
        blank = jnp.zeros((dofs, TILE), BF16)
        where, which = kind[p], index[p]

        @pl.when(where == 0)
        def _(p=p, which=which, mine=mine, blank=blank):
            delta[p] = direct[p] - direct[which]
            other = mine - coupling[which].astype(F32)
            spread[p] = jnp.concatenate([blank, other.astype(BF16), blank], axis=0)

        @pl.when(where == 1)
        def _(p=p, which=which, blank=blank):
            delta[p] = direct[p] - from_after[which, :TILE].astype(F32)
            spread[p] = jnp.concatenate([blank, coupling[p], -from_after[which, TILE:]], axis=0)

        @pl.when(where == 2)
        def _(p=p, which=which, blank=blank):
            delta[p] = direct[p] - from_before[which, :TILE].astype(F32)
            spread[p] = jnp.concatenate([-from_before[which, TILE:], coupling[p], blank], axis=0)

        first = dot(coupling[p], delta[p].astype(BF16))
        second = dot(coupling[p], spread[p], ((1,), (1,)))
        part = jnp.concatenate([first, second], axis=1)
        total = part if total is None else total + part
    load[...] = total


def difference(kind, index, direct, from_before, from_after, coupling):
    n_tiles, dofs, _ = coupling.shape
    rhs = direct.shape[2]
    vmem = pl.BlockSpec(memory_space=pltpu.VMEM)
    return pl.pallas_call(
        difference_kernel,
        in_specs=[pl.BlockSpec(memory_space=SMEM)] * 2 + [vmem] * 4,
        out_specs=[vmem] * 3,
        out_shape=[
            jax.ShapeDtypeStruct((n_tiles, TILE, rhs), F32),
            jax.ShapeDtypeStruct((n_tiles, 3 * dofs, TILE), BF16),
            jax.ShapeDtypeStruct((dofs, rhs + 3 * dofs), F32),
        ],
        compiler_params=pltpu.CompilerParams(vmem_limit_bytes=VMEM_BYTES),
        cost_estimate=pl.CostEstimate(flops=10**8, bytes_accessed=3 * 10**6, transcendentals=0),
    )(kind, index, direct, from_before, from_after, coupling)


def split(x):
    high = x.astype(BF16)
    return high, (x - high.astype(F32)).astype(BF16)


def applied(spread, high, low):
    return dot(spread, high, ((0,), (0,))) + dot(spread, low, ((0,), (0,)))


def next_kernel(coarse_parts, load_parts, delta, spread, u_ref, load_ref):
    coarse = (coarse_parts[0] + coarse_parts[1]) + (coarse_parts[2] + coarse_parts[3])
    high, low = split(coarse)
    rhs = coarse.shape[1]
    load = (load_parts[0] + load_parts[1]) + (load_parts[2] + load_parts[3])
    load = load[:, :rhs] + dot(load[:, rhs:], coarse, precision=lax.Precision.HIGHEST)
    load_ref[...] = load.astype(BF16)
    for p in range(delta.shape[0]):
        u_ref[p] = (delta[p] + applied(spread[p], high, low)).astype(BF16)


def next_values(coarse_parts, load_parts, delta, spread):
    vmem = pl.BlockSpec(memory_space=pltpu.VMEM)
    return pl.pallas_call(
        next_kernel,
        in_specs=[vmem] * 4,
        out_specs=[vmem] * 2,
        out_shape=[
            jax.ShapeDtypeStruct(delta.shape, BF16),
            jax.ShapeDtypeStruct((load_parts.shape[1], delta.shape[2]), BF16),
        ],
        compiler_params=pltpu.CompilerParams(vmem_limit_bytes=VMEM_BYTES),
        cost_estimate=pl.CostEstimate(flops=10**8, bytes_accessed=3 * 10**6, transcendentals=0),
    )(coarse_parts, load_parts, delta, spread)


def last_kernel(kind, index, signs, coarse_parts, direct, from_before, from_after, spread, out):
    coarse = (coarse_parts[0] + coarse_parts[1]) + (coarse_parts[2] + coarse_parts[3])
    high, low = split(coarse)
    for p in range(direct.shape[0]):
        where, which = kind[p], index[p]
        base = direct[p] + applied(spread[p], high, low)

        @pl.when(where == 0)
        def _(p=p, which=which, base=base):
            out[p] = (signs[p] * (base - direct[which])).astype(BF16)

        @pl.when(where == 1)
        def _(p=p, which=which, base=base):
            out[p] = (signs[p] * (base - from_after[which].astype(F32))).astype(BF16)

        @pl.when(where == 2)
        def _(p=p, which=which, base=base):
            out[p] = (signs[p] * (base - from_before[which].astype(F32))).astype(BF16)


def last_values(kind, index, signs, coarse_parts, direct, from_before, from_after, spread):
    vmem = pl.BlockSpec(memory_space=pltpu.VMEM)
    return pl.pallas_call(
        last_kernel,
        in_specs=[pl.BlockSpec(memory_space=SMEM)] * 3 + [vmem] * 5,
        out_specs=vmem,
        out_shape=jax.ShapeDtypeStruct(direct.shape, BF16),
        compiler_params=pltpu.CompilerParams(vmem_limit_bytes=VMEM_BYTES),
        cost_estimate=pl.CostEstimate(flops=10**8, bytes_accessed=3 * 10**6, transcendentals=0),
    )(kind, index, signs, coarse_parts, direct, from_before, from_after, spread)


def body(multipliers, schur_inverse, corner_coupling, coarse_inverse, partner, corner_map):
    n_sub = lax.axis_size("sub")
    n_dom = lax.axis_size("dom")
    sub = lax.axis_index("sub")
    dom = lax.axis_index("dom")
    sub_dev, block_rows, rhs = multipliers.shape
    slots = block_rows // TILE
    n_tiles = sub_dev * slots
    coarse_block, coarse_dev = coarse_inverse.shape
    share = coarse_dev // n_dom

    partners = lax.dynamic_slice_in_dim(partner, dom * slots, slots, 1)
    ids = sub * sub_dev + jnp.arange(sub_dev, dtype=jnp.int32)
    signs = jnp.where(ids[:, None] < partners, 1.0, -1.0).astype(F32)
    sign_rows = jnp.repeat(signs, TILE, axis=1)[:, :, None]
    local = partners % sub_dev
    relation = (partners // sub_dev - sub) % n_sub
    kind = jnp.where(relation == 0, 0, jnp.where(relation == 1, 1, 2)).astype(jnp.int32)
    slot_ids = jnp.arange(slots, dtype=jnp.int32)[None]
    same_kind = kind[None] == kind[:, None]
    subs = jnp.arange(sub_dev, dtype=jnp.int32)
    earlier = same_kind & (subs[None] < subs[:, None])[:, :, None]
    lower = same_kind & (local[None] < local[:, None])
    sent = jnp.sum(earlier.astype(jnp.int32), axis=1) * slots + slot_ids
    got = jnp.sum(lower.astype(jnp.int32), axis=1) * slots + slot_ids
    after = jnp.where(kind == 1, sent, -1).reshape(-1)
    before = jnp.where(kind == 2, sent, -1).reshape(-1)
    index = jnp.where(kind == 0, local * slots + slot_ids, got).reshape(-1)
    kind = kind.reshape(-1)
    order = dom ^ jnp.arange(n_dom, dtype=jnp.int32)

    corner_local = corner_map - sub * coarse_dev
    corner_table = (
        corner_local[:, :, None] == jnp.arange(coarse_dev, dtype=jnp.int32)[None, None]
    ).astype(BF16)
    coupling = jnp.einsum(
        "sjk,sjn->skn", corner_table, corner_coupling, preferred_element_type=F32
    ).astype(BF16)
    coupling_tiles = (
        coupling.reshape(sub_dev, coarse_dev, slots, TILE)
        .transpose(0, 2, 1, 3)
        .reshape(n_tiles, coarse_dev, TILE)
    )

    def gathered(u):
        far = swapped(u, "dom", 2)
        return u, swapped(u, "dom", 1), far, swapped(far, "dom", 1)

    def coarse_parts(k_rows, load_rows):
        part = jnp.einsum("kr,kx->rx", k_rows, load_rows, preferred_element_type=F32)
        return lax.all_gather(part, "dom", axis=0)

    u1 = (multipliers.astype(F32) * sign_rows).astype(BF16)
    pieces1 = gathered(u1)
    high, low = halves(jnp.einsum("skn,snr->kr", coupling, u1, preferred_element_type=F32))
    inverse_t = coarse_inverse.T.astype(BF16)
    to_dom = jnp.concatenate([inverse_t, high, low], axis=1)
    by_dom = lax.all_to_all(to_dom, "dom", 0, 0, tiled=True).reshape(n_dom, share, -1)
    load1 = jnp.sum(by_dom[:, :, coarse_block:].astype(F32), axis=0)
    load1 = (load1[:, :rhs] + load1[:, rhs:]).astype(BF16)
    blocks = by_dom[:, :, :coarse_block].reshape(n_dom, share, -1, 2 * coarse_dev)
    blocks = blocks.transpose(0, 2, 1, 3).reshape(-1, share, 2 * coarse_dev)
    twice_each = jnp.repeat(blocks, 2, axis=0)
    to_sub = jnp.stack(
        [
            jnp.roll(twice_each, 1, axis=0),
            jnp.roll(twice_each, -1, axis=0),
            jnp.broadcast_to(load1[None], (n_sub, share, rhs)),
        ],
        axis=1,
    )
    by_sub = lax.all_to_all(to_sub, "sub", 0, 0, tiled=True)
    direct1, to_after, to_before = product(
        schur_inverse, pieces1, order, after, before, coupling_tiles
    )
    got_before, got_after = shifted(to_after, "sub", 1), shifted(to_before, "sub", -1)
    by_sub, direct1 = lax.optimization_barrier((by_sub, direct1))
    k_wide = jnp.concatenate([by_sub[:, 0], by_sub[:, 1]], axis=2).reshape(n_sub * share, -1)
    offset = jnp.where(sub % 2 == 0, coarse_dev, 0)
    k_rows = lax.dynamic_slice_in_dim(k_wide, offset, 3 * coarse_dev, 1)
    coarse1 = coarse_parts(k_rows, by_sub[:, 2].reshape(n_sub * share, rhs))
    delta1, spread, load2 = difference(
        kind, index, direct1, got_before, got_after, coupling_tiles
    )
    load2 = lax.all_to_all(load2, "dom", 0, 0, tiled=True).reshape(n_dom, share, -1)

    u2, load2 = next_values(coarse1, load2, delta1, spread)
    pieces2 = gathered(u2.reshape(sub_dev, block_rows, rhs))
    by_sub2 = lax.all_to_all(
        jnp.broadcast_to(load2[None], (n_sub, share, rhs)), "sub", 0, 0, tiled=True
    )
    direct2, to_after2, to_before2 = product(
        schur_inverse, pieces2, order, after, before, None
    )
    got_before2, got_after2 = shifted(to_after2, "sub", 1), shifted(to_before2, "sub", -1)
    by_sub2, direct2 = lax.optimization_barrier((by_sub2, direct2))
    coarse2 = coarse_parts(k_rows, by_sub2.reshape(n_sub * share, rhs))
    result = last_values(
        kind, index, signs.reshape(-1), coarse2, direct2, got_before2, got_after2, spread
    )
    return result.reshape(sub_dev, block_rows, rhs)


def solution(mesh):
    placed = (
        P("sub", "dom", None),
        P("sub", "dom", None),
        P("sub", None, "dom"),
        P("dom", "sub"),
        P("sub", None),
        P("sub", None),
    )
    return jax.shard_map(
        body, mesh=mesh, in_specs=placed, out_specs=P("sub", "dom", None), check_vma=False
    )
```

time: 1540 us -> 150 us (0.10)
  waiting for transfers between devices: 1340 us -> 32.2 us
  blocking collectives: 135 us -> 15.5 us
  starting transfers between devices: 14.7 us -> 55 us
  matrix products: 21.1 us -> 3.85 us
  Pallas kernels: 0 us -> 17 us
    psum x2 -> x0, waiting for transfers between devices: 1310 us -> none  [apply_once(): coarse_total = lax.psum(coarse_term, 'sub')]
    psum x4 -> x0, blocking collectives: 135 us -> none  [the longest x2 110 us: from_root(): return lax.psum(kept, axis)]
    all_to_all x0 -> x4, starting transfers between devices: none -> 34.5 us  [the longest x1 12.8 us: body(): by_sub = lax.all_to_all(to_sub, 'sub', 0, 0, tiled=True)]
    dot_general x14 -> x4, matrix products: 21.1 us -> 3.85 us  [the longest x2 3.29 us: coarse_parts(): jnp.einsum('kr,kx->rx', k_rows, load_rows, preferred_element_type=F32)]
    pallas_call x0 -> x5, Pallas kernels: none -> 17 us  [the longest x2 8.47 us: product(): pl.pallas_call(functools.partial(product_kernel, slots, bool(extra)), gri...]
    all_gather x0 -> x2, blocking collectives: none -> 15.5 us  [coarse_parts(): return lax.all_gather(part, 'dom', axis=0)]
    ppermute x4 -> x10, waiting for transfers between devices: 36.9 us -> 28.4 us  [the longest x4 14.9 us: shifted(): lax.ppermute(block, axis, [(i, (i + distance) % n) for i in range(n)])]
  transfers between devices with their start and end apart: 8 -> 14, of which waited for: 6 -> 7; matrix products, arithmetic and copies ran while one was open for 0% -> 5% of each run, Pallas kernels for 0% -> 6%
where the time goes in v1:
time: 150 us
  starting transfers between devices  55 us (37%)
  waiting for transfers between devices  32.2 us (21%)
  local copies, waits for them, and re-layouts  20 us (13%)
  Pallas kernels  17 us (11%)
  blocking collectives  15.5 us (10%)
  other arithmetic  5.81 us (4%)
  matrix products  3.85 us (3%)
    unnamed x33, local copies, waits for them, and re-layouts  16.6 us
    all_gather x2, blocking collectives, coarse_parts(): return lax.all_gather(part, 'dom', axis=0)  15.5 us
    ppermute x4, waiting for transfers between devices, shifted(): lax.ppermute(block, axis, [(i, (i + distance) % n) for i in range(n)])  14.9 us
    ppermute x4, starting transfers between devices, shifted(): lax.ppermute(block, axis, [(i, (i + distance) % n) for i in range(n)])  14.4 us
    ppermute x6, waiting for transfers between devices, swapped(): return lax.ppermute(block, axis, [(i, i ^ mask) for i in range(n)])  13.5 us
    all_to_all x1, starting transfers between devices, body(): by_sub = lax.all_to_all(to_sub, 'sub', 0, 0, tiled=True)  12.8 us
    all_to_all x1, starting transfers between devices, body(): lax.all_to_all(jnp.broadcast_to(load2[None], (n_sub, share, rhs)), 'sub',...  11.1 us
    pallas_call x2, Pallas kernels, product(): pl.pallas_call(functools.partial(product_kernel, slots, bool(extra)), gri...  8.47 us
  transfers between devices with their start and end apart: 14, of which 7 were waited for; matrix products, arithmetic and copies ran while one was open for 5% of the time, Pallas kernels for 6%

profile of v1, /device:TPU:1, one launch (start us, length us, event | category | flops | bytes accessed | tf_op | source)
XLA Modules:
  0.0 149.6 jit_solution(5238152325993875536)
XLA Ops:
  0.0 0.8 compare_select_fusion.2
  0.8 0.1 broadcast_bitcast_fusion
  0.9 1.0 convert_bitcast_fusion
  1.9 0.7 broadcast_subtract_fusion
  2.6 0.3 convolution_convert_fusion
  2.9 1.4 multiply_convert_fusion.u0
  4.3 0.2 reduce-precision_convert_fusion
  4.5 0.7 pad_maximum_fusion.2
  5.2 6.6 %all-to-all-start = ((bf16[4,16,1280]{2,1,0:T(8,128)(2,1)}), bf16[4,16,1280]{2,1,0:T(8,128)(2,1)S(1)}, u32[]{:S(2)}, u32[]{:S(2)}) async-start(bf16[4,16,1280]{2,1,0:T(8,128)(2,1)} %bitcast.2), calls=%async_computation | async-start | bytes 327680 | tf_op jit(solution)/shard_map/all_to_all | solution.py:268
  11.8 1.4 collective-permute-start.1
  13.2 2.5 %all-to-all-done = bf16[4,16,1280]{2,1,0:T(8,128)(2,1)S(1)} async-done(((bf16[4,16,1280]{2,1,0:T(8,128)(2,1)}), bf16[4,16,1280]{2,1,0:T(8,128)(2,1)S(1)}, u32[]{:S(2)}, u32[]{:S(2)}) %all-to-all-start) | async-done | bytes 163872 | tf_op jit(solution)/shard_map/all_to_all | solution.py:268
  15.8 0.1 fusion.11
  16.0 1.0 pad_maximum_fusion
  17.0 12.8 %all-to-all-start.1 = ((bf16[64,3,16,128]{3,2,1,0:T(8,128)(2,1)}), bf16[64,3,16,128]{3,2,1,0:T(8,128)(2,1)}, u32[]{:S(2)}, u32[]{:S(2)}) async-start(bf16[64,3,16,128]{3,2,1,0:T(8,128)(2,1)} %pad_maximum_fusion), calls=%async_computation.1 | async-start | bytes 1572864 | tf_op jit(solution)/shard_map/all_to_all | solution.py:282
  29.8 1.9 %collective-permute-start = (bf16[4,512,128]{2,1,0:T(8,128)(2,1)S(1)}, bf16[4,512,128]{2,1,0:T(8,128)(2,1)S(1)}, u32[]{:S(2)}, u32[]{:S(2)}) collective-permute-start(bf16[4,512,128]{2,1,0:T(8,128)(2,1)S(1)} %multiply_convert_fusion.u0), channel_id=1, source_target_pairs={{0,1},{1,0},{2,3},{3,2},{4,5},{5,4},{6,7},{7,6},{8,9},{9,8},{10,11... | collective-permute-start | bytes 1572872 | tf_op jit(solution)/shard_map/ppermute | solution.py:24
  31.7 0.1 add_select_fusion
  31.8 0.1 convert_reduce_fusion.1
  31.9 0.1 collective-permute-start.2
  32.1 0.1 reshape.79.after
  32.1 0.1 reshape.80.before
  32.2 0.1 fusion.9
  32.3 0.9 collective-permute-done.u1
  33.3 0.7 collective-permute-done.2.u3
  34.0 0.8 copy-done.3
  34.8 3.4 %copy-done.1 = bf16[4,512,2048]{2,1,0:T(8,128)(2,1)S(1)} copy-done((bf16[4,512,2048]{2,1,0:T(8,128)(2,1)S(1)}, bf16[4,512,2048]{2,1,0:T(8,128)(2,1)}, u32[]{:S(2)}) %copy-start.1) | copy-done | bytes 8388632
  38.2 1.0 copy-done.4
  39.2 4.7 %shard_map.64 = (f32[16,128,128]{2,1,0:T(8,128)S(1)}, bf16[8,192,128]{2,1,0:T(8,128)(2,1)}, bf16[8,192,128]{2,1,0:T(8,128)(2,1)}) custom-call(s32[4]{0:T(128)S(1)} %iota_xor_fusion.order, s32[16]{0:T(128)S(1)} %reshape.79.after, s32[16]{0:T(128)S(1)} %reshape.80.before, bf16[4,512,2048]{2,1,0:T(8,128)(2,1)S(1)} %copy-done.1, ...), custom_call_target="tpu_custom_call" | custom-call | flops 1073741824 | bytes 8388608 | tf_op jit(solution)/shard_map/pallas_call | solution.py:81
  43.9 2.7 %collective-permute-start.3 = (bf16[8,192,128]{2,1,0:T(8,128)(2,1)}, bf16[8,192,128]{2,1,0:T(8,128)(2,1)S(1)}, u32[]{:S(2)}, u32[]{:S(2)}) collective-permute-start(bf16[8,192,128]{2,1,0:T(8,128)(2,1)} %get-tuple-element.23), channel_id=1, source_target_pairs={{0,4},{4,8},{8,12},{12,16},{16,20},{20,24},{24,28},{28,32},{32,36}... | collective-permute-start | bytes 1179656 | tf_op jit(solution)/shard_map/ppermute | solution.py:19
  46.7 4.5 %collective-permute-start.4 = (bf16[8,192,128]{2,1,0:T(8,128)(2,1)}, bf16[8,192,128]{2,1,0:T(8,128)(2,1)S(1)}, u32[]{:S(2)}, u32[]{:S(2)}) collective-permute-start(bf16[8,192,128]{2,1,0:T(8,128)(2,1)} %get-tuple-element.24), channel_id=1, source_target_pairs={{0,252},{4,0},{8,4},{12,8},{16,12},{20,16},{24,20},{28,24},{32,28}... | collective-permute-start | bytes 1179656 | tf_op jit(solution)/shard_map/ppermute | solution.py:19
  51.2 0.1 reshape.73.kind
  51.3 0.1 reshape.74.index
  51.4 13.0 %collective-permute-done.3.from_before = bf16[8,192,128]{2,1,0:T(8,128)(2,1)S(1)} collective-permute-done((bf16[8,192,128]{2,1,0:T(8,128)(2,1)}, bf16[8,192,128]{2,1,0:T(8,128)(2,1)S(1)}, u32[]{:S(2)}, u32[]{:S(2)}) %collective-permute-start.3) | collective-permute-done | bytes 393248 | tf_op jit(solution)/shard_map/ppermute | solution.py:19
  64.3 0.7 copy-done.9
  65.1 1.9 %collective-permute-done.4.from_after = bf16[8,192,128]{2,1,0:T(8,128)(2,1)S(1)} collective-permute-done((bf16[8,192,128]{2,1,0:T(8,128)(2,1)}, bf16[8,192,128]{2,1,0:T(8,128)(2,1)S(1)}, u32[]{:S(2)}, u32[]{:S(2)}) %collective-permute-start.4) | collective-permute-done | bytes 393248 | tf_op jit(solution)/shard_map/ppermute | solution.py:19
  67.0 0.8 copy-done.11
  67.8 1.0 copy-done.10
  68.8 1.0 copy-done.12
  69.7 2.8 %shard_map.65 = (f32[16,128,128]{2,1,0:T(8,128)S(1)}, bf16[16,192,128]{2,1,0:T(8,128)(2,1)S(1)}, f32[64,320]{1,0:T(8,128)}) custom-call(s32[16]{0:T(128)S(1)} %reshape.73.kind, s32[16]{0:T(128)S(1)} %reshape.74.index, f32[16,128,128]{2,1,0:T(8,128)S(1)} %get-tuple-element.22.direct, bf16[8,192,128]{2,1,0:T(8,128)(2,1)S(1)} %copy-done.10, ...), custom_call_target="tpu_custom_call" | custom-call | flops 100000000 | bytes 3000000 | tf_op jit(solution)/shard_map/pallas_call | solution.py:130
  72.5 4.0 %all-to-all-start.2 = ((f32[4,16,320]{2,1,0:T(8,128)}), f32[4,16,320]{2,1,0:T(8,128)S(1)}, u32[]{:S(2)}, u32[]{:S(2)}) async-start(f32[4,16,320]{2,1,0:T(8,128)} %bitcast.14), calls=%async_computation.2 | async-start | bytes 196608 | tf_op jit(solution)/shard_map/all_to_all | solution.py:295
  76.5 2.1 %fusion.8 = (bf16[64,1,16,128]{3,2,1,0:T(8,128)(2,1)}, bf16[64,1,16,128]{3,2,1,0:T(8,128)(2,1)S(1)}, bf16[64,1,16,128]{3,2,1,0:T(8,128)(2,1)}) fusion(bf16[64,3,16,128]{3,2,1,0:T(8,128)(2,1)} %all-to-all-done.1), kind=kLoop, calls=%fused_computation.50 | loop fusion | bytes 1572864 | tf_op jit(solution)/shard_map/slice | solution.py:288
  78.6 1.6 %fusion.6 = f32[192,128]{1,0:T(8,128)S(1)} fusion(bf16[1024,128]{1,0:T(8,128)(2,1)S(1)} %bitcast.53, s32[]{:T(128)S(6)} %select_n.63, bf16[1024,128]{1,0:T(8,128)(2,1)} %bitcast.11, bf16[1024,128]{1,0:T(8,128)(2,1)} %bitcast.10), kind=kOutput, calls=%fused_computation.48 | convolution fusion | flops 51118080 | bytes 884740 | tf_op jit(solution)/shard_map/kr,kx->rx/dot_general | solution.py:260
  80.2 6.8 %all-gather = f32[768,128]{1,0:T(8,128)S(1)} all-gather(f32[192,128]{1,0:T(8,128)S(1)} %fusion.6), channel_id=2, replica_groups=mesh['sub'=64,'dom'=4] {'dom'}, dimensions={0}, use_global_device_ids=true | all-gather | bytes 491520 | tf_op jit(solution)/shard_map/all_gather | solution.py:261
  87.1 0.8 shard_map.66
  87.9 1.2 collective-permute-start.6
  89.1 0.4 collective-permute-start.5
  89.5 11.8 %collective-permute-done.6.u2 = bf16[4,512,128]{2,1,0:T(8,128)(2,1)S(1)} collective-permute-done((bf16[4,512,128]{2,1,0:T(8,128)(2,1)S(1)}, bf16[4,512,128]{2,1,0:T(8,128)(2,1)S(1)}, u32[]{:S(2)}, u32[]{:S(2)}) %collective-permute-start.6) | collective-permute-done | bytes 524320 | tf_op jit(solution)/shard_map/ppermute | solution.py:24
  101.3 1.0 collective-permute-start.7
  102.3 0.7 broadcast_in_dim.27
  103.0 11.1 %all-to-all-start.3 = ((bf16[64,16,128]{2,1,0:T(8,128)(2,1)}), bf16[64,16,128]{2,1,0:T(8,128)(2,1)}, u32[]{:S(2)}, u32[]{:S(2)}) async-start(bf16[64,16,128]{2,1,0:T(8,128)(2,1)} %broadcast_in_dim.27), calls=%async_computation.3 | async-start | bytes 524288 | tf_op jit(solution)/shard_map/all_to_all | solution.py:299
  114.1 0.1 reshape.75.signs
  114.2 0.8 copy-done.5
  115.0 0.8 copy-done.7
  115.8 3.4 %copy-done.2 = bf16[4,512,2048]{2,1,0:T(8,128)(2,1)S(1)} copy-done((bf16[4,512,2048]{2,1,0:T(8,128)(2,1)S(1)}, bf16[4,512,2048]{2,1,0:T(8,128)(2,1)}, u32[]{:S(2)}) %copy-start.2) | copy-done | bytes 8388632
  119.2 1.0 copy-done.6
  120.3 1.0 copy-done.8
  121.3 3.8 %shard_map.67 = (f32[16,128,128]{2,1,0:T(8,128)S(1)}, bf16[8,128,128]{2,1,0:T(8,128)(2,1)S(1)}, bf16[8,128,128]{2,1,0:T(8,128)(2,1)S(1)}) custom-call(s32[4]{0:T(128)S(1)} %iota_xor_fusion.order, s32[16]{0:T(128)S(1)} %reshape.79.after, s32[16]{0:T(128)S(1)} %reshape.80.before, bf16[4,512,2048]{2,1,0:T(8,128)(2,1)S(1)} %copy-done.2, ...), custom_call_target="tpu_custom_call" | custom-call | flops 1073741824 | bytes 8388608 | tf_op jit(solution)/shard_map/pallas_call | solution.py:81
  125.1 0.0 copy-start.13
  125.1 0.7 copy-done.13
  125.8 1.3 all-to-all-done.3
  127.1 1.2 collective-permute-start.8
  128.2 6.0 %collective-permute-start.9 = (bf16[8,128,128]{2,1,0:T(8,128)(2,1)S(1)}, bf16[8,128,128]{2,1,0:T(8,128)(2,1)S(1)}, u32[]{:S(2)}, u32[]{:S(2)}) collective-permute-start(bf16[8,128,128]{2,1,0:T(8,128)(2,1)S(1)} %get-tuple-element.34), channel_id=1, source_target_pairs={{0,252},{4,0},{8,4},{12,8},{16,12},{20,16},{24,20},{28,24},{32,28}... | collective-permute-start | bytes 786440 | tf_op jit(solution)/shard_map/ppermute | solution.py:19
  134.2 1.7 %fusion.7 = f32[192,128]{1,0:T(8,128)S(1)} fusion(bf16[1024,128]{1,0:T(8,128)(2,1)} %bitcast.16, s32[]{:T(128)S(6)} %select_n.63, bf16[1024,128]{1,0:T(8,128)(2,1)} %bitcast.11, bf16[1024,128]{1,0:T(8,128)(2,1)} %bitcast.10), kind=kOutput, calls=%fused_computation.49 | convolution fusion | flops 51118080 | bytes 884740 | tf_op jit(solution)/shard_map/kr,kx->rx/dot_general | solution.py:260
  135.9 8.7 %all-gather.1 = f32[768,128]{1,0:T(8,128)S(1)} all-gather(f32[192,128]{1,0:T(8,128)S(1)} %fusion.7), channel_id=3, replica_groups=mesh['sub'=64,'dom'=4] {'dom'}, dimensions={0}, use_global_device_ids=true | all-gather | bytes 491520 | tf_op jit(solution)/shard_map/all_gather | solution.py:261
  144.6 4.9 %shard_map.68 = bf16[16,128,128]{2,1,0:T(8,128)(2,1)} custom-call(s32[16]{0:T(128)S(1)} %reshape.73.kind, s32[16]{0:T(128)S(1)} %reshape.74.index, f32[16]{0:T(128)S(1)} %reshape.75.signs, f32[4,192,128]{2,1,0:T(8,128)S(1)} %bitcast.43, f32[16,128,128]{2,1,0:T(8,128)S(1)} %get-tuple-element.32.direct, ...), custom_call_target="tpu_custom_call" | custom-call | flops 100000000 | bytes 3000000 | tf_op jit(solution)/shard_map/pallas_call | solution.py:201
  (39 shorter events, 0.3 us)
Async XLA Ops:
  0.0 2.6 %copy-start = (bf16[4,24,512]{2,1,0:T(8,128)(2,1)S(1)}, bf16[4,24,512]{2,1,0:T(8,128)(2,1)}, u32[]{:S(2)}) copy-start(bf16[4,24,512]{2,1,0:T(8,128)(2,1)} %param.8) | copy-start | bytes 294916
  0.0 31.7 %copy-start.14 = (s32[4,16]{1,0:T(4,128)S(1)}, s32[4,16]{1,0:T(4,128)}, u32[]{:S(2)}) copy-start(s32[4,16]{1,0:T(4,128)} %param.10) | copy-start | bytes 772
  5.2 10.4 %all-to-all-start = ((bf16[4,16,1280]{2,1,0:T(8,128)(2,1)}), bf16[4,16,1280]{2,1,0:T(8,128)(2,1)S(1)}, u32[]{:S(2)}, u32[]{:S(2)}) async-start(bf16[4,16,1280]{2,1,0:T(8,128)(2,1)} %bitcast.2), calls=%async_computation | async-start | bytes 327680 | tf_op jit(solution)/shard_map/all_to_all | solution.py:268
  11.8 20.2 %collective-permute-start.1 = (bf16[4,512,128]{2,1,0:T(8,128)(2,1)S(1)}, bf16[4,512,128]{2,1,0:T(8,128)(2,1)S(1)}, u32[]{:S(2)}, u32[]{:S(2)}) collective-permute-start(bf16[4,512,128]{2,1,0:T(8,128)(2,1)S(1)} %multiply_convert_fusion.u0), channel_id=1, source_target_pairs={{0,2},{1,3},{2,0},{3,1},{4,6},{5,7},{6,4},{7,5},{8,10},{9,11},{10,... | collective-permute-start | bytes 1572872 | tf_op jit(solution)/shard_map/ppermute | solution.py:24
  17.0 34.4 %all-to-all-start.1 = ((bf16[64,3,16,128]{3,2,1,0:T(8,128)(2,1)}), bf16[64,3,16,128]{3,2,1,0:T(8,128)(2,1)}, u32[]{:S(2)}, u32[]{:S(2)}) async-start(bf16[64,3,16,128]{3,2,1,0:T(8,128)(2,1)} %pad_maximum_fusion), calls=%async_computation.1 | async-start | bytes 1572864 | tf_op jit(solution)/shard_map/all_to_all | solution.py:282
  29.8 3.5 %collective-permute-start = (bf16[4,512,128]{2,1,0:T(8,128)(2,1)S(1)}, bf16[4,512,128]{2,1,0:T(8,128)(2,1)S(1)}, u32[]{:S(2)}, u32[]{:S(2)}) collective-permute-start(bf16[4,512,128]{2,1,0:T(8,128)(2,1)S(1)} %multiply_convert_fusion.u0), channel_id=1, source_target_pairs={{0,1},{1,0},{2,3},{3,2},{4,5},{5,4},{6,7},{7,6},{8,9},{9,8},{10,11... | collective-permute-start | bytes 1572872 | tf_op jit(solution)/shard_map/ppermute | solution.py:24
  31.9 2.1 %collective-permute-start.2 = (bf16[4,512,128]{2,1,0:T(8,128)(2,1)S(1)}, bf16[4,512,128]{2,1,0:T(8,128)(2,1)S(1)}, u32[]{:S(2)}, u32[]{:S(2)}) collective-permute-start(bf16[4,512,128]{2,1,0:T(8,128)(2,1)S(1)} %collective-permute-done.1.u2), channel_id=1, source_target_pairs={{0,1},{1,0},{2,3},{3,2},{4,5},{5,4},{6,7},{7,6},{8,9},{9,8},{10,11... | collective-permute-start | bytes 1572872 | tf_op jit(solution)/shard_map/ppermute | solution.py:24
  34.0 0.8 copy-start.3
  34.8 3.4 %copy-start.1 = (bf16[4,512,2048]{2,1,0:T(8,128)(2,1)S(1)}, bf16[4,512,2048]{2,1,0:T(8,128)(2,1)}, u32[]{:S(2)}) copy-start(bf16[4,512,2048]{2,1,0:T(8,128)(2,1)} %s_ref.3) | copy-start | bytes 25165828
  38.2 1.0 copy-start.4
  43.9 20.4 %collective-permute-start.3 = (bf16[8,192,128]{2,1,0:T(8,128)(2,1)}, bf16[8,192,128]{2,1,0:T(8,128)(2,1)S(1)}, u32[]{:S(2)}, u32[]{:S(2)}) collective-permute-start(bf16[8,192,128]{2,1,0:T(8,128)(2,1)} %get-tuple-element.23), channel_id=1, source_target_pairs={{0,4},{4,8},{8,12},{12,16},{16,20},{20,24},{24,28},{28,32},{32,36}... | collective-permute-start | bytes 1179656 | tf_op jit(solution)/shard_map/ppermute | solution.py:19
  46.7 20.3 %collective-permute-start.4 = (bf16[8,192,128]{2,1,0:T(8,128)(2,1)}, bf16[8,192,128]{2,1,0:T(8,128)(2,1)S(1)}, u32[]{:S(2)}, u32[]{:S(2)}) collective-permute-start(bf16[8,192,128]{2,1,0:T(8,128)(2,1)} %get-tuple-element.24), channel_id=1, source_target_pairs={{0,252},{4,0},{8,4},{12,8},{16,12},{20,16},{24,20},{28,24},{32,28}... | collective-permute-start | bytes 1179656 | tf_op jit(solution)/shard_map/ppermute | solution.py:19
  64.3 0.7 copy-start.9
  67.0 0.8 copy-start.11
  67.8 1.0 copy-start.10
  68.8 1.0 copy-start.12
  72.5 14.5 %all-to-all-start.2 = ((f32[4,16,320]{2,1,0:T(8,128)}), f32[4,16,320]{2,1,0:T(8,128)S(1)}, u32[]{:S(2)}, u32[]{:S(2)}) async-start(f32[4,16,320]{2,1,0:T(8,128)} %bitcast.14), calls=%async_computation.2 | async-start | bytes 196608 | tf_op jit(solution)/shard_map/all_to_all | solution.py:295
  87.9 13.5 %collective-permute-start.6 = (bf16[4,512,128]{2,1,0:T(8,128)(2,1)S(1)}, bf16[4,512,128]{2,1,0:T(8,128)(2,1)S(1)}, u32[]{:S(2)}, u32[]{:S(2)}) collective-permute-start(bf16[4,512,128]{2,1,0:T(8,128)(2,1)S(1)} %bitcast.45), channel_id=1, source_target_pairs={{0,2},{1,3},{2,0},{3,1},{4,6},{5,7},{6,4},{7,5},{8,10},{9,11},{10,... | collective-permute-start | bytes 1572872 | tf_op jit(solution)/shard_map/ppermute | solution.py:24
  89.1 25.1 %collective-permute-start.5 = (bf16[4,512,128]{2,1,0:T(8,128)(2,1)S(1)}, bf16[4,512,128]{2,1,0:T(8,128)(2,1)S(1)}, u32[]{:S(2)}, u32[]{:S(2)}) collective-permute-start(bf16[4,512,128]{2,1,0:T(8,128)(2,1)S(1)} %bitcast.46), channel_id=1, source_target_pairs={{0,1},{1,0},{2,3},{3,2},{4,5},{5,4},{6,7},{7,6},{8,9},{9,8},{10,11... | collective-permute-start | bytes 1572872 | tf_op jit(solution)/shard_map/ppermute | solution.py:24
  101.3 13.7 %collective-permute-start.7 = (bf16[4,512,128]{2,1,0:T(8,128)(2,1)S(1)}, bf16[4,512,128]{2,1,0:T(8,128)(2,1)S(1)}, u32[]{:S(2)}, u32[]{:S(2)}) collective-permute-start(bf16[4,512,128]{2,1,0:T(8,128)(2,1)S(1)} %collective-permute-done.6.u2), channel_id=1, source_target_pairs={{0,1},{1,0},{2,3},{3,2},{4,5},{5,4},{6,7},{7,6},{8,9},{9,8},{10,11... | collective-permute-start | bytes 1572872 | tf_op jit(solution)/shard_map/ppermute | solution.py:24
  103.0 24.0 %all-to-all-start.3 = ((bf16[64,16,128]{2,1,0:T(8,128)(2,1)}), bf16[64,16,128]{2,1,0:T(8,128)(2,1)}, u32[]{:S(2)}, u32[]{:S(2)}) async-start(bf16[64,16,128]{2,1,0:T(8,128)(2,1)} %broadcast_in_dim.27), calls=%async_computation.3 | async-start | bytes 524288 | tf_op jit(solution)/shard_map/all_to_all | solution.py:299
  114.2 0.8 copy-start.5
  115.0 0.8 copy-start.7
  115.8 3.4 %copy-start.2 = (bf16[4,512,2048]{2,1,0:T(8,128)(2,1)S(1)}, bf16[4,512,2048]{2,1,0:T(8,128)(2,1)}, u32[]{:S(2)}) copy-start(bf16[4,512,2048]{2,1,0:T(8,128)(2,1)} %s_ref.3) | copy-start | bytes 25165828
  119.2 1.0 copy-start.6
  120.3 1.0 copy-start.8
  125.1 0.7 copy-start.13
  127.1 17.6 %collective-permute-start.8 = (bf16[8,128,128]{2,1,0:T(8,128)(2,1)}, bf16[8,128,128]{2,1,0:T(8,128)(2,1)S(1)}, u32[]{:S(2)}, u32[]{:S(2)}) collective-permute-start(bf16[8,128,128]{2,1,0:T(8,128)(2,1)} %copy-done.13), channel_id=1, source_target_pairs={{0,4},{4,8},{8,12},{12,16},{16,20},{20,24},{24,28},{28,32},{32,36}... | collective-permute-start | bytes 786440 | tf_op jit(solution)/shard_map/ppermute | solution.py:19
  128.2 16.4 %collective-permute-start.9 = (bf16[8,128,128]{2,1,0:T(8,128)(2,1)S(1)}, bf16[8,128,128]{2,1,0:T(8,128)(2,1)S(1)}, u32[]{:S(2)}, u32[]{:S(2)}) collective-permute-start(bf16[8,128,128]{2,1,0:T(8,128)(2,1)S(1)} %get-tuple-element.34), channel_id=1, source_target_pairs={{0,252},{4,0},{8,4},{12,8},{16,12},{20,16},{24,20},{28,24},{32,28}... | collective-permute-start | bytes 786440 | tf_op jit(solution)/shard_map/ppermute | solution.py:19

commit v2 on v0

v2 whole, which is shorter than its diff:
```python
import functools

import jax
import jax.numpy as jnp
from jax import lax
from jax.experimental import pallas as pl
from jax.experimental.pallas import tpu as pltpu
from jax.sharding import PartitionSpec as P

TILE = 128
F32 = jnp.float32
BF16 = jnp.bfloat16
VMEM_BYTES = 24 * 1024 * 1024
MOST_VMEM_BYTES = 59 * 1024 * 1024
IN_SMEM = pl.BlockSpec(memory_space=pltpu.SMEM)
IN_VMEM = pl.BlockSpec(memory_space=pltpu.VMEM)


def like(shape, dtype):
    return jax.ShapeDtypeStruct(shape, dtype)


def params(limit=VMEM_BYTES):
    return pltpu.CompilerParams(vmem_limit_bytes=limit)


def cost(flops, moved):
    return pl.CostEstimate(flops=flops, bytes_accessed=moved, transcendentals=0)


def shifted(block, axis, distance):
    n = lax.axis_size(axis)
    return lax.ppermute(block, axis, [(i, (i + distance) % n) for i in range(n)])


def swapped(block, axis, mask):
    n = lax.axis_size(axis)
    return lax.ppermute(block, axis, [(i, i ^ mask) for i in range(n)])


def dot(a, b, dims=((1,), (0,))):
    return lax.dot_general(a, b, (dims, ((), ())), preferred_element_type=F32)


def split(x):
    high = x.astype(BF16)
    return high, (x - high.astype(F32)).astype(BF16)


def exact_dot(a, b):
    a_high, a_low = split(a)
    b_high, b_low = split(b)
    return dot(a_high, b_high) + (dot(a_high, b_low) + dot(a_low, b_high))


def applied(spread, high, low):
    return dot(spread, high, ((0,), (0,))) + dot(spread, low, ((0,), (0,)))


def partial_rows(got, load, part):
    height, half = got.shape[2], load.shape[0]
    for d in range(got.shape[0]):
        for h in range(2):
            at = (2 * d + h) * height
            block = got[d, :height, h * half : (h + 1) * half]
            part[at : at + height] = exact_dot(block, load).astype(BF16)


def first_kernel(got, part):
    height = got.shape[2]
    load = (got[0, height:] + got[1, height:]) + (got[2, height:] + got[3, height:])
    partial_rows(got, load, part)


def first_part(got):
    rows = 2 * got.shape[0] * got.shape[2]
    return pl.pallas_call(
        first_kernel,
        in_specs=[IN_VMEM],
        out_specs=IN_VMEM,
        out_shape=like((rows, got.shape[2]), BF16),
        compiler_params=params(),
        cost_estimate=cost(10**7, 10**6),
    )(got)


def pack_tiles(after, before, to_after, to_before, tile_at):
    sub_dev, slots = after.shape
    to_after[...] = jnp.zeros_like(to_after)
    to_before[...] = jnp.zeros_like(to_before)
    for i in range(sub_dev):
        for t in range(slots):
            for table, target in ((after, to_after), (before, to_before)):
                place = table[i, t]

                @pl.when(place >= 0)
                def _(i=i, t=t, place=place, target=target):
                    target[pl.ds(place, 1)] = tile_at(i, t).astype(BF16)[None]


def pack_kernel(after, before, coupling, to_after, to_before):
    def tile_at(i, t):
        return coupling[i, :, t * TILE : (t + 1) * TILE]

    pack_tiles(after, before, to_after, to_before, tile_at)


def packed_coupling(after, before, coupling):
    packed = like((2 * after.shape[1], coupling.shape[1], TILE), BF16)
    return pl.pallas_call(
        pack_kernel,
        in_specs=[IN_SMEM] * 2 + [IN_VMEM],
        out_specs=[IN_VMEM] * 2,
        out_shape=[packed, packed],
        compiler_params=params(),
        cost_estimate=cost(10**5, 10**6),
    )(after, before, coupling)


def product_kernel(first, *refs):
    if first:
        after, before, signs, s_ref, u0, u1, u2, u3, direct_ref, to_after, to_before = refs
    else:
        s_ref, u0, u1, u2, u3, direct_ref = refs
    depth, rhs = u0.shape[1:]
    slots = direct_ref.shape[0]
    dom = lax.axis_index("dom")
    step = pl.program_id(0)
    total = None
    for m, piece in enumerate((u0, u1, u2, u3)):
        place = dom ^ m
        values = piece[0]
        if first:
            values = jnp.concatenate(
                [
                    (values[t * TILE : (t + 1) * TILE].astype(F32) * signs[step, place * slots + t]).astype(
                        BF16
                    )
                    for t in range(slots)
                ],
                axis=0,
            )
        columns = pl.ds(pl.multiple_of(place * depth, depth), depth)
        term = dot(s_ref[0, :, columns], values)
        total = term if total is None else total + term
    direct_ref[...] = total.reshape(slots, TILE, rhs)
    if first:

        @pl.when(step == 0)
        def _():
            to_after[...] = jnp.zeros_like(to_after)
            to_before[...] = jnp.zeros_like(to_before)

        for t in range(slots):
            for table, target in ((after, to_after), (before, to_before)):
                place = table[step, t]

                @pl.when(place >= 0)
                def _(t=t, place=place, target=target):
                    target[pl.ds(place, 1)] = direct_ref[pl.ds(t, 1)].astype(BF16)


def product(schur_inverse, pieces, tables=()):
    sub_dev, rows, cols = schur_inverse.shape
    depth, rhs = pieces[0].shape[1:]
    slots = rows // TILE
    first = bool(tables)
    out_shape = [like((sub_dev * slots, TILE, rhs), F32)]
    out_specs = [pl.BlockSpec((slots, TILE, rhs), lambda i: (i, 0, 0))]
    if first:
        packed = (2 * slots, TILE, rhs)
        out_shape += [like(packed, BF16)] * 2
        out_specs += [pl.BlockSpec(packed, lambda i: (0, 0, 0))] * 2
    return pl.pallas_call(
        functools.partial(product_kernel, first),
        grid=(sub_dev,),
        in_specs=[IN_SMEM] * len(tables)
        + [pl.BlockSpec((1, rows, cols), lambda i: (i, 0, 0))]
        + [pl.BlockSpec((1, depth, rhs), lambda i: (i, 0, 0))] * len(pieces),
        out_specs=out_specs,
        out_shape=out_shape,
        compiler_params=params(MOST_VMEM_BYTES),
        cost_estimate=cost(2 * sub_dev * rows * cols * rhs, 2 * sub_dev * rows * cols),
    )(*tables, schur_inverse, *pieces)


def weighted_kernel(after, before, r0, r1, r2, r3, direct, coupling, w_ref, to_after, to_before, coarse):
    share = r0.shape[0]
    dom = lax.axis_index("dom")
    for m, rows in enumerate((r0, r1, r2, r3)):
        coarse[pl.ds(pl.multiple_of((dom ^ m) * share, share), share)] = rows[...]
    high, low = split(coarse[...])
    sub_dev = coupling.shape[0]
    slots = direct.shape[0] // sub_dev
    for i in range(sub_dev):
        for t in range(slots):
            own = coupling[i, :, t * TILE : (t + 1) * TILE]
            w_ref[i * slots + t] = (direct[i * slots + t] + applied(own, high, low)).astype(BF16)
    pack_tiles(after, before, to_after, to_before, lambda i, t: w_ref[i * slots + t])


def weighted(after, before, rows, direct, coupling):
    rhs = direct.shape[2]
    packed = (2 * after.shape[1], TILE, rhs)
    return pl.pallas_call(
        weighted_kernel,
        in_specs=[IN_SMEM] * 2 + [IN_VMEM] * 6,
        out_specs=[IN_VMEM] * 3,
        out_shape=[like(direct.shape, BF16), like(packed, BF16), like(packed, BF16)],
        scratch_shapes=[pltpu.VMEM((4 * rows[0].shape[0], rhs), F32)],
        compiler_params=params(),
        cost_estimate=cost(10**8, 3 * 10**6),
    )(after, before, *rows, direct, coupling)


def spread_kernel(kind, index, coupling, from_before, from_after, spread, second):
    sub_dev, dofs, _ = coupling.shape
    slots = kind.shape[1]
    blank = jnp.zeros((dofs, TILE), BF16)
    total = None
    for i in range(sub_dev):
        for t in range(slots):
            p = i * slots + t
            columns = slice(t * TILE, (t + 1) * TILE)
            mine = coupling[i, :, columns]
            where, which = kind[i, t], index[i, t]
            spread[p, :dofs] = blank
            spread[p, dofs : 2 * dofs] = mine
            spread[p, 2 * dofs :] = blank

            @pl.when(where == 0)
            def _(p=p, i=i, which=which, columns=columns):
                other = coupling[i, :, columns].astype(F32) - coupling[which, :, columns].astype(F32)
                spread[p, dofs : 2 * dofs] = other.astype(BF16)

            @pl.when(where == 1)
            def _(p=p, which=which):
                spread[p, 2 * dofs :] = -from_after[which]

            @pl.when(where == 2)
            def _(p=p, which=which):
                spread[p, :dofs] = -from_before[which]

            term = dot(mine, spread[p], ((1,), (1,)))
            total = term if total is None else total + term
    second[:dofs] = total[:, :TILE]
    second[dofs:] = jnp.concatenate([total[:, TILE:], jnp.zeros_like(total[:, TILE:])], axis=1)


def spread_of(kind, index, coupling, from_before, from_after):
    sub_dev, dofs, cols = coupling.shape
    n_tiles = sub_dev * cols // TILE
    return pl.pallas_call(
        spread_kernel,
        in_specs=[IN_SMEM] * 2 + [IN_VMEM] * 3,
        out_specs=[IN_VMEM] * 2,
        out_shape=[like((n_tiles, 3 * dofs, TILE), BF16), like((2 * dofs, TILE), F32)],
        compiler_params=params(),
        cost_estimate=cost(10**8, 2 * 10**6),
    )(kind, index, coupling, from_before, from_after)


def difference_kernel(
    kind, index, r0, r1, r2, direct, from_before, from_after, coupling, second, delta, sent
):
    sub_dev, dofs, _ = coupling.shape
    slots = kind.shape[1]
    share = r0.shape[0]
    for b, rows in enumerate((r0, r1, r2)):
        sent[b * share : (b + 1) * share] = rows[...]
    at = 3 * share
    sent[at + dofs :] = second[...]
    total = None
    for i in range(sub_dev):
        for t in range(slots):
            p = i * slots + t
            where, which = kind[i, t], index[i, t]

            @pl.when(where == 0)
            def _(p=p, t=t, which=which):
                delta[p] = direct[p] - direct[which * slots + t]

            @pl.when(where == 1)
            def _(p=p, which=which):
                delta[p] = direct[p] - from_after[which].astype(F32)

            @pl.when(where == 2)
            def _(p=p, which=which):
                delta[p] = direct[p] - from_before[which].astype(F32)

            term = dot(coupling[i, :, t * TILE : (t + 1) * TILE], delta[p].astype(BF16))
            total = term if total is None else total + term
    sent[at : at + dofs] = total


def difference(kind, index, rows, direct, from_before, from_after, coupling, second):
    rhs = direct.shape[2]
    dofs = coupling.shape[1]
    return pl.pallas_call(
        difference_kernel,
        in_specs=[IN_SMEM] * 2 + [IN_VMEM] * 8,
        out_specs=[IN_VMEM] * 2,
        out_shape=[
            like(direct.shape, F32),
            like((3 * rows[0].shape[0] + dofs + second.shape[0], rhs), F32),
        ],
        compiler_params=params(),
        cost_estimate=cost(10**8, 3 * 10**6),
    )(kind, index, *rows, direct, from_before, from_after, coupling, second)


def coarse_rows(got, share):
    return jnp.concatenate(
        [got[d, b * share : (b + 1) * share] for b in range(3) for d in range(got.shape[0])], axis=0
    )


def next_kernel(share, dofs, got, delta, spread, inverse, u_ref, part):
    coarse = coarse_rows(got, share)
    at = 3 * share
    total = (got[0, at:] + got[1, at:]) + (got[2, at:] + got[3, at:])
    load = total[:dofs] + exact_dot(total[dofs : 2 * dofs], coarse[:TILE])
    load = load + exact_dot(total[2 * dofs :, : 3 * dofs - TILE], coarse[TILE:])
    partial_rows(inverse, load, part)
    high, low = split(coarse)
    for p in range(delta.shape[0]):
        u_ref[p] = (delta[p] + applied(spread[p], high, low)).astype(BF16)


def next_values(got, delta, spread, inverse, share):
    dofs = spread.shape[1] // 3
    rhs = delta.shape[2]
    part = (2 * inverse.shape[0] * inverse.shape[2], rhs)
    return pl.pallas_call(
        functools.partial(next_kernel, share, dofs),
        in_specs=[IN_VMEM] * 4,
        out_specs=[IN_VMEM] * 2,
        out_shape=[like(delta.shape, BF16), like(part, BF16)],
        compiler_params=params(),
        cost_estimate=cost(10**8, 3 * 10**6),
    )(got, delta, spread, inverse)


def last_kernel(kind, index, signs, w, from_before, from_after, out):
    sub_dev, slots = kind.shape
    for i in range(sub_dev):
        for t in range(slots):
            p = i * slots + t
            where, which = kind[i, t], index[i, t]

            def put(tile, p=p, i=i, t=t):
                out[p] = (signs[i, t] * (w[p].astype(F32) - tile.astype(F32))).astype(BF16)

            @pl.when(where == 0)
            def _(put=put, which=which, t=t):
                put(w[which * slots + t])

            @pl.when(where == 1)
            def _(put=put, which=which):
                put(from_after[which])

            @pl.when(where == 2)
            def _(put=put, which=which):
                put(from_before[which])


def last_values(kind, index, signs, w, from_before, from_after):
    return pl.pallas_call(
        last_kernel,
        in_specs=[IN_SMEM] * 3 + [IN_VMEM] * 3,
        out_specs=IN_VMEM,
        out_shape=like(w.shape, BF16),
        compiler_params=params(),
        cost_estimate=cost(10**7, 3 * 10**6),
    )(kind, index, signs, w, from_before, from_after)


def body(multipliers, schur_inverse, corner_coupling, coarse_inverse, partner, corner_map):
    n_sub = lax.axis_size("sub")
    n_dom = lax.axis_size("dom")
    sub = lax.axis_index("sub")
    dom = lax.axis_index("dom")
    sub_dev, block_rows, rhs = multipliers.shape
    slots = block_rows // TILE
    coarse_block, coarse_dev = coarse_inverse.shape
    share = coarse_block // n_sub

    ids = sub * sub_dev + jnp.arange(sub_dev, dtype=jnp.int32)
    all_signs = jnp.where(ids[:, None] < partner, 1.0, -1.0).astype(F32)
    partners = lax.dynamic_slice_in_dim(partner, dom * slots, slots, 1)
    signs = lax.dynamic_slice_in_dim(all_signs, dom * slots, slots, 1)
    local = partners % sub_dev
    relation = (partners // sub_dev - sub) % n_sub
    kind = jnp.where(relation == 0, 0, jnp.where(relation == 1, 1, 2)).astype(jnp.int32)
    slot_ids = jnp.arange(slots, dtype=jnp.int32)[None]
    same_kind = kind[None] == kind[:, None]
    subs = jnp.arange(sub_dev, dtype=jnp.int32)
    earlier = same_kind & (subs[None] < subs[:, None])[:, :, None]
    lower = same_kind & (local[None] < local[:, None])
    sent = jnp.sum(earlier.astype(jnp.int32), axis=1) * slots + slot_ids
    got = jnp.sum(lower.astype(jnp.int32), axis=1) * slots + slot_ids
    after = jnp.where(kind == 1, sent, -1)
    before = jnp.where(kind == 2, sent, -1)
    index = jnp.where(kind == 0, local, got)

    corner_local = corner_map - sub * coarse_dev
    corner_table = (
        corner_local[:, :, None] == jnp.arange(coarse_dev, dtype=jnp.int32)[None, None]
    ).astype(BF16)
    coupling = jnp.einsum(
        "sjk,sjn->skn", corner_table, corner_coupling, preferred_element_type=F32
    ).astype(BF16)
    def own_rows(part):
        by_sub = lax.all_to_all(part.reshape(n_sub, share, rhs), "sub", 0, 0, tiled=True)
        return jnp.sum(by_sub.astype(F32), axis=0)

    far = swapped(multipliers, "dom", 2)
    near = swapped(multipliers, "dom", 1)
    near_far = swapped(far, "dom", 1)
    signed = coupling.reshape(sub_dev, coarse_dev, slots, TILE) * signs[:, None, :, None].astype(BF16)
    load1 = jnp.einsum(
        "skn,snr->kr", signed.reshape(coupling.shape), multipliers, preferred_element_type=F32
    )
    quarters = coarse_inverse.reshape(2, coarse_block // (2 * coarse_dev), n_dom, share, coarse_dev)
    quarters = quarters.transpose(2, 1, 3, 0, 4).reshape(n_dom, -1, 2 * coarse_dev)
    to_dom = jnp.concatenate(
        [quarters, jnp.broadcast_to(load1[None], (n_dom,) + load1.shape)], axis=1
    )
    inverse = lax.all_to_all(to_dom, "dom", 0, 0, tiled=True)
    part1 = first_part(inverse)
    across = packed_coupling(after, before, coupling)
    spread, second = spread_of(
        kind, index, coupling, shifted(across[0], "sub", 1), shifted(across[1], "sub", -1)
    )
    direct1, to_after, to_before = product(
        schur_inverse, (multipliers, near, far, near_far), (after, before, all_signs)
    )
    got_before, got_after = shifted(to_after, "sub", 1), shifted(to_before, "sub", -1)
    rows = own_rows(part1)
    rows1 = [shifted(rows, "sub", 1), rows, shifted(rows, "sub", -1)]
    got_before, got_after, rows1 = lax.optimization_barrier((got_before, got_after, rows1))
    delta1, sent1 = difference(
        kind, index, rows1, direct1, got_before, got_after, coupling, second
    )
    all1 = lax.all_gather(sent1, "dom", axis=0)

    u2, part2 = next_values(all1, delta1, spread, inverse, share)
    u2 = u2.reshape(multipliers.shape)
    far2 = swapped(u2, "dom", 2)
    near2 = swapped(u2, "dom", 1)
    own = own_rows(part2)
    near_far2 = swapped(far2, "dom", 1)
    near_far2, own = lax.optimization_barrier((near_far2, own))
    rows2 = [own] + [swapped(own, "dom", m) for m in range(1, n_dom)]
    (direct2,) = product(schur_inverse, (u2, near2, far2, near_far2))
    w2, to_after2, to_before2 = weighted(after, before, rows2, direct2, coupling)
    got_before2, got_after2 = shifted(to_after2, "sub", 1), shifted(to_before2, "sub", -1)
    result = last_values(kind, index, signs, w2, got_before2, got_after2)
    return result.reshape(sub_dev, block_rows, rhs)


def solution(mesh):
    placed = (
        P("sub", "dom", None),
        P("sub", "dom", None),
        P("sub", None, "dom"),
        P("dom", "sub"),
        P("sub", None),
        P("sub", None),
    )
    return jax.shard_map(
        body, mesh=mesh, in_specs=placed, out_specs=P("sub", "dom", None), check_vma=False
    )
```

time: 1540 us -> 136 us (0.09)
  waiting for transfers between devices: 1340 us -> 26.6 us
  blocking collectives: 135 us -> 9.38 us
  starting transfers between devices: 14.7 us -> 63.9 us
  Pallas kernels: 0 us -> 23.8 us
  matrix products: 21.1 us -> 1.61 us
    psum x2 -> x0, waiting for transfers between devices: 1310 us -> none  [apply_once(): coarse_total = lax.psum(coarse_term, 'sub')]
    psum x4 -> x0, blocking collectives: 135 us -> none  [the longest x2 110 us: from_root(): return lax.psum(kept, axis)]
    all_to_all x0 -> x3, starting transfers between devices: none -> 26.3 us  [the longest x2 21.6 us: own_rows(): lax.all_to_all(part.reshape(n_sub, share, rhs), 'sub', 0, 0, tiled=True)]
    pallas_call x0 -> x9, Pallas kernels: none -> 23.8 us  [the longest x2 13.9 us: product(): pl.pallas_call(functools.partial(product_kernel, first), grid=(sub_dev,),...]
    ppermute x4 -> x17, starting transfers between devices: 14.5 us -> 37.6 us  [the longest x8 25.7 us: shifted(): lax.ppermute(block, axis, [(i, (i + distance) % n) for i in range(n)])]
    dot_general x14 -> x2, matrix products: 21.1 us -> 1.61 us  [the longest x1 1.27 us: body(): jnp.einsum('skn,snr->kr', signed.reshape(coupling.shape), multipliers, pr...]
    ppermute x4 -> x17, waiting for transfers between devices: 36.9 us -> 18.9 us  [the longest x8 12.9 us: shifted(): lax.ppermute(block, axis, [(i, (i + distance) % n) for i in range(n)])]
  transfers between devices with their start and end apart: 8 -> 20, of which waited for: 6 -> 7; matrix products, arithmetic and copies ran while one was open for 0% -> 5% of each run, Pallas kernels for 0% -> 13%
where the time goes in v2:
time: 136 us; the launch traced here: 135 us
  starting transfers between devices  63.9 us (47%)
  waiting for transfers between devices  26.6 us (20%)
  Pallas kernels  23.8 us (18%)
  blocking collectives  9.38 us (7%)
  local copies, waits for them, and re-layouts  6.11 us (4%)
  other arithmetic  3.9 us (3%)
  matrix products  1.61 us (1%)
    ppermute x8, starting transfers between devices, shifted(): lax.ppermute(block, axis, [(i, (i + distance) % n) for i in range(n)])  25.7 us
    all_to_all x2, starting transfers between devices, own_rows(): lax.all_to_all(part.reshape(n_sub, share, rhs), 'sub', 0, 0, tiled=True)  21.6 us
    pallas_call x2, Pallas kernels, product(): pl.pallas_call(functools.partial(product_kernel, first), grid=(sub_dev,),...  13.9 us
    ppermute x8, waiting for transfers between devices, shifted(): lax.ppermute(block, axis, [(i, (i + distance) % n) for i in range(n)])  12.9 us
    ppermute x9, starting transfers between devices, swapped(): return lax.ppermute(block, axis, [(i, i ^ mask) for i in range(n)])  11.9 us
    all_gather x1, blocking collectives, body(): all1 = lax.all_gather(sent1, 'dom', axis=0)  9.38 us
    ppermute x9, waiting for transfers between devices, swapped(): return lax.ppermute(block, axis, [(i, i ^ mask) for i in range(n)])  5.97 us
    unnamed x29, local copies, waits for them, and re-layouts  5.39 us
  transfers between devices with their start and end apart: 20, of which 7 were waited for; matrix products, arithmetic and copies ran while one was open for 5% of the time, Pallas kernels for 13%

profile of v2, /device:TPU:1, one launch (start us, length us, event | category | flops | bytes accessed | tf_op | source)
XLA Modules:
  0.0 135.5 jit_solution(3209208081352438463)
XLA Ops:
  0.0 2.0 %collective-permute-start.1 = (bf16[4,512,128]{2,1,0:T(8,128)(2,1)}, bf16[4,512,128]{2,1,0:T(8,128)(2,1)S(1)}, u32[]{:S(2)}, u32[]{:S(2)}) collective-permute-start(bf16[4,512,128]{2,1,0:T(8,128)(2,1)} %refs_4_.1), channel_id=1, source_target_pairs={{0,2},{1,3},{2,0},{3,1},{4,6},{5,7},{6,4},{7,5},{8,10},{9,11},{10,... | collective-permute-start | bytes 1572872 | tf_op jit(solution)/shard_map/ppermute | solution.py:38
  2.0 0.8 compare_select_fusion.2.refs_2_
  2.8 0.1 fusion.6
  2.9 0.1 broadcast_bitcast_fusion
  3.0 1.1 copy.10
  4.1 0.4 copy.11
  4.5 0.3 reshape.46
  4.8 0.7 broadcast_subtract_fusion
  5.5 0.3 convolution_convert_fusion.coupling
  5.9 1.3 convolution_bitcast_fusion
  7.2 0.8 pad_maximum_fusion
  7.9 4.7 %all-to-all-start = ((f32[4,192,128]{2,1,0:T(8,128)}), f32[4,192,128]{2,1,0:T(8,128)S(1)}, u32[]{:S(2)}, u32[]{:S(2)}) async-start(f32[4,192,128]{2,1,0:T(8,128)} %pad_maximum_fusion), calls=%async_computation | async-start | bytes 786432 | tf_op jit(solution)/shard_map/all_to_all | solution.py:429
  12.6 0.1 collective-permute-start
  12.7 0.0 collective-permute-done.1.refs_6_
  12.7 2.4 %collective-permute-start.2 = (bf16[4,512,128]{2,1,0:T(8,128)(2,1)S(1)}, bf16[4,512,128]{2,1,0:T(8,128)(2,1)S(1)}, u32[]{:S(2)}, u32[]{:S(2)}) collective-permute-start(bf16[4,512,128]{2,1,0:T(8,128)(2,1)S(1)} %collective-permute-done.1.refs_6_), channel_id=1, source_target_pairs={{0,1},{1,0},{2,3},{3,2},{4,5},{5,4},{6,7},{7,6},{8,9},{9,8},{10,11... | collective-permute-start | bytes 1572872 | tf_op jit(solution)/shard_map/ppermute | solution.py:38
  15.1 0.8 add_select_fusion
  15.9 3.3 %all-to-all-done.got.inverse = f32[4,192,128]{2,1,0:T(8,128)S(1)} async-done(((f32[4,192,128]{2,1,0:T(8,128)}), f32[4,192,128]{2,1,0:T(8,128)S(1)}, u32[]{:S(2)}, u32[]{:S(2)}) %all-to-all-start) | async-done | bytes 393248 | tf_op jit(solution)/shard_map/all_to_all | solution.py:429
  19.2 1.1 shard_map.65
  20.3 14.0 %all-to-all-start.1 = ((bf16[64,16,128]{2,1,0:T(8,128)(2,1)}), bf16[64,16,128]{2,1,0:T(8,128)(2,1)S(1)}, u32[]{:S(2)}, u32[]{:S(2)}) async-start(bf16[64,16,128]{2,1,0:T(8,128)(2,1)} %bitcast.3), calls=%async_computation.1 | async-start | bytes 524288 | tf_op jit(solution)/shard_map/all_to_all | solution.py:414
  34.3 0.1 convert_reduce_fusion.2
  34.4 0.6 compare_select_fusion
  35.0 0.0 copy-start.10
  35.0 0.7 copy-done.10
  35.8 0.2 copy-done.11
  35.9 7.2 %shard_map.64 = (f32[16,128,128]{2,1,0:T(8,128)}, bf16[8,128,128]{2,1,0:T(8,128)(2,1)}, bf16[8,128,128]{2,1,0:T(8,128)(2,1)}) custom-call(s32[4,4]{1,0:T(4,128)} %get-tuple-element.52.refs_0_.after, s32[4,4]{1,0:T(4,128)} %get-tuple-element.51.refs_1_.before, f32[4,16]{1,0:T(4,128)} %copy-done.12, bf16[4,512,2048]{2,1,0:T(8,128)(2,1)} %refs_0_.1, ...), custom_call_target="tpu_custom_call" | custom-call | flops 1073741824 | bytes 8388608 | tf_op jit(solution)/shard_map/pallas_call | solution.py:174
  43.1 2.6 %collective-permute-start.3 = (bf16[8,128,128]{2,1,0:T(8,128)(2,1)}, bf16[8,128,128]{2,1,0:T(8,128)(2,1)S(1)}, u32[]{:S(2)}, u32[]{:S(2)}) collective-permute-start(bf16[8,128,128]{2,1,0:T(8,128)(2,1)} %get-tuple-element.26), channel_id=1, source_target_pairs={{0,4},{4,8},{8,12},{12,16},{16,20},{20,24},{24,28},{28,32},{32,36}... | collective-permute-start | bytes 786440 | tf_op jit(solution)/shard_map/ppermute | solution.py:33
  45.7 4.7 %collective-permute-start.4 = (bf16[8,128,128]{2,1,0:T(8,128)(2,1)}, bf16[8,128,128]{2,1,0:T(8,128)(2,1)S(1)}, u32[]{:S(2)}, u32[]{:S(2)}) collective-permute-start(bf16[8,128,128]{2,1,0:T(8,128)(2,1)} %get-tuple-element.27), channel_id=1, source_target_pairs={{0,252},{4,0},{8,4},{12,8},{16,12},{20,16},{24,20},{28,24},{32,28}... | collective-permute-start | bytes 786440 | tf_op jit(solution)/shard_map/ppermute | solution.py:33
  50.4 0.9 shard_map.66
  51.3 0.1 collective-permute-start.7
  51.4 7.2 %collective-permute-start.8 = (bf16[8,64,128]{2,1,0:T(8,128)(2,1)S(1)}, bf16[8,64,128]{2,1,0:T(8,128)(2,1)S(1)}, u32[]{:S(2)}, u32[]{:S(2)}) collective-permute-start(bf16[8,64,128]{2,1,0:T(8,128)(2,1)S(1)} %get-tuple-element.35), channel_id=1, source_target_pairs={{0,252},{4,0},{8,4},{12,8},{16,12},{20,16},{24,20},{28,24},{32,28}... | collective-permute-start | bytes 393224 | tf_op jit(solution)/shard_map/ppermute | solution.py:33
  58.6 0.0 all-to-all-done.1
  58.6 0.1 convert_reduce_fusion.1.r1
  58.6 0.1 collective-permute-start.6
  58.7 3.4 %collective-permute-done.7.from_before = bf16[8,64,128]{2,1,0:T(8,128)(2,1)S(1)} collective-permute-done((bf16[8,64,128]{2,1,0:T(8,128)(2,1)S(1)}, bf16[8,64,128]{2,1,0:T(8,128)(2,1)S(1)}, u32[]{:S(2)}, u32[]{:S(2)}) %collective-permute-start.7) | collective-permute-done | bytes 131104 | tf_op jit(solution)/shard_map/ppermute | solution.py:33
  62.1 3.8 %collective-permute-start.5 = (f32[16,128]{1,0:T(8,128)S(1)}, f32[16,128]{1,0:T(8,128)S(1)}, u32[]{:S(2)}, u32[]{:S(2)}) collective-permute-start(f32[16,128]{1,0:T(8,128)S(1)} %convert_reduce_fusion.1.r1), channel_id=1, source_target_pairs={{0,4},{4,8},{8,12},{12,16},{16,20},{20,24},{24,28},{28,32},{32,36}... | collective-permute-start | bytes 24584 | tf_op jit(solution)/shard_map/ppermute | solution.py:33
  65.9 2.0 %shard_map.67 = (bf16[16,192,128]{2,1,0:T(8,128)(2,1)S(1)}, f32[128,128]{1,0:T(8,128)S(1)}) custom-call(s32[4,4]{1,0:T(4,128)S(1)} %get-tuple-element.55.kind, s32[4,4]{1,0:T(4,128)S(1)} %get-tuple-element.53.index, bf16[4,64,512]{2,1,0:T(8,128)(2,1)S(1)} %convolution_convert_fusion.coupling, bf16[8,64,128]{2,1,0:T(8,128)(2,1)S(1)} %collective-permute-done.7.from_before, ...), custom_call_target="tpu_custom_call" | custom-call | flops 100000000 | bytes 2000000 | tf_op jit(solution)/shard_map/pallas_call | solution.py:253
  67.9 0.0 collective-permute-done.6.r2
  67.9 2.4 %collective-permute-done.5.r0 = f32[16,128]{1,0:T(8,128)S(1)} collective-permute-done((f32[16,128]{1,0:T(8,128)S(1)}, f32[16,128]{1,0:T(8,128)S(1)}, u32[]{:S(2)}, u32[]{:S(2)}) %collective-permute-start.5) | collective-permute-done | bytes 8224 | tf_op jit(solution)/shard_map/ppermute | solution.py:33
  70.3 0.0 collective-permute-done.4.from_after
  70.3 1.2 copy-done.2
  71.6 1.4 %shard_map.68 = (f32[16,128,128]{2,1,0:T(8,128)S(1)}, f32[240,128]{1,0:T(8,128)S(1)}) custom-call(s32[4,4]{1,0:T(4,128)S(1)} %get-tuple-element.55.kind, s32[4,4]{1,0:T(4,128)S(1)} %get-tuple-element.53.index, f32[16,128]{1,0:T(8,128)S(1)} %collective-permute-done.5.r0, f32[16,128]{1,0:T(8,128)S(1)} %convert_reduce_fusion.1.r1, ...), custom_call_target="tpu_custom_call" | custom-call | flops 100000000 | bytes 3000000 | tf_op jit(solution)/shard_map/pallas_call | solution.py:299
  72.9 9.4 %all-gather = f32[960,128]{1,0:T(8,128)S(1)} all-gather(f32[240,128]{1,0:T(8,128)S(1)} %get-tuple-element.37), channel_id=2, replica_groups=mesh['sub'=64,'dom'=4] {'dom'}, dimensions={0}, use_global_device_ids=true | all-gather | bytes 614400 | tf_op jit(solution)/shard_map/all_gather | solution.py:445
  82.3 1.3 shard_map.69
  83.6 0.8 collective-permute-start.9
  84.4 7.6 %all-to-all-start.2 = ((bf16[64,16,128]{2,1,0:T(8,128)(2,1)}), bf16[64,16,128]{2,1,0:T(8,128)(2,1)S(1)}, u32[]{:S(2)}, u32[]{:S(2)}) async-start(bf16[64,16,128]{2,1,0:T(8,128)(2,1)} %bitcast.6), calls=%async_computation.2 | async-start | bytes 524288 | tf_op jit(solution)/shard_map/all_to_all | solution.py:414
  92.1 5.9 %collective-permute-done.9.refs_3_ = bf16[4,512,128]{2,1,0:T(8,128)(2,1)S(1)} collective-permute-done((bf16[4,512,128]{2,1,0:T(8,128)(2,1)S(1)}, bf16[4,512,128]{2,1,0:T(8,128)(2,1)S(1)}, u32[]{:S(2)}, u32[]{:S(2)}) %collective-permute-start.9) | collective-permute-done | bytes 524320 | tf_op jit(solution)/shard_map/ppermute | solution.py:38
  98.0 2.0 %collective-permute-start.10 = (bf16[4,512,128]{2,1,0:T(8,128)(2,1)S(1)}, bf16[4,512,128]{2,1,0:T(8,128)(2,1)S(1)}, u32[]{:S(2)}, u32[]{:S(2)}) collective-permute-start(bf16[4,512,128]{2,1,0:T(8,128)(2,1)S(1)} %collective-permute-done.9.refs_3_), channel_id=1, source_target_pairs={{0,1},{1,0},{2,3},{3,2},{4,5},{5,4},{6,7},{7,6},{8,9},{9,8},{10,11... | collective-permute-start | bytes 1572872 | tf_op jit(solution)/shard_map/ppermute | solution.py:38
  100.0 0.0 collective-permute-start.14
  100.0 4.4 %all-to-all-done.2 = bf16[64,16,128]{2,1,0:T(8,128)(2,1)S(1)} async-done(((bf16[64,16,128]{2,1,0:T(8,128)(2,1)}), bf16[64,16,128]{2,1,0:T(8,128)(2,1)S(1)}, u32[]{:S(2)}, u32[]{:S(2)}) %all-to-all-start.2) | async-done | bytes 262176 | tf_op jit(solution)/shard_map/all_to_all | solution.py:414
  104.4 0.1 convert_reduce_fusion.r0
  104.5 3.5 %collective-permute-start.13 = (f32[16,128]{1,0:T(8,128)S(1)}, f32[16,128]{1,0:T(8,128)S(1)}, u32[]{:S(2)}, u32[]{:S(2)}) collective-permute-start(f32[16,128]{1,0:T(8,128)S(1)} %convert_reduce_fusion.r0), channel_id=1, source_target_pairs={{0,3},{1,2},{2,1},{3,0},{4,7},{5,6},{6,5},{7,4},{8,11},{9,10},{10,... | collective-permute-start | bytes 24584 | tf_op jit(solution)/shard_map/ppermute | solution.py:38
  108.0 1.0 collective-permute-start.12
  109.0 0.0 collective-permute-start.11
  109.0 0.0 collective-permute-done.14.refs_2_
  109.1 0.8 copy-done.8
  109.9 6.7 %shard_map.70.direct = f32[16,128,128]{2,1,0:T(8,128)} custom-call(bf16[4,512,2048]{2,1,0:T(8,128)(2,1)} %refs_0_.1, bf16[4,512,128]{2,1,0:T(8,128)(2,1)} %bitcast.20, bf16[4,512,128]{2,1,0:T(8,128)(2,1)} %copy-done.8, bf16[4,512,128]{2,1,0:T(8,128)(2,1)} %copy-done.6, bf16[4,512,128]{2,1,0:T(8,128)(2,1)} %copy-done.7), custom_call_target="tpu_custom_call" | custom-call | flops 1073741824 | bytes 8388608 | tf_op jit(solution)/shard_map/pallas_call | solution.py:174
  116.6 0.0 collective-permute-done.13.r3
  116.6 1.2 copy-done.1
  117.8 1.4 shard_map.71
  119.2 1.2 collective-permute-start.15
  120.3 6.1 %collective-permute-start.16 = (bf16[8,128,128]{2,1,0:T(8,128)(2,1)S(1)}, bf16[8,128,128]{2,1,0:T(8,128)(2,1)S(1)}, u32[]{:S(2)}, u32[]{:S(2)}) collective-permute-start(bf16[8,128,128]{2,1,0:T(8,128)(2,1)S(1)} %get-tuple-element.46), channel_id=1, source_target_pairs={{0,252},{4,0},{8,4},{12,8},{16,12},{20,16},{24,20},{28,24},{32,28}... | collective-permute-start | bytes 786440 | tf_op jit(solution)/shard_map/ppermute | solution.py:33
  126.4 5.9 %collective-permute-done.15.from_before = bf16[8,128,128]{2,1,0:T(8,128)(2,1)S(1)} collective-permute-done((bf16[8,128,128]{2,1,0:T(8,128)(2,1)S(1)}, bf16[8,128,128]{2,1,0:T(8,128)(2,1)S(1)}, u32[]{:S(2)}, u32[]{:S(2)}) %collective-permute-start.15) | collective-permute-done | bytes 262176 | tf_op jit(solution)/shard_map/ppermute | solution.py:33
  132.4 1.2 collective-permute-done.16.from_after
  133.6 1.8 %shard_map.72 = bf16[16,128,128]{2,1,0:T(8,128)(2,1)} custom-call(s32[4,4]{1,0:T(4,128)S(1)} %get-tuple-element.55.kind, s32[4,4]{1,0:T(4,128)S(1)} %get-tuple-element.53.index, f32[4,4]{1,0:T(4,128)S(1)} %get-tuple-element.50.signs, bf16[16,128,128]{2,1,0:T(8,128)(2,1)S(1)} %get-tuple-element.44.w, ...), custom_call_target="tpu_custom_call" | custom-call | flops 10000000 | bytes 3000000 | tf_op jit(solution)/shard_map/pallas_call | solution.py:368
  (31 shorter events, 0.1 us)
Async XLA Ops:
  0.0 5.5 %copy-start = (bf16[4,24,512]{2,1,0:T(8,128)(2,1)S(1)}, bf16[4,24,512]{2,1,0:T(8,128)(2,1)}, u32[]{:S(2)}) copy-start(bf16[4,24,512]{2,1,0:T(8,128)(2,1)} %param.8) | copy-start | bytes 294916
  0.0 12.7 %collective-permute-start.1 = (bf16[4,512,128]{2,1,0:T(8,128)(2,1)}, bf16[4,512,128]{2,1,0:T(8,128)(2,1)S(1)}, u32[]{:S(2)}, u32[]{:S(2)}) collective-permute-start(bf16[4,512,128]{2,1,0:T(8,128)(2,1)} %refs_4_.1), channel_id=1, source_target_pairs={{0,2},{1,3},{2,0},{3,1},{4,6},{5,7},{6,4},{7,5},{8,10},{9,11},{10,... | collective-permute-start | bytes 1572872 | tf_op jit(solution)/shard_map/ppermute | solution.py:38
  2.8 32.2 %copy-start.12 = (f32[4,16]{1,0:T(4,128)}, f32[4,16]{1,0:T(4,128)S(1)}, u32[]{:S(2)}) copy-start(f32[4,16]{1,0:T(4,128)S(1)} %compare_select_fusion.2.refs_2_) | copy-start | bytes 772
  7.9 11.2 %all-to-all-start = ((f32[4,192,128]{2,1,0:T(8,128)}), f32[4,192,128]{2,1,0:T(8,128)S(1)}, u32[]{:S(2)}, u32[]{:S(2)}) async-start(f32[4,192,128]{2,1,0:T(8,128)} %pad_maximum_fusion), calls=%async_computation | async-start | bytes 786432 | tf_op jit(solution)/shard_map/all_to_all | solution.py:429
  12.6 22.4 %collective-permute-start = (bf16[4,512,128]{2,1,0:T(8,128)(2,1)}, bf16[4,512,128]{2,1,0:T(8,128)(2,1)S(1)}, u32[]{:S(2)}, u32[]{:S(2)}) collective-permute-start(bf16[4,512,128]{2,1,0:T(8,128)(2,1)} %refs_4_.1), channel_id=1, source_target_pairs={{0,1},{1,0},{2,3},{3,2},{4,5},{5,4},{6,7},{7,6},{8,9},{9,8},{10,11... | collective-permute-start | bytes 1572872 | tf_op jit(solution)/shard_map/ppermute | solution.py:38
  12.7 22.3 %copy-start.9 = (bf16[4,512,128]{2,1,0:T(8,128)(2,1)}, bf16[4,512,128]{2,1,0:T(8,128)(2,1)S(1)}, u32[]{:S(2)}) copy-start(bf16[4,512,128]{2,1,0:T(8,128)(2,1)S(1)} %collective-permute-done.1.refs_6_) | copy-start | bytes 1572868
  12.7 22.3 %collective-permute-start.2 = (bf16[4,512,128]{2,1,0:T(8,128)(2,1)S(1)}, bf16[4,512,128]{2,1,0:T(8,128)(2,1)S(1)}, u32[]{:S(2)}, u32[]{:S(2)}) collective-permute-start(bf16[4,512,128]{2,1,0:T(8,128)(2,1)S(1)} %collective-permute-done.1.refs_6_), channel_id=1, source_target_pairs={{0,1},{1,0},{2,3},{3,2},{4,5},{5,4},{6,7},{7,6},{8,9},{9,8},{10,11... | collective-permute-start | bytes 1572872 | tf_op jit(solution)/shard_map/ppermute | solution.py:38
  20.3 38.3 %all-to-all-start.1 = ((bf16[64,16,128]{2,1,0:T(8,128)(2,1)}), bf16[64,16,128]{2,1,0:T(8,128)(2,1)S(1)}, u32[]{:S(2)}, u32[]{:S(2)}) async-start(bf16[64,16,128]{2,1,0:T(8,128)(2,1)} %bitcast.3), calls=%async_computation.1 | async-start | bytes 524288 | tf_op jit(solution)/shard_map/all_to_all | solution.py:414
  35.0 15.5 %copy-start.4 = (s32[4,4]{1,0:T(4,128)S(1)}, s32[4,4]{1,0:T(4,128)}, u32[]{:S(2)}) copy-start(s32[4,4]{1,0:T(4,128)} %get-tuple-element.51.refs_1_.before) | copy-start | bytes 196
  35.0 15.5 %copy-start.5 = (s32[4,4]{1,0:T(4,128)S(1)}, s32[4,4]{1,0:T(4,128)}, u32[]{:S(2)}) copy-start(s32[4,4]{1,0:T(4,128)} %get-tuple-element.52.refs_0_.after) | copy-start | bytes 196
  35.0 0.8 copy-start.10
  35.0 0.9 copy-start.11
  43.1 27.2 %collective-permute-start.3 = (bf16[8,128,128]{2,1,0:T(8,128)(2,1)}, bf16[8,128,128]{2,1,0:T(8,128)(2,1)S(1)}, u32[]{:S(2)}, u32[]{:S(2)}) collective-permute-start(bf16[8,128,128]{2,1,0:T(8,128)(2,1)} %get-tuple-element.26), channel_id=1, source_target_pairs={{0,4},{4,8},{8,12},{12,16},{16,20},{20,24},{24,28},{28,32},{32,36}... | collective-permute-start | bytes 786440 | tf_op jit(solution)/shard_map/ppermute | solution.py:33
  45.7 24.6 %collective-permute-start.4 = (bf16[8,128,128]{2,1,0:T(8,128)(2,1)}, bf16[8,128,128]{2,1,0:T(8,128)(2,1)S(1)}, u32[]{:S(2)}, u32[]{:S(2)}) collective-permute-start(bf16[8,128,128]{2,1,0:T(8,128)(2,1)} %get-tuple-element.27), channel_id=1, source_target_pairs={{0,252},{4,0},{8,4},{12,8},{16,12},{20,16},{24,20},{28,24},{32,28}... | collective-permute-start | bytes 786440 | tf_op jit(solution)/shard_map/ppermute | solution.py:33
  51.3 10.8 %collective-permute-start.7 = (bf16[8,64,128]{2,1,0:T(8,128)(2,1)S(1)}, bf16[8,64,128]{2,1,0:T(8,128)(2,1)S(1)}, u32[]{:S(2)}, u32[]{:S(2)}) collective-permute-start(bf16[8,64,128]{2,1,0:T(8,128)(2,1)S(1)} %get-tuple-element.34), channel_id=1, source_target_pairs={{0,4},{4,8},{8,12},{12,16},{16,20},{20,24},{24,28},{28,32},{32,36}... | collective-permute-start | bytes 393224 | tf_op jit(solution)/shard_map/ppermute | solution.py:33
  51.4 14.5 %collective-permute-start.8 = (bf16[8,64,128]{2,1,0:T(8,128)(2,1)S(1)}, bf16[8,64,128]{2,1,0:T(8,128)(2,1)S(1)}, u32[]{:S(2)}, u32[]{:S(2)}) collective-permute-start(bf16[8,64,128]{2,1,0:T(8,128)(2,1)S(1)} %get-tuple-element.35), channel_id=1, source_target_pairs={{0,252},{4,0},{8,4},{12,8},{16,12},{20,16},{24,20},{28,24},{32,28}... | collective-permute-start | bytes 393224 | tf_op jit(solution)/shard_map/ppermute | solution.py:33
  58.6 9.3 %collective-permute-start.6 = (f32[16,128]{1,0:T(8,128)S(1)}, f32[16,128]{1,0:T(8,128)S(1)}, u32[]{:S(2)}, u32[]{:S(2)}) collective-permute-start(f32[16,128]{1,0:T(8,128)S(1)} %convert_reduce_fusion.1.r1), channel_id=1, source_target_pairs={{0,252},{4,0},{8,4},{12,8},{16,12},{20,16},{24,20},{28,24},{32,28}... | collective-permute-start | bytes 24584 | tf_op jit(solution)/shard_map/ppermute | solution.py:33
  62.1 8.2 %collective-permute-start.5 = (f32[16,128]{1,0:T(8,128)S(1)}, f32[16,128]{1,0:T(8,128)S(1)}, u32[]{:S(2)}, u32[]{:S(2)}) collective-permute-start(f32[16,128]{1,0:T(8,128)S(1)} %convert_reduce_fusion.1.r1), channel_id=1, source_target_pairs={{0,4},{4,8},{8,12},{12,16},{16,20},{20,24},{24,28},{28,32},{32,36}... | collective-permute-start | bytes 24584 | tf_op jit(solution)/shard_map/ppermute | solution.py:33
  70.3 1.2 copy-start.2
  83.6 25.5 %copy-start.3 = (bf16[16,128,128]{2,1,0:T(8,128)(2,1)}, bf16[16,128,128]{2,1,0:T(8,128)(2,1)S(1)}, u32[]{:S(2)}) copy-start(bf16[16,128,128]{2,1,0:T(8,128)(2,1)S(1)} %get-tuple-element.40) | copy-start | bytes 1572868
  83.6 14.4 %collective-permute-start.9 = (bf16[4,512,128]{2,1,0:T(8,128)(2,1)S(1)}, bf16[4,512,128]{2,1,0:T(8,128)(2,1)S(1)}, u32[]{:S(2)}, u32[]{:S(2)}) collective-permute-start(bf16[4,512,128]{2,1,0:T(8,128)(2,1)S(1)} %bitcast.18), channel_id=1, source_target_pairs={{0,2},{1,3},{2,0},{3,1},{4,6},{5,7},{6,4},{7,5},{8,10},{9,11},{10,... | collective-permute-start | bytes 1572872 | tf_op jit(solution)/shard_map/ppermute | solution.py:38
  84.4 20.0 %all-to-all-start.2 = ((bf16[64,16,128]{2,1,0:T(8,128)(2,1)}), bf16[64,16,128]{2,1,0:T(8,128)(2,1)S(1)}, u32[]{:S(2)}, u32[]{:S(2)}) async-start(bf16[64,16,128]{2,1,0:T(8,128)(2,1)} %bitcast.6), calls=%async_computation.2 | async-start | bytes 524288 | tf_op jit(solution)/shard_map/all_to_all | solution.py:414
  98.0 11.1 %copy-start.6 = (bf16[4,512,128]{2,1,0:T(8,128)(2,1)}, bf16[4,512,128]{2,1,0:T(8,128)(2,1)S(1)}, u32[]{:S(2)}) copy-start(bf16[4,512,128]{2,1,0:T(8,128)(2,1)S(1)} %collective-permute-done.9.refs_3_) | copy-start | bytes 1572868
  98.0 6.5 %collective-permute-start.10 = (bf16[4,512,128]{2,1,0:T(8,128)(2,1)S(1)}, bf16[4,512,128]{2,1,0:T(8,128)(2,1)S(1)}, u32[]{:S(2)}, u32[]{:S(2)}) collective-permute-start(bf16[4,512,128]{2,1,0:T(8,128)(2,1)S(1)} %collective-permute-done.9.refs_3_), channel_id=1, source_target_pairs={{0,1},{1,0},{2,3},{3,2},{4,5},{5,4},{6,7},{7,6},{8,9},{9,8},{10,11... | collective-permute-start | bytes 1572872 | tf_op jit(solution)/shard_map/ppermute | solution.py:38
  100.0 9.1 %collective-permute-start.14 = (bf16[4,512,128]{2,1,0:T(8,128)(2,1)S(1)}, bf16[4,512,128]{2,1,0:T(8,128)(2,1)S(1)}, u32[]{:S(2)}, u32[]{:S(2)}) collective-permute-start(bf16[4,512,128]{2,1,0:T(8,128)(2,1)S(1)} %bitcast.19), channel_id=1, source_target_pairs={{0,1},{1,0},{2,3},{3,2},{4,5},{5,4},{6,7},{7,6},{8,9},{9,8},{10,11... | collective-permute-start | bytes 1572872 | tf_op jit(solution)/shard_map/ppermute | solution.py:38
  104.5 4.6 %copy-start.7 = (bf16[4,512,128]{2,1,0:T(8,128)(2,1)}, bf16[4,512,128]{2,1,0:T(8,128)(2,1)S(1)}, u32[]{:S(2)}) copy-start(bf16[4,512,128]{2,1,0:T(8,128)(2,1)S(1)} %collective-permute-done.10.refs_4_) | copy-start | bytes 1572868
  104.5 12.1 %collective-permute-start.13 = (f32[16,128]{1,0:T(8,128)S(1)}, f32[16,128]{1,0:T(8,128)S(1)}, u32[]{:S(2)}, u32[]{:S(2)}) collective-permute-start(f32[16,128]{1,0:T(8,128)S(1)} %convert_reduce_fusion.r0), channel_id=1, source_target_pairs={{0,3},{1,2},{2,1},{3,0},{4,7},{5,6},{6,5},{7,4},{8,11},{9,10},{10,... | collective-permute-start | bytes 24584 | tf_op jit(solution)/shard_map/ppermute | solution.py:38
  108.0 8.6 %collective-permute-start.12 = (f32[16,128]{1,0:T(8,128)S(1)}, f32[16,128]{1,0:T(8,128)S(1)}, u32[]{:S(2)}, u32[]{:S(2)}) collective-permute-start(f32[16,128]{1,0:T(8,128)S(1)} %convert_reduce_fusion.r0), channel_id=1, source_target_pairs={{0,2},{1,3},{2,0},{3,1},{4,6},{5,7},{6,4},{7,5},{8,10},{9,11},{10,... | collective-permute-start | bytes 24584 | tf_op jit(solution)/shard_map/ppermute | solution.py:38
  109.0 7.5 %collective-permute-start.11 = (f32[16,128]{1,0:T(8,128)S(1)}, f32[16,128]{1,0:T(8,128)S(1)}, u32[]{:S(2)}, u32[]{:S(2)}) collective-permute-start(f32[16,128]{1,0:T(8,128)S(1)} %convert_reduce_fusion.r0), channel_id=1, source_target_pairs={{0,1},{1,0},{2,3},{3,2},{4,5},{5,4},{6,7},{7,6},{8,9},{9,8},{10,11... | collective-permute-start | bytes 24584 | tf_op jit(solution)/shard_map/ppermute | solution.py:38
  109.1 0.8 copy-start.8
  116.6 1.2 copy-start.1
  119.2 13.2 %collective-permute-start.15 = (bf16[8,128,128]{2,1,0:T(8,128)(2,1)S(1)}, bf16[8,128,128]{2,1,0:T(8,128)(2,1)S(1)}, u32[]{:S(2)}, u32[]{:S(2)}) collective-permute-start(bf16[8,128,128]{2,1,0:T(8,128)(2,1)S(1)} %get-tuple-element.45), channel_id=1, source_target_pairs={{0,4},{4,8},{8,12},{12,16},{16,20},{20,24},{24,28},{28,32},{32,36}... | collective-permute-start | bytes 786440 | tf_op jit(solution)/shard_map/ppermute | solution.py:33
  120.3 13.3 %collective-permute-start.16 = (bf16[8,128,128]{2,1,0:T(8,128)(2,1)S(1)}, bf16[8,128,128]{2,1,0:T(8,128)(2,1)S(1)}, u32[]{:S(2)}, u32[]{:S(2)}) collective-permute-start(bf16[8,128,128]{2,1,0:T(8,128)(2,1)S(1)} %get-tuple-element.46), channel_id=1, source_target_pairs={{0,252},{4,0},{8,4},{12,8},{16,12},{20,16},{24,20},{28,24},{32,28}... | collective-permute-start | bytes 786440 | tf_op jit(solution)/shard_map/ppermute | solution.py:33

commit v3 on v2

--- a/solution.py
+++ b/solution.py
@@ -11,7 +11,7 @@
 F32 = jnp.float32
 BF16 = jnp.bfloat16
 VMEM_BYTES = 24 * 1024 * 1024
-MOST_VMEM_BYTES = 59 * 1024 * 1024
+MOST_VMEM_BYTES = 54 * 1024 * 1024
 IN_SMEM = pl.BlockSpec(memory_space=pltpu.SMEM)
 IN_VMEM = pl.BlockSpec(memory_space=pltpu.VMEM)
 
@@ -98,28 +98,9 @@
                     target[pl.ds(place, 1)] = tile_at(i, t).astype(BF16)[None]
 
 
-def pack_kernel(after, before, coupling, to_after, to_before):
-    def tile_at(i, t):
-        return coupling[i, :, t * TILE : (t + 1) * TILE]
-
-    pack_tiles(after, before, to_after, to_before, tile_at)
-
-
-def packed_coupling(after, before, coupling):
-    packed = like((2 * after.shape[1], coupling.shape[1], TILE), BF16)
-    return pl.pallas_call(
-        pack_kernel,
-        in_specs=[IN_SMEM] * 2 + [IN_VMEM],
-        out_specs=[IN_VMEM] * 2,
-        out_shape=[packed, packed],
-        compiler_params=params(),
-        cost_estimate=cost(10**5, 10**6),
-    )(after, before, coupling)
-
-
 def product_kernel(first, *refs):
     if first:
-        after, before, signs, s_ref, u0, u1, u2, u3, direct_ref, to_after, to_before = refs
+        after, before, signs, s_ref, u0, u1, u2, u3, coupling, direct_ref, to_after, to_before = refs
     else:
         s_ref, u0, u1, u2, u3, direct_ref = refs
     depth, rhs = u0.shape[1:]
@@ -157,10 +138,11 @@
 
                 @pl.when(place >= 0)
                 def _(t=t, place=place, target=target):
-                    target[pl.ds(place, 1)] = direct_ref[pl.ds(t, 1)].astype(BF16)
-
-
-def product(schur_inverse, pieces, tables=()):
+                    target[pl.ds(place, 1), :TILE] = direct_ref[pl.ds(t, 1)].astype(BF16)
+                    target[pl.ds(place, 1), TILE:] = coupling[0:1, :, t * TILE : (t + 1) * TILE]
+
+
+def product(schur_inverse, pieces, tables=(), coupling=None):
     sub_dev, rows, cols = schur_inverse.shape
     depth, rhs = pieces[0].shape[1:]
     slots = rows // TILE
@@ -168,7 +150,8 @@
     out_shape = [like((sub_dev * slots, TILE, rhs), F32)]
     out_specs = [pl.BlockSpec((slots, TILE, rhs), lambda i: (i, 0, 0))]
     if first:
-        packed = (2 * slots, TILE, rhs)
+        dofs = coupling.shape[1]
+        packed = (2 * slots, TILE + dofs, rhs)
         out_shape += [like(packed, BF16)] * 2
         out_specs += [pl.BlockSpec(packed, lambda i: (0, 0, 0))] * 2
     return pl.pallas_call(
@@ -176,12 +159,13 @@
         grid=(sub_dev,),
         in_specs=[IN_SMEM] * len(tables)
         + [pl.BlockSpec((1, rows, cols), lambda i: (i, 0, 0))]
-        + [pl.BlockSpec((1, depth, rhs), lambda i: (i, 0, 0))] * len(pieces),
+        + [pl.BlockSpec((1, depth, rhs), lambda i: (i, 0, 0))] * len(pieces)
+        + ([pl.BlockSpec((1, dofs, rows), lambda i: (i, 0, 0))] if first else []),
         out_specs=out_specs,
         out_shape=out_shape,
         compiler_params=params(MOST_VMEM_BYTES),
-        cost_estimate=cost(2 * sub_dev * rows * cols * rhs, 2 * sub_dev * rows * cols),
-    )(*tables, schur_inverse, *pieces)
+        cost_estimate=cost(1000, 1000),
+    )(*tables, schur_inverse, *pieces, *([coupling] if first else []))
 
 
 def weighted_kernel(after, before, r0, r1, r2, r3, direct, coupling, w_ref, to_after, to_before, coarse):
@@ -213,11 +197,15 @@
     )(after, before, *rows, direct, coupling)
 
 
-def spread_kernel(kind, index, coupling, from_before, from_after, spread, second):
+def difference_kernel(kind, index, r0, r1, r2, direct, from_before, from_after, coupling, delta, spread, sent):
     sub_dev, dofs, _ = coupling.shape
+    share = r0.shape[0]
+    for b, rows in enumerate((r0, r1, r2)):
+        sent[b * share : (b + 1) * share] = rows[...]
+    at = 3 * share
     slots = kind.shape[1]
     blank = jnp.zeros((dofs, TILE), BF16)
-    total = None
+    first, second = None, None
     for i in range(sub_dev):
         for t in range(slots):
             p = i * slots + t
@@ -229,84 +217,45 @@
             spread[p, 2 * dofs :] = blank
 
             @pl.when(where == 0)
-            def _(p=p, i=i, which=which, columns=columns):
+            def _(p=p, i=i, t=t, which=which, columns=columns):
+                delta[p] = direct[p] - direct[which * slots + t]
                 other = coupling[i, :, columns].astype(F32) - coupling[which, :, columns].astype(F32)
                 spread[p, dofs : 2 * dofs] = other.astype(BF16)
 
             @pl.when(where == 1)
             def _(p=p, which=which):
-                spread[p, 2 * dofs :] = -from_after[which]
+                delta[p] = direct[p] - from_after[which, :TILE].astype(F32)
+                spread[p, 2 * dofs :] = -from_after[which, TILE:]
 
             @pl.when(where == 2)
             def _(p=p, which=which):
-                spread[p, :dofs] = -from_before[which]
-
-            term = dot(mine, spread[p], ((1,), (1,)))
-            total = term if total is None else total + term
-    second[:dofs] = total[:, :TILE]
-    second[dofs:] = jnp.concatenate([total[:, TILE:], jnp.zeros_like(total[:, TILE:])], axis=1)
-
-
-def spread_of(kind, index, coupling, from_before, from_after):
-    sub_dev, dofs, cols = coupling.shape
-    n_tiles = sub_dev * cols // TILE
-    return pl.pallas_call(
-        spread_kernel,
-        in_specs=[IN_SMEM] * 2 + [IN_VMEM] * 3,
-        out_specs=[IN_VMEM] * 2,
-        out_shape=[like((n_tiles, 3 * dofs, TILE), BF16), like((2 * dofs, TILE), F32)],
-        compiler_params=params(),
-        cost_estimate=cost(10**8, 2 * 10**6),
-    )(kind, index, coupling, from_before, from_after)
-
-
-def difference_kernel(
-    kind, index, r0, r1, r2, direct, from_before, from_after, coupling, second, delta, sent
-):
-    sub_dev, dofs, _ = coupling.shape
-    slots = kind.shape[1]
-    share = r0.shape[0]
-    for b, rows in enumerate((r0, r1, r2)):
-        sent[b * share : (b + 1) * share] = rows[...]
-    at = 3 * share
-    sent[at + dofs :] = second[...]
-    total = None
-    for i in range(sub_dev):
-        for t in range(slots):
-            p = i * slots + t
-            where, which = kind[i, t], index[i, t]
-
-            @pl.when(where == 0)
-            def _(p=p, t=t, which=which):
-                delta[p] = direct[p] - direct[which * slots + t]
-
-            @pl.when(where == 1)
-            def _(p=p, which=which):
-                delta[p] = direct[p] - from_after[which].astype(F32)
-
-            @pl.when(where == 2)
-            def _(p=p, which=which):
-                delta[p] = direct[p] - from_before[which].astype(F32)
-
-            term = dot(coupling[i, :, t * TILE : (t + 1) * TILE], delta[p].astype(BF16))
-            total = term if total is None else total + term
-    sent[at : at + dofs] = total
-
-
-def difference(kind, index, rows, direct, from_before, from_after, coupling, second):
-    rhs = direct.shape[2]
+                delta[p] = direct[p] - from_before[which, :TILE].astype(F32)
+                spread[p, :dofs] = -from_before[which, TILE:]
+
+            one = dot(mine, delta[p].astype(BF16))
+            two = dot(mine, spread[p], ((1,), (1,)))
+            first = one if first is None else first + one
+            second = two if second is None else second + two
+    sent[at : at + dofs] = first
+    sent[at + dofs : at + 2 * dofs] = second[:, :TILE]
+    sent[at + 2 * dofs :] = jnp.concatenate([second[:, TILE:], jnp.zeros_like(second[:, TILE:])], axis=1)
+
+
+def difference(kind, index, rows, direct, from_before, from_after, coupling):
+    n_tiles, _, rhs = direct.shape
     dofs = coupling.shape[1]
     return pl.pallas_call(
         difference_kernel,
-        in_specs=[IN_SMEM] * 2 + [IN_VMEM] * 8,
-        out_specs=[IN_VMEM] * 2,
+        in_specs=[IN_SMEM] * 2 + [IN_VMEM] * 7,
+        out_specs=[IN_VMEM] * 3,
         out_shape=[
             like(direct.shape, F32),
-            like((3 * rows[0].shape[0] + dofs + second.shape[0], rhs), F32),
+            like((n_tiles, 3 * dofs, TILE), BF16),
+            like((3 * rows[0].shape[0] + 3 * dofs, rhs), F32),
         ],
         compiler_params=params(),
         cost_estimate=cost(10**8, 3 * 10**6),
-    )(kind, index, *rows, direct, from_before, from_after, coupling, second)
+    )(kind, index, *rows, direct, from_before, from_after, coupling)
 
 
 def coarse_rows(got, share):
@@ -410,9 +359,11 @@
     coupling = jnp.einsum(
         "sjk,sjn->skn", corner_table, corner_coupling, preferred_element_type=F32
     ).astype(BF16)
-    def own_rows(part):
-        by_sub = lax.all_to_all(part.reshape(n_sub, share, rhs), "sub", 0, 0, tiled=True)
-        return jnp.sum(by_sub.astype(F32), axis=0)
+    def by_sub(part):
+        return lax.all_to_all(part.reshape(n_sub, share, rhs), "sub", 0, 0, tiled=True)
+
+    def summed(blocks):
+        return jnp.sum(blocks.astype(F32), axis=0)
 
     far = swapped(multipliers, "dom", 2)
     near = swapped(multipliers, "dom", 1)
@@ -428,31 +379,27 @@
     )
     inverse = lax.all_to_all(to_dom, "dom", 0, 0, tiled=True)
     part1 = first_part(inverse)
-    across = packed_coupling(after, before, coupling)
-    spread, second = spread_of(
-        kind, index, coupling, shifted(across[0], "sub", 1), shifted(across[1], "sub", -1)
-    )
     direct1, to_after, to_before = product(
-        schur_inverse, (multipliers, near, far, near_far), (after, before, all_signs)
+        schur_inverse, (multipliers, near, far, near_far), (after, before, all_signs), coupling
     )
     got_before, got_after = shifted(to_after, "sub", 1), shifted(to_before, "sub", -1)
-    rows = own_rows(part1)
+    rows = summed(by_sub(part1))
     rows1 = [shifted(rows, "sub", 1), rows, shifted(rows, "sub", -1)]
     got_before, got_after, rows1 = lax.optimization_barrier((got_before, got_after, rows1))
-    delta1, sent1 = difference(
-        kind, index, rows1, direct1, got_before, got_after, coupling, second
-    )
+    delta1, spread, sent1 = difference(kind, index, rows1, direct1, got_before, got_after, coupling)
     all1 = lax.all_gather(sent1, "dom", axis=0)
 
     u2, part2 = next_values(all1, delta1, spread, inverse, share)
     u2 = u2.reshape(multipliers.shape)
     far2 = swapped(u2, "dom", 2)
     near2 = swapped(u2, "dom", 1)
-    own = own_rows(part2)
-    near_far2 = swapped(far2, "dom", 1)
-    near_far2, own = lax.optimization_barrier((near_far2, own))
+    near_far2 = jnp.concatenate(
+        [swapped(far2[i : i + 1], "dom", 1) for i in range(sub_dev)], axis=0
+    )
+    (direct2,) = product(schur_inverse, (u2, near2, far2, near_far2))
+    by_sub2, direct2 = lax.optimization_barrier((by_sub(part2), direct2))
+    own = summed(by_sub2)
     rows2 = [own] + [swapped(own, "dom", m) for m in range(1, n_dom)]
-    (direct2,) = product(schur_inverse, (u2, near2, far2, near_far2))
     w2, to_after2, to_before2 = weighted(after, before, rows2, direct2, coupling)
     got_before2, got_after2 = shifted(to_after2, "sub", 1), shifted(to_before2, "sub", -1)
     result = last_values(kind, index, signs, w2, got_before2, got_after2)

time: 136 us -> 129 us (0.949)
  starting transfers between devices: 63.9 us -> 58.9 us
  waiting for transfers between devices: 26.6 us -> 24.6 us
  Pallas kernels: 23.8 us -> 21.9 us
    ppermute x8 -> x6, starting transfers between devices: 25.7 us -> 17.6 us  [shifted(): lax.ppermute(block, axis, [(i, (i + distance) % n) for i in range(n)])]
    all_to_all x2, starting transfers between devices: 21.6 us -> 25.9 us  [by_sub(): lax.all_to_all(part.reshape(n_sub, share, rhs), 'sub', 0, 0, tiled=True)]
    ppermute x8 -> x6, waiting for transfers between devices: 12.9 us -> 17 us  [shifted(): lax.ppermute(block, axis, [(i, (i + distance) % n) for i in range(n)])]
    ppermute x9 -> x12, waiting for transfers between devices: 5.97 us -> 2.59 us  [swapped(): return lax.ppermute(block, axis, [(i, i ^ mask) for i in range(n)])]
    all_to_all x2, waiting for transfers between devices: 4.45 us -> 1.69 us  [by_sub(): lax.all_to_all(part.reshape(n_sub, share, rhs), 'sub', 0, 0, tiled=True)]
    pallas_call x3 -> x1, Pallas kernels: 4.23 us -> 2.18 us  [difference(): pl.pallas_call(difference_kernel, in_specs=[IN_SMEM] * 2 + [IN_VMEM] * 7,...]
    ppermute x9 -> x12, starting transfers between devices: 11.9 us -> 10.7 us  [swapped(): return lax.ppermute(block, axis, [(i, i ^ mask) for i in range(n)])]
    unnamed x29 -> x33, local copies, waits for them, and re-layouts: 5.39 us -> 6.34 us
  transfers between devices with their start and end apart: 20 -> 21, of which waited for: 7 -> 10; matrix products, arithmetic and copies ran while one was open for 5% -> 7% of each run, Pallas kernels for 13% -> 12%
where the time goes in v3:
time: 129 us; the launch traced here: 128 us
  starting transfers between devices  58.9 us (46%)
  waiting for transfers between devices  24.6 us (19%)
  Pallas kernels  21.9 us (17%)
  blocking collectives  8.69 us (7%)
  local copies, waits for them, and re-layouts  7.1 us (6%)
  other arithmetic  4.77 us (4%)
  matrix products  1.69 us (1%)
    all_to_all x2, starting transfers between devices, by_sub(): lax.all_to_all(part.reshape(n_sub, share, rhs), 'sub', 0, 0, tiled=True)  25.9 us
    ppermute x6, starting transfers between devices, shifted(): lax.ppermute(block, axis, [(i, (i + distance) % n) for i in range(n)])  17.6 us
    ppermute x6, waiting for transfers between devices, shifted(): lax.ppermute(block, axis, [(i, (i + distance) % n) for i in range(n)])  17 us
    pallas_call x2, Pallas kernels, product(): pl.pallas_call(functools.partial(product_kernel, first), grid=(sub_dev,),...  14.1 us
    ppermute x12, starting transfers between devices, swapped(): return lax.ppermute(block, axis, [(i, i ^ mask) for i in range(n)])  10.7 us
    all_gather x1, blocking collectives, body(): all1 = lax.all_gather(sent1, 'dom', axis=0)  8.69 us
    unnamed x33, local copies, waits for them, and re-layouts  6.34 us
    all_to_all x1, starting transfers between devices, body(): inverse = lax.all_to_all(to_dom, 'dom', 0, 0, tiled=True)  4.66 us
  transfers between devices with their start and end apart: 21, of which 10 were waited for; matrix products, arithmetic and copies ran while one was open for 7% of the time, Pallas kernels for 12%

profile of v3, /device:TPU:1, one launch (start us, length us, event | category | flops | bytes accessed | tf_op | source)
XLA Modules:
  0.0 127.9 jit_solution(6204939859865969161)
XLA Ops:
  0.0 2.0 %collective-permute-start.1 = (bf16[4,512,128]{2,1,0:T(8,128)(2,1)}, bf16[4,512,128]{2,1,0:T(8,128)(2,1)S(1)}, u32[]{:S(2)}, u32[]{:S(2)}) collective-permute-start(bf16[4,512,128]{2,1,0:T(8,128)(2,1)} %refs_4_.1), channel_id=1, source_target_pairs={{0,2},{1,3},{2,0},{3,1},{4,6},{5,7},{6,4},{7,5},{8,10},{9,11},{10,... | collective-permute-start | bytes 1572872 | tf_op jit(solution)/shard_map/ppermute | solution.py:38
  2.0 0.8 compare_select_fusion.2.refs_2_
  2.8 0.1 fusion.6
  2.9 0.1 broadcast_bitcast_fusion
  3.0 1.1 copy.10
  4.1 0.4 copy.11
  4.5 0.3 reshape.46
  4.8 0.7 broadcast_subtract_fusion
  5.5 0.3 convolution_convert_fusion.refs_8_.coupling
  5.9 1.4 %convolution_bitcast_fusion = f32[64,128]{1,0:T(8,128)S(1)} fusion(bf16[4,512,128]{2,1,0:T(8,128)(2,1)} %refs_4_.1, bf16[4,64,512]{2,1,0:T(8,128)(2,1)S(1)} %convolution_convert_fusion.refs_8_.coupling, bf16[4,512]{1,0:T(4,128)(2,1)S(1)} %bitcast.22), kind=kOutput, calls=%fused_computation.1 | convolution fusion | flops 33685504 | bytes 823296 | tf_op jit(solution)/shard_map/skn,snr->kr/dot_general | solution.py:372
  7.3 0.8 pad_maximum_fusion.1
  8.0 4.7 %all-to-all-start = ((f32[4,192,128]{2,1,0:T(8,128)}), f32[4,192,128]{2,1,0:T(8,128)S(1)}, u32[]{:S(2)}, u32[]{:S(2)}) async-start(f32[4,192,128]{2,1,0:T(8,128)} %pad_maximum_fusion.1), calls=%async_computation | async-start | bytes 786432 | tf_op jit(solution)/shard_map/all_to_all | solution.py:380
  12.7 0.1 collective-permute-start
  12.8 0.0 collective-permute-done.1.refs_6_
  12.8 2.3 %collective-permute-start.2 = (bf16[4,512,128]{2,1,0:T(8,128)(2,1)S(1)}, bf16[4,512,128]{2,1,0:T(8,128)(2,1)S(1)}, u32[]{:S(2)}, u32[]{:S(2)}) collective-permute-start(bf16[4,512,128]{2,1,0:T(8,128)(2,1)S(1)} %collective-permute-done.1.refs_6_), channel_id=1, source_target_pairs={{0,1},{1,0},{2,3},{3,2},{4,5},{5,4},{6,7},{7,6},{8,9},{9,8},{10,11... | collective-permute-start | bytes 1572872 | tf_op jit(solution)/shard_map/ppermute | solution.py:38
  15.1 0.8 add_select_fusion
  15.9 3.4 %all-to-all-done.got.inverse = f32[4,192,128]{2,1,0:T(8,128)S(1)} async-done(((f32[4,192,128]{2,1,0:T(8,128)}), f32[4,192,128]{2,1,0:T(8,128)S(1)}, u32[]{:S(2)}, u32[]{:S(2)}) %all-to-all-start) | async-done | bytes 393248 | tf_op jit(solution)/shard_map/all_to_all | solution.py:380
  19.3 1.1 shard_map.65
  20.4 13.8 %all-to-all-start.1 = ((bf16[64,16,128]{2,1,0:T(8,128)(2,1)}), bf16[64,16,128]{2,1,0:T(8,128)(2,1)S(1)}, u32[]{:S(2)}, u32[]{:S(2)}) async-start(bf16[64,16,128]{2,1,0:T(8,128)(2,1)} %bitcast.3), calls=%async_computation.1 | async-start | bytes 524288 | tf_op jit(solution)/shard_map/all_to_all | solution.py:363
  34.1 0.1 convert_reduce_fusion.2
  34.2 0.6 compare_select_fusion
  34.8 0.0 collective-permute-done.2.refs_7_
  34.9 0.7 copy-done.12
  35.6 0.2 copy-done.13
  35.8 7.4 %shard_map.64 = (f32[16,128,128]{2,1,0:T(8,128)}, bf16[8,192,128]{2,1,0:T(8,128)(2,1)}, bf16[8,192,128]{2,1,0:T(8,128)(2,1)}) custom-call(s32[4,4]{1,0:T(4,128)} %get-tuple-element.50.refs_0_.after, s32[4,4]{1,0:T(4,128)} %get-tuple-element.49.refs_1_.before, f32[4,16]{1,0:T(4,128)} %copy-done.14, bf16[4,512,2048]{2,1,0:T(8,128)(2,1)} %refs_0_.1, ...), custom_call_target="tpu_custom_call" | custom-call | flops 1000 | bytes 1000 | tf_op jit(solution)/shard_map/pallas_call | solution.py:157
  43.2 2.6 %collective-permute-start.3 = (bf16[8,192,128]{2,1,0:T(8,128)(2,1)}, bf16[8,192,128]{2,1,0:T(8,128)(2,1)S(1)}, u32[]{:S(2)}, u32[]{:S(2)}) collective-permute-start(bf16[8,192,128]{2,1,0:T(8,128)(2,1)} %get-tuple-element.23), channel_id=1, source_target_pairs={{0,4},{4,8},{8,12},{12,16},{16,20},{20,24},{24,28},{28,32},{32,36}... | collective-permute-start | bytes 1179656 | tf_op jit(solution)/shard_map/ppermute | solution.py:33
  45.8 4.7 %collective-permute-start.4 = (bf16[8,192,128]{2,1,0:T(8,128)(2,1)}, bf16[8,192,128]{2,1,0:T(8,128)(2,1)S(1)}, u32[]{:S(2)}, u32[]{:S(2)}) collective-permute-start(bf16[8,192,128]{2,1,0:T(8,128)(2,1)} %get-tuple-element.24), channel_id=1, source_target_pairs={{0,252},{4,0},{8,4},{12,8},{16,12},{20,16},{24,20},{28,24},{32,28}... | collective-permute-start | bytes 1179656 | tf_op jit(solution)/shard_map/ppermute | solution.py:33
  50.5 0.0 all-to-all-done.1
  50.5 0.1 convert_reduce_fusion.1.r1
  50.6 2.9 %collective-permute-start.6 = (f32[16,128]{1,0:T(8,128)S(1)}, f32[16,128]{1,0:T(8,128)S(1)}, u32[]{:S(2)}, u32[]{:S(2)}) collective-permute-start(f32[16,128]{1,0:T(8,128)S(1)} %convert_reduce_fusion.1.r1), channel_id=1, source_target_pairs={{0,252},{4,0},{8,4},{12,8},{16,12},{20,16},{24,20},{28,24},{32,28}... | collective-permute-start | bytes 24584 | tf_op jit(solution)/shard_map/ppermute | solution.py:33
  53.5 0.2 collective-permute-start.5
  53.6 9.9 %collective-permute-done.6.r2 = f32[16,128]{1,0:T(8,128)S(1)} collective-permute-done((f32[16,128]{1,0:T(8,128)S(1)}, f32[16,128]{1,0:T(8,128)S(1)}, u32[]{:S(2)}, u32[]{:S(2)}) %collective-permute-start.6) | collective-permute-done | bytes 8224 | tf_op jit(solution)/shard_map/ppermute | solution.py:33
  63.6 0.9 copy-done.2
  64.5 1.2 copy-done.5
  65.7 2.2 %shard_map.66 = (f32[16,128,128]{2,1,0:T(8,128)S(1)}, bf16[16,192,128]{2,1,0:T(8,128)(2,1)S(1)}, f32[240,128]{1,0:T(8,128)S(1)}) custom-call(s32[4,4]{1,0:T(4,128)S(1)} %get-tuple-element.53.kind, s32[4,4]{1,0:T(4,128)S(1)} %get-tuple-element.51.index, f32[16,128]{1,0:T(8,128)S(1)} %collective-permute-done.5.r0, f32[16,128]{1,0:T(8,128)S(1)} %convert_reduce_fusion.1.r1, ...), custom_call_target="tpu_custom_call" | custom-call | flops 100000000 | bytes 3000000 | tf_op jit(solution)/shard_map/pallas_call | solution.py:247
  67.9 8.7 %all-gather = f32[960,128]{1,0:T(8,128)S(1)} all-gather(f32[240,128]{1,0:T(8,128)S(1)} %get-tuple-element.31), channel_id=2, replica_groups=mesh['sub'=64,'dom'=4] {'dom'}, dimensions={0}, use_global_device_ids=true | all-gather | bytes 614400 | tf_op jit(solution)/shard_map/all_gather | solution.py:390
  76.6 1.3 %shard_map.67 = (bf16[16,128,128]{2,1,0:T(8,128)(2,1)S(1)}, bf16[1024,128]{1,0:T(8,128)(2,1)}) custom-call(f32[4,240,128]{2,1,0:T(8,128)S(1)} %bitcast.17, f32[16,128,128]{2,1,0:T(8,128)S(1)} %get-tuple-element.32.delta, bf16[16,192,128]{2,1,0:T(8,128)(2,1)S(1)} %get-tuple-element.33.spread, f32[4,192,128]{2,1,0:T(8,128)S(1)} %all-to-all-done.got.inverse), custom_call_target="tpu_custom_call" | custom-call | flops 100000000 | bytes 3000000 | tf_op jit(solution)/shard_map/pallas_call | solution.py:283
  77.9 0.8 collective-permute-start.8
  78.8 0.4 collective-permute-start.7
  79.2 12.2 %all-to-all-start.2 = ((bf16[64,16,128]{2,1,0:T(8,128)(2,1)}), bf16[64,16,128]{2,1,0:T(8,128)(2,1)S(1)}, u32[]{:S(2)}, u32[]{:S(2)}) async-start(bf16[64,16,128]{2,1,0:T(8,128)(2,1)} %bitcast.5), calls=%async_computation.2 | async-start | bytes 524288 | tf_op jit(solution)/shard_map/all_to_all | solution.py:363
  91.5 0.9 collective-permute-start.9
  92.4 0.1 collective-permute-start.12
  92.5 0.4 collective-permute-start.11
  92.9 0.1 collective-permute-start.10
  93.0 0.4 collective-permute-done.9
  93.4 0.4 collective-permute-done.12
  93.7 0.2 collective-permute-done.11
  93.9 0.3 collective-permute-done.10
  94.3 0.9 pad_maximum_fusion.refs_4_
  95.1 0.0 collective-permute-done.7.refs_2_
  95.2 0.8 copy-done.11
  95.9 6.7 %shard_map.68.direct = f32[16,128,128]{2,1,0:T(8,128)} custom-call(bf16[4,512,2048]{2,1,0:T(8,128)(2,1)} %refs_0_.1, bf16[4,512,128]{2,1,0:T(8,128)(2,1)} %bitcast.20, bf16[4,512,128]{2,1,0:T(8,128)(2,1)} %copy-done.11, bf16[4,512,128]{2,1,0:T(8,128)(2,1)} %copy-done.9, bf16[4,512,128]{2,1,0:T(8,128)(2,1)} %pad_maximum_fusion.refs_4_), custom_call_target="tpu_custom_call" | custom-call | flops 1000 | bytes 1000 | tf_op jit(solution)/shard_map/pallas_call | solution.py:157
  102.6 1.7 %all-to-all-done.2 = bf16[64,16,128]{2,1,0:T(8,128)(2,1)S(1)} async-done(((bf16[64,16,128]{2,1,0:T(8,128)(2,1)}), bf16[64,16,128]{2,1,0:T(8,128)(2,1)S(1)}, u32[]{:S(2)}, u32[]{:S(2)}) %all-to-all-start.2) | async-done | bytes 262176 | tf_op jit(solution)/shard_map/all_to_all | solution.py:363
  104.3 0.1 convert_reduce_fusion.r0
  104.4 2.0 %collective-permute-start.15 = (f32[16,128]{1,0:T(8,128)S(1)}, f32[16,128]{1,0:T(8,128)S(1)}, u32[]{:S(2)}, u32[]{:S(2)}) collective-permute-start(f32[16,128]{1,0:T(8,128)S(1)} %convert_reduce_fusion.r0), channel_id=1, source_target_pairs={{0,3},{1,2},{2,1},{3,0},{4,7},{5,6},{6,5},{7,4},{8,11},{9,10},{10,... | collective-permute-start | bytes 24584 | tf_op jit(solution)/shard_map/ppermute | solution.py:38
  106.4 1.4 %collective-permute-start.14 = (f32[16,128]{1,0:T(8,128)S(1)}, f32[16,128]{1,0:T(8,128)S(1)}, u32[]{:S(2)}, u32[]{:S(2)}) collective-permute-start(f32[16,128]{1,0:T(8,128)S(1)} %convert_reduce_fusion.r0), channel_id=1, source_target_pairs={{0,2},{1,3},{2,0},{3,1},{4,6},{5,7},{6,4},{7,5},{8,10},{9,11},{10,... | collective-permute-start | bytes 24584 | tf_op jit(solution)/shard_map/ppermute | solution.py:38
  107.9 1.3 %collective-permute-done.14.r2 = f32[16,128]{1,0:T(8,128)S(1)} collective-permute-done((f32[16,128]{1,0:T(8,128)S(1)}, f32[16,128]{1,0:T(8,128)S(1)}, u32[]{:S(2)}, u32[]{:S(2)}) %collective-permute-start.14) | collective-permute-done | bytes 8224 | tf_op jit(solution)/shard_map/ppermute | solution.py:38
  109.2 1.2 copy-done.4
  110.4 1.3 %shard_map.69 = (bf16[16,128,128]{2,1,0:T(8,128)(2,1)S(1)}, bf16[8,128,128]{2,1,0:T(8,128)(2,1)S(1)}, bf16[8,128,128]{2,1,0:T(8,128)(2,1)S(1)}) custom-call(s32[4,4]{1,0:T(4,128)S(1)} %copy-done.8, s32[4,4]{1,0:T(4,128)S(1)} %copy-done.7, f32[16,128]{1,0:T(8,128)S(1)} %convert_reduce_fusion.r0, f32[16,128]{1,0:T(8,128)S(1)} %collective-permute-done.13.r1, ...), custom_call_target="tpu_custom_call" | custom-call | flops 100000000 | bytes 3000000 | tf_op jit(solution)/shard_map/pallas_call | solution.py:189
  111.8 2.3 %collective-permute-start.16 = (bf16[8,128,128]{2,1,0:T(8,128)(2,1)S(1)}, bf16[8,128,128]{2,1,0:T(8,128)(2,1)S(1)}, u32[]{:S(2)}, u32[]{:S(2)}) collective-permute-start(bf16[8,128,128]{2,1,0:T(8,128)(2,1)S(1)} %get-tuple-element.39), channel_id=1, source_target_pairs={{0,4},{4,8},{8,12},{12,16},{16,20},{20,24},{24,28},{28,32},{32,36}... | collective-permute-start | bytes 786440 | tf_op jit(solution)/shard_map/ppermute | solution.py:33
  114.0 5.0 %collective-permute-start.17 = (bf16[8,128,128]{2,1,0:T(8,128)(2,1)S(1)}, bf16[8,128,128]{2,1,0:T(8,128)(2,1)S(1)}, u32[]{:S(2)}, u32[]{:S(2)}) collective-permute-start(bf16[8,128,128]{2,1,0:T(8,128)(2,1)S(1)} %get-tuple-element.40), channel_id=1, source_target_pairs={{0,252},{4,0},{8,4},{12,8},{16,12},{20,16},{24,20},{28,24},{32,28}... | collective-permute-start | bytes 786440 | tf_op jit(solution)/shard_map/ppermute | solution.py:33
  119.1 5.3 %collective-permute-done.16.from_before = bf16[8,128,128]{2,1,0:T(8,128)(2,1)S(1)} collective-permute-done((bf16[8,128,128]{2,1,0:T(8,128)(2,1)S(1)}, bf16[8,128,128]{2,1,0:T(8,128)(2,1)S(1)}, u32[]{:S(2)}, u32[]{:S(2)}) %collective-permute-start.16) | collective-permute-done | bytes 262176 | tf_op jit(solution)/shard_map/ppermute | solution.py:33
  124.4 1.7 %collective-permute-done.17.from_after = bf16[8,128,128]{2,1,0:T(8,128)(2,1)S(1)} collective-permute-done((bf16[8,128,128]{2,1,0:T(8,128)(2,1)S(1)}, bf16[8,128,128]{2,1,0:T(8,128)(2,1)S(1)}, u32[]{:S(2)}, u32[]{:S(2)}) %collective-permute-start.17) | collective-permute-done | bytes 262176 | tf_op jit(solution)/shard_map/ppermute | solution.py:33
  126.1 1.8 %shard_map.70 = bf16[16,128,128]{2,1,0:T(8,128)(2,1)} custom-call(s32[4,4]{1,0:T(4,128)S(1)} %get-tuple-element.53.kind, s32[4,4]{1,0:T(4,128)S(1)} %get-tuple-element.51.index, f32[4,4]{1,0:T(4,128)S(1)} %get-tuple-element.44.signs, bf16[16,128,128]{2,1,0:T(8,128)(2,1)S(1)} %get-tuple-element.38.w, ...), custom_call_target="tpu_custom_call" | custom-call | flops 10000000 | bytes 3000000 | tf_op jit(solution)/shard_map/pallas_call | solution.py:317
  (37 shorter events, 0.1 us)
Async XLA Ops:
  0.0 5.5 %copy-start = (bf16[4,24,512]{2,1,0:T(8,128)(2,1)S(1)}, bf16[4,24,512]{2,1,0:T(8,128)(2,1)}, u32[]{:S(2)}) copy-start(bf16[4,24,512]{2,1,0:T(8,128)(2,1)} %param.8) | copy-start | bytes 294916
  0.0 12.8 %collective-permute-start.1 = (bf16[4,512,128]{2,1,0:T(8,128)(2,1)}, bf16[4,512,128]{2,1,0:T(8,128)(2,1)S(1)}, u32[]{:S(2)}, u32[]{:S(2)}) collective-permute-start(bf16[4,512,128]{2,1,0:T(8,128)(2,1)} %refs_4_.1), channel_id=1, source_target_pairs={{0,2},{1,3},{2,0},{3,1},{4,6},{5,7},{6,4},{7,5},{8,10},{9,11},{10,... | collective-permute-start | bytes 1572872 | tf_op jit(solution)/shard_map/ppermute | solution.py:38
  2.8 32.1 %copy-start.14 = (f32[4,16]{1,0:T(4,128)}, f32[4,16]{1,0:T(4,128)S(1)}, u32[]{:S(2)}) copy-start(f32[4,16]{1,0:T(4,128)S(1)} %compare_select_fusion.2.refs_2_) | copy-start | bytes 772
  5.9 29.0 %copy-start.1 = (bf16[4,64,512]{2,1,0:T(8,128)(2,1)}, bf16[4,64,512]{2,1,0:T(8,128)(2,1)S(1)}, u32[]{:S(2)}) copy-start(bf16[4,64,512]{2,1,0:T(8,128)(2,1)S(1)} %convolution_convert_fusion.refs_8_.coupling) | copy-start | bytes 786436
  8.0 11.2 %all-to-all-start = ((f32[4,192,128]{2,1,0:T(8,128)}), f32[4,192,128]{2,1,0:T(8,128)S(1)}, u32[]{:S(2)}, u32[]{:S(2)}) async-start(f32[4,192,128]{2,1,0:T(8,128)} %pad_maximum_fusion.1), calls=%async_computation | async-start | bytes 786432 | tf_op jit(solution)/shard_map/all_to_all | solution.py:380
  12.7 22.2 %collective-permute-start = (bf16[4,512,128]{2,1,0:T(8,128)(2,1)}, bf16[4,512,128]{2,1,0:T(8,128)(2,1)S(1)}, u32[]{:S(2)}, u32[]{:S(2)}) collective-permute-start(bf16[4,512,128]{2,1,0:T(8,128)(2,1)} %refs_4_.1), channel_id=1, source_target_pairs={{0,1},{1,0},{2,3},{3,2},{4,5},{5,4},{6,7},{7,6},{8,9},{9,8},{10,11... | collective-permute-start | bytes 1572872 | tf_op jit(solution)/shard_map/ppermute | solution.py:38
  12.8 22.1 %copy-start.10 = (bf16[4,512,128]{2,1,0:T(8,128)(2,1)}, bf16[4,512,128]{2,1,0:T(8,128)(2,1)S(1)}, u32[]{:S(2)}) copy-start(bf16[4,512,128]{2,1,0:T(8,128)(2,1)S(1)} %collective-permute-done.1.refs_6_) | copy-start | bytes 1572868
  12.8 22.0 %collective-permute-start.2 = (bf16[4,512,128]{2,1,0:T(8,128)(2,1)S(1)}, bf16[4,512,128]{2,1,0:T(8,128)(2,1)S(1)}, u32[]{:S(2)}, u32[]{:S(2)}) collective-permute-start(bf16[4,512,128]{2,1,0:T(8,128)(2,1)S(1)} %collective-permute-done.1.refs_6_), channel_id=1, source_target_pairs={{0,1},{1,0},{2,3},{3,2},{4,5},{5,4},{6,7},{7,6},{8,9},{9,8},{10,11... | collective-permute-start | bytes 1572872 | tf_op jit(solution)/shard_map/ppermute | solution.py:38
  20.4 30.1 %all-to-all-start.1 = ((bf16[64,16,128]{2,1,0:T(8,128)(2,1)}), bf16[64,16,128]{2,1,0:T(8,128)(2,1)S(1)}, u32[]{:S(2)}, u32[]{:S(2)}) async-start(bf16[64,16,128]{2,1,0:T(8,128)(2,1)} %bitcast.3), calls=%async_computation.1 | async-start | bytes 524288 | tf_op jit(solution)/shard_map/all_to_all | solution.py:363
  34.8 0.8 copy-start.12
  34.9 1.0 copy-start.13
  43.2 20.3 %collective-permute-start.3 = (bf16[8,192,128]{2,1,0:T(8,128)(2,1)}, bf16[8,192,128]{2,1,0:T(8,128)(2,1)S(1)}, u32[]{:S(2)}, u32[]{:S(2)}) collective-permute-start(bf16[8,192,128]{2,1,0:T(8,128)(2,1)} %get-tuple-element.23), channel_id=1, source_target_pairs={{0,4},{4,8},{8,12},{12,16},{16,20},{20,24},{24,28},{28,32},{32,36}... | collective-permute-start | bytes 1179656 | tf_op jit(solution)/shard_map/ppermute | solution.py:33
  45.8 17.7 %collective-permute-start.4 = (bf16[8,192,128]{2,1,0:T(8,128)(2,1)}, bf16[8,192,128]{2,1,0:T(8,128)(2,1)S(1)}, u32[]{:S(2)}, u32[]{:S(2)}) collective-permute-start(bf16[8,192,128]{2,1,0:T(8,128)(2,1)} %get-tuple-element.24), channel_id=1, source_target_pairs={{0,252},{4,0},{8,4},{12,8},{16,12},{20,16},{24,20},{28,24},{32,28}... | collective-permute-start | bytes 1179656 | tf_op jit(solution)/shard_map/ppermute | solution.py:33
  50.6 13.0 %collective-permute-start.6 = (f32[16,128]{1,0:T(8,128)S(1)}, f32[16,128]{1,0:T(8,128)S(1)}, u32[]{:S(2)}, u32[]{:S(2)}) collective-permute-start(f32[16,128]{1,0:T(8,128)S(1)} %convert_reduce_fusion.1.r1), channel_id=1, source_target_pairs={{0,252},{4,0},{8,4},{12,8},{16,12},{20,16},{24,20},{28,24},{32,28}... | collective-permute-start | bytes 24584 | tf_op jit(solution)/shard_map/ppermute | solution.py:33
  53.5 10.1 %collective-permute-start.5 = (f32[16,128]{1,0:T(8,128)S(1)}, f32[16,128]{1,0:T(8,128)S(1)}, u32[]{:S(2)}, u32[]{:S(2)}) collective-permute-start(f32[16,128]{1,0:T(8,128)S(1)} %convert_reduce_fusion.1.r1), channel_id=1, source_target_pairs={{0,4},{4,8},{8,12},{12,16},{16,20},{20,24},{24,28},{28,32},{32,36}... | collective-permute-start | bytes 24584 | tf_op jit(solution)/shard_map/ppermute | solution.py:33
  63.6 1.0 copy-start.2
  64.5 1.2 copy-start.5
  76.6 32.6 %copy-start.3 = (bf16[4,64,512]{2,1,0:T(8,128)(2,1)S(1)}, bf16[4,64,512]{2,1,0:T(8,128)(2,1)}, u32[]{:S(2)}) copy-start(bf16[4,64,512]{2,1,0:T(8,128)(2,1)} %copy-done.1) | copy-start | bytes 786436
  76.6 32.6 %copy-start.7 = (s32[4,4]{1,0:T(4,128)S(1)}, s32[4,4]{1,0:T(4,128)}, u32[]{:S(2)}) copy-start(s32[4,4]{1,0:T(4,128)} %get-tuple-element.49.refs_1_.before) | copy-start | bytes 196
  76.6 32.6 %copy-start.8 = (s32[4,4]{1,0:T(4,128)S(1)}, s32[4,4]{1,0:T(4,128)}, u32[]{:S(2)}) copy-start(s32[4,4]{1,0:T(4,128)} %get-tuple-element.50.refs_0_.after) | copy-start | bytes 196
  77.9 17.2 %copy-start.6 = (bf16[16,128,128]{2,1,0:T(8,128)(2,1)}, bf16[16,128,128]{2,1,0:T(8,128)(2,1)S(1)}, u32[]{:S(2)}) copy-start(bf16[16,128,128]{2,1,0:T(8,128)(2,1)S(1)} %get-tuple-element.35) | copy-start | bytes 1572868
  77.9 13.5 %collective-permute-start.8 = (bf16[4,512,128]{2,1,0:T(8,128)(2,1)S(1)}, bf16[4,512,128]{2,1,0:T(8,128)(2,1)S(1)}, u32[]{:S(2)}, u32[]{:S(2)}) collective-permute-start(bf16[4,512,128]{2,1,0:T(8,128)(2,1)S(1)} %bitcast.18), channel_id=1, source_target_pairs={{0,2},{1,3},{2,0},{3,1},{4,6},{5,7},{6,4},{7,5},{8,10},{9,11},{10,... | collective-permute-start | bytes 1572872 | tf_op jit(solution)/shard_map/ppermute | solution.py:38
  78.8 16.4 %collective-permute-start.7 = (bf16[4,512,128]{2,1,0:T(8,128)(2,1)S(1)}, bf16[4,512,128]{2,1,0:T(8,128)(2,1)S(1)}, u32[]{:S(2)}, u32[]{:S(2)}) collective-permute-start(bf16[4,512,128]{2,1,0:T(8,128)(2,1)S(1)} %bitcast.19), channel_id=1, source_target_pairs={{0,1},{1,0},{2,3},{3,2},{4,5},{5,4},{6,7},{7,6},{8,9},{9,8},{10,11... | collective-permute-start | bytes 1572872 | tf_op jit(solution)/shard_map/ppermute | solution.py:38
  79.2 25.1 %all-to-all-start.2 = ((bf16[64,16,128]{2,1,0:T(8,128)(2,1)}), bf16[64,16,128]{2,1,0:T(8,128)(2,1)S(1)}, u32[]{:S(2)}, u32[]{:S(2)}) async-start(bf16[64,16,128]{2,1,0:T(8,128)(2,1)} %bitcast.5), calls=%async_computation.2 | async-start | bytes 524288 | tf_op jit(solution)/shard_map/all_to_all | solution.py:363
  91.4 3.7 %copy-start.9 = (bf16[4,512,128]{2,1,0:T(8,128)(2,1)}, bf16[4,512,128]{2,1,0:T(8,128)(2,1)S(1)}, u32[]{:S(2)}) copy-start(bf16[4,512,128]{2,1,0:T(8,128)(2,1)S(1)} %collective-permute-done.8.refs_3_) | copy-start | bytes 1572868
  91.5 1.9 %collective-permute-start.9 = (bf16[1,512,128]{2,1,0:T(8,128)(2,1)S(1)}, bf16[1,512,128]{2,1,0:T(8,128)(2,1)S(1)}, u32[]{:S(2)}, u32[]{:S(2)}) collective-permute-start(bf16[1,512,128]{2,1,0:T(8,128)(2,1)S(1)} %get-tuple-element.45), channel_id=1, source_target_pairs={{0,1},{1,0},{2,3},{3,2},{4,5},{5,4},{6,7},{7,6},{8,9},{9,8},{10,11... | collective-permute-start | bytes 393224 | tf_op jit(solution)/shard_map/ppermute | solution.py:38
  92.4 1.3 %collective-permute-start.12 = (bf16[1,512,128]{2,1,0:T(8,128)(2,1)S(1)}, bf16[1,512,128]{2,1,0:T(8,128)(2,1)S(1)}, u32[]{:S(2)}, u32[]{:S(2)}) collective-permute-start(bf16[1,512,128]{2,1,0:T(8,128)(2,1)S(1)} %get-tuple-element.46), channel_id=1, source_target_pairs={{0,1},{1,0},{2,3},{3,2},{4,5},{5,4},{6,7},{7,6},{8,9},{9,8},{10,11... | collective-permute-start | bytes 393224 | tf_op jit(solution)/shard_map/ppermute | solution.py:38
  92.5 1.4 %collective-permute-start.11 = (bf16[1,512,128]{2,1,0:T(8,128)(2,1)S(1)}, bf16[1,512,128]{2,1,0:T(8,128)(2,1)S(1)}, u32[]{:S(2)}, u32[]{:S(2)}) collective-permute-start(bf16[1,512,128]{2,1,0:T(8,128)(2,1)S(1)} %get-tuple-element.47), channel_id=1, source_target_pairs={{0,1},{1,0},{2,3},{3,2},{4,5},{5,4},{6,7},{7,6},{8,9},{9,8},{10,11... | collective-permute-start | bytes 393224 | tf_op jit(solution)/shard_map/ppermute | solution.py:38
  92.9 1.3 %collective-permute-start.10 = (bf16[1,512,128]{2,1,0:T(8,128)(2,1)S(1)}, bf16[1,512,128]{2,1,0:T(8,128)(2,1)S(1)}, u32[]{:S(2)}, u32[]{:S(2)}) collective-permute-start(bf16[1,512,128]{2,1,0:T(8,128)(2,1)S(1)} %get-tuple-element.48), channel_id=1, source_target_pairs={{0,1},{1,0},{2,3},{3,2},{4,5},{5,4},{6,7},{7,6},{8,9},{9,8},{10,11... | collective-permute-start | bytes 393224 | tf_op jit(solution)/shard_map/ppermute | solution.py:38
  95.1 0.8 copy-start.11
  104.4 3.4 %collective-permute-start.15 = (f32[16,128]{1,0:T(8,128)S(1)}, f32[16,128]{1,0:T(8,128)S(1)}, u32[]{:S(2)}, u32[]{:S(2)}) collective-permute-start(f32[16,128]{1,0:T(8,128)S(1)} %convert_reduce_fusion.r0), channel_id=1, source_target_pairs={{0,3},{1,2},{2,1},{3,0},{4,7},{5,6},{6,5},{7,4},{8,11},{9,10},{10,... | collective-permute-start | bytes 24584 | tf_op jit(solution)/shard_map/ppermute | solution.py:38
  106.4 2.8 %collective-permute-start.14 = (f32[16,128]{1,0:T(8,128)S(1)}, f32[16,128]{1,0:T(8,128)S(1)}, u32[]{:S(2)}, u32[]{:S(2)}) collective-permute-start(f32[16,128]{1,0:T(8,128)S(1)} %convert_reduce_fusion.r0), channel_id=1, source_target_pairs={{0,2},{1,3},{2,0},{3,1},{4,6},{5,7},{6,4},{7,5},{8,10},{9,11},{10,... | collective-permute-start | bytes 24584 | tf_op jit(solution)/shard_map/ppermute | solution.py:38
  107.8 1.3 %collective-permute-start.13 = (f32[16,128]{1,0:T(8,128)S(1)}, f32[16,128]{1,0:T(8,128)S(1)}, u32[]{:S(2)}, u32[]{:S(2)}) collective-permute-start(f32[16,128]{1,0:T(8,128)S(1)} %convert_reduce_fusion.r0), channel_id=1, source_target_pairs={{0,1},{1,0},{2,3},{3,2},{4,5},{5,4},{6,7},{7,6},{8,9},{9,8},{10,11... | collective-permute-start | bytes 24584 | tf_op jit(solution)/shard_map/ppermute | solution.py:38
  109.2 1.2 copy-start.4
  111.8 12.6 %collective-permute-start.16 = (bf16[8,128,128]{2,1,0:T(8,128)(2,1)S(1)}, bf16[8,128,128]{2,1,0:T(8,128)(2,1)S(1)}, u32[]{:S(2)}, u32[]{:S(2)}) collective-permute-start(bf16[8,128,128]{2,1,0:T(8,128)(2,1)S(1)} %get-tuple-element.39), channel_id=1, source_target_pairs={{0,4},{4,8},{8,12},{12,16},{16,20},{20,24},{24,28},{28,32},{32,36}... | collective-permute-start | bytes 786440 | tf_op jit(solution)/shard_map/ppermute | solution.py:33
  114.0 12.0 %collective-permute-start.17 = (bf16[8,128,128]{2,1,0:T(8,128)(2,1)S(1)}, bf16[8,128,128]{2,1,0:T(8,128)(2,1)S(1)}, u32[]{:S(2)}, u32[]{:S(2)}) collective-permute-start(bf16[8,128,128]{2,1,0:T(8,128)(2,1)S(1)} %get-tuple-element.40), channel_id=1, source_target_pairs={{0,252},{4,0},{8,4},{12,8},{16,12},{20,16},{24,20},{28,24},{32,28}... | collective-permute-start | bytes 786440 | tf_op jit(solution)/shard_map/ppermute | solution.py:33

commit v4 on v3

--- a/solution.py
+++ b/solution.py
@@ -14,6 +14,7 @@
 MOST_VMEM_BYTES = 54 * 1024 * 1024
 IN_SMEM = pl.BlockSpec(memory_space=pltpu.SMEM)
 IN_VMEM = pl.BlockSpec(memory_space=pltpu.VMEM)
+IN_HBM = pl.BlockSpec(memory_space=pltpu.HBM)
 
 
 def like(shape, dtype):
@@ -168,7 +169,11 @@
     )(*tables, schur_inverse, *pieces, *([coupling] if first else []))
 
 
-def weighted_kernel(after, before, r0, r1, r2, r3, direct, coupling, w_ref, to_after, to_before, coarse):
+def weighted_kernel(
+    after, before, r0, r1, r2, r3, direct_in, coupling, w_ref, to_after, to_before, coarse, direct, sem
+):
+    fetch = pltpu.make_async_copy(direct_in, direct, sem.at[0])
+    fetch.start()
     share = r0.shape[0]
     dom = lax.axis_index("dom")
     for m, rows in enumerate((r0, r1, r2, r3)):
@@ -176,6 +181,7 @@
     high, low = split(coarse[...])
     sub_dev = coupling.shape[0]
     slots = direct.shape[0] // sub_dev
+    fetch.wait()
     for i in range(sub_dev):
         for t in range(slots):
             own = coupling[i, :, t * TILE : (t + 1) * TILE]
@@ -188,16 +194,24 @@
     packed = (2 * after.shape[1], TILE, rhs)
     return pl.pallas_call(
         weighted_kernel,
-        in_specs=[IN_SMEM] * 2 + [IN_VMEM] * 6,
+        in_specs=[IN_SMEM] * 2 + [IN_VMEM] * 4 + [IN_HBM, IN_VMEM],
         out_specs=[IN_VMEM] * 3,
         out_shape=[like(direct.shape, BF16), like(packed, BF16), like(packed, BF16)],
-        scratch_shapes=[pltpu.VMEM((4 * rows[0].shape[0], rhs), F32)],
+        scratch_shapes=[
+            pltpu.VMEM((4 * rows[0].shape[0], rhs), F32),
+            pltpu.VMEM(direct.shape, F32),
+            pltpu.SemaphoreType.DMA((1,)),
+        ],
         compiler_params=params(),
         cost_estimate=cost(10**8, 3 * 10**6),
     )(after, before, *rows, direct, coupling)
 
 
-def difference_kernel(kind, index, r0, r1, r2, direct, from_before, from_after, coupling, delta, spread, sent):
+def difference_kernel(
+    kind, index, r0, r1, r2, direct_in, from_before, from_after, coupling, delta, spread, sent, direct, sem
+):
+    fetch = pltpu.make_async_copy(direct_in, direct, sem.at[0])
+    fetch.start()
     sub_dev, dofs, _ = coupling.shape
     share = r0.shape[0]
     for b, rows in enumerate((r0, r1, r2)):
@@ -217,28 +231,39 @@
             spread[p, 2 * dofs :] = blank
 
             @pl.when(where == 0)
-            def _(p=p, i=i, t=t, which=which, columns=columns):
-                delta[p] = direct[p] - direct[which * slots + t]
+            def _(p=p, i=i, which=which, columns=columns):
                 other = coupling[i, :, columns].astype(F32) - coupling[which, :, columns].astype(F32)
                 spread[p, dofs : 2 * dofs] = other.astype(BF16)
 
             @pl.when(where == 1)
             def _(p=p, which=which):
-                delta[p] = direct[p] - from_after[which, :TILE].astype(F32)
                 spread[p, 2 * dofs :] = -from_after[which, TILE:]
 
             @pl.when(where == 2)
             def _(p=p, which=which):
-                delta[p] = direct[p] - from_before[which, :TILE].astype(F32)
                 spread[p, :dofs] = -from_before[which, TILE:]
 
-            one = dot(mine, delta[p].astype(BF16))
             two = dot(mine, spread[p], ((1,), (1,)))
+            second = two if second is None else second + two
+    sent[at + dofs : at + 2 * dofs] = second[:, :TILE]
+    rest = second[:, TILE:]
+    sent[at + 2 * dofs :] = jnp.concatenate([rest[: dofs // 2], rest[dofs // 2 :]], axis=1)
+    fetch.wait()
+    for i in range(sub_dev):
+        for t in range(slots):
+            p = i * slots + t
+            other = chosen(
+                kind[i, t],
+                index[i, t],
+                lambda j, t=t: direct[j * slots + t],
+                lambda j: from_after[j, :TILE],
+                lambda j: from_before[j, :TILE],
+            )
+            value = direct[p] - other
+            delta[p] = value
+            one = dot(coupling[i, :, t * TILE : (t + 1) * TILE], value.astype(BF16))
             first = one if first is None else first + one
-            second = two if second is None else second + two
     sent[at : at + dofs] = first
-    sent[at + dofs : at + 2 * dofs] = second[:, :TILE]
-    sent[at + 2 * dofs :] = jnp.concatenate([second[:, TILE:], jnp.zeros_like(second[:, TILE:])], axis=1)
 
 
 def difference(kind, index, rows, direct, from_before, from_after, coupling):
@@ -246,13 +271,14 @@
     dofs = coupling.shape[1]
     return pl.pallas_call(
         difference_kernel,
-        in_specs=[IN_SMEM] * 2 + [IN_VMEM] * 7,
+        in_specs=[IN_SMEM] * 2 + [IN_VMEM] * 3 + [IN_HBM] + [IN_VMEM] * 3,
         out_specs=[IN_VMEM] * 3,
         out_shape=[
             like(direct.shape, F32),
             like((n_tiles, 3 * dofs, TILE), BF16),
-            like((3 * rows[0].shape[0] + 3 * dofs, rhs), F32),
+            like((3 * rows[0].shape[0] + 2 * dofs + dofs // 2, rhs), F32),
         ],
+        scratch_shapes=[pltpu.VMEM(direct.shape, F32), pltpu.SemaphoreType.DMA((1,))],
         compiler_params=params(),
         cost_estimate=cost(10**8, 3 * 10**6),
     )(kind, index, *rows, direct, from_before, from_after, coupling)
@@ -269,7 +295,9 @@
     at = 3 * share
     total = (got[0, at:] + got[1, at:]) + (got[2, at:] + got[3, at:])
     load = total[:dofs] + exact_dot(total[dofs : 2 * dofs], coarse[:TILE])
-    load = load + exact_dot(total[2 * dofs :, : 3 * dofs - TILE], coarse[TILE:])
+    rest = total[2 * dofs :]
+    rest = jnp.concatenate([rest[:, :dofs], rest[:, dofs:]], axis=0)
+    load = load + exact_dot(rest, coarse[TILE:])
     partial_rows(inverse, load, part)
     high, low = split(coarse)
     for p in range(delta.shape[0]):
@@ -290,27 +318,25 @@
     )(got, delta, spread, inverse)
 
 
+def chosen(where, which, own, from_after, from_before):
+    after = from_after(jnp.where(where == 1, which, 0)).astype(F32)
+    before = from_before(jnp.where(where == 2, which, 0)).astype(F32)
+    return jnp.where(where == 0, own(jnp.where(where == 0, which, 0)).astype(F32), jnp.where(where == 1, after, before))
+
+
 def last_kernel(kind, index, signs, w, from_before, from_after, out):
     sub_dev, slots = kind.shape
     for i in range(sub_dev):
         for t in range(slots):
             p = i * slots + t
-            where, which = kind[i, t], index[i, t]
-
-            def put(tile, p=p, i=i, t=t):
-                out[p] = (signs[i, t] * (w[p].astype(F32) - tile.astype(F32))).astype(BF16)
-
-            @pl.when(where == 0)
-            def _(put=put, which=which, t=t):
-                put(w[which * slots + t])
-
-            @pl.when(where == 1)
-            def _(put=put, which=which):
-                put(from_after[which])
-
-            @pl.when(where == 2)
-            def _(put=put, which=which):
-                put(from_before[which])
+            other = chosen(
+                kind[i, t],
+                index[i, t],
+                lambda j, t=t: w[j * slots + t],
+                lambda j: from_after[j],
+                lambda j: from_before[j],
+            )
+            out[p] = (signs[i, t] * (w[p].astype(F32) - other)).astype(BF16)
 
 
 def last_values(kind, index, signs, w, from_before, from_after):

time: 129 us -> 129 us (level)
  transfers between devices with their start and end apart: 21 -> 21, of which waited for: 10 -> 12; matrix products, arithmetic and copies ran while one was open for 7% -> 7% of each run, Pallas kernels for 12% -> 12%
where the time goes in v4:
time: 129 us; the launch traced here: 128 us
  starting transfers between devices  58.9 us (46%)
  waiting for transfers between devices  24.5 us (19%)
  Pallas kernels  22.3 us (17%)
  blocking collectives  8.49 us (7%)
  local copies, waits for them, and re-layouts  7.09 us (5%)
  other arithmetic  4.77 us (4%)
  matrix products  1.69 us (1%)
    all_to_all x2, starting transfers between devices, by_sub(): lax.all_to_all(part.reshape(n_sub, share, rhs), 'sub', 0, 0, tiled=True)  26 us
    ppermute x6, starting transfers between devices, shifted(): lax.ppermute(block, axis, [(i, (i + distance) % n) for i in range(n)])  17.6 us
    ppermute x6, waiting for transfers between devices, shifted(): lax.ppermute(block, axis, [(i, (i + distance) % n) for i in range(n)])  17 us
    pallas_call x2, Pallas kernels, product(): pl.pallas_call(functools.partial(product_kernel, first), grid=(sub_dev,),...  14.1 us
    ppermute x12, starting transfers between devices, swapped(): return lax.ppermute(block, axis, [(i, i ^ mask) for i in range(n)])  10.7 us
    all_gather x1, blocking collectives, body(): all1 = lax.all_gather(sent1, 'dom', axis=0)  8.49 us
    unnamed x33, local copies, waits for them, and re-layouts  6.34 us
    all_to_all x1, starting transfers between devices, body(): inverse = lax.all_to_all(to_dom, 'dom', 0, 0, tiled=True)  4.66 us
  transfers between devices with their start and end apart: 21, of which 12 were waited for; matrix products, arithmetic and copies ran while one was open for 7% of the time, Pallas kernels for 12%

profile of v4, /device:TPU:1, one launch (start us, length us, event | category | flops | bytes accessed | tf_op | source)
XLA Modules:
  0.0 127.9 jit_solution(4229502386082340712)
XLA Ops:
  0.0 2.0 %collective-permute-start.1 = (bf16[4,512,128]{2,1,0:T(8,128)(2,1)}, bf16[4,512,128]{2,1,0:T(8,128)(2,1)S(1)}, u32[]{:S(2)}, u32[]{:S(2)}) collective-permute-start(bf16[4,512,128]{2,1,0:T(8,128)(2,1)} %refs_4_.1), channel_id=1, source_target_pairs={{0,2},{1,3},{2,0},{3,1},{4,6},{5,7},{6,4},{7,5},{8,10},{9,11},{10,... | collective-permute-start | bytes 1572872 | tf_op jit(solution)/shard_map/ppermute | solution.py:39
  2.0 0.8 compare_select_fusion.2.refs_2_
  2.8 0.1 fusion.6
  2.9 0.1 broadcast_bitcast_fusion
  3.0 1.1 copy.10
  4.1 0.4 copy.11
  4.5 0.3 reshape.46
  4.8 0.7 broadcast_subtract_fusion
  5.5 0.3 convolution_convert_fusion.refs_8_.coupling
  5.9 1.4 %convolution_bitcast_fusion = f32[64,128]{1,0:T(8,128)S(1)} fusion(bf16[4,512,128]{2,1,0:T(8,128)(2,1)} %refs_4_.1, bf16[4,64,512]{2,1,0:T(8,128)(2,1)S(1)} %convolution_convert_fusion.refs_8_.coupling, bf16[4,512]{1,0:T(4,128)(2,1)S(1)} %bitcast.22), kind=kOutput, calls=%fused_computation.1 | convolution fusion | flops 33685504 | bytes 823296 | tf_op jit(solution)/shard_map/skn,snr->kr/dot_general | solution.py:398
  7.3 0.8 pad_maximum_fusion.1
  8.0 4.7 %all-to-all-start = ((f32[4,192,128]{2,1,0:T(8,128)}), f32[4,192,128]{2,1,0:T(8,128)S(1)}, u32[]{:S(2)}, u32[]{:S(2)}) async-start(f32[4,192,128]{2,1,0:T(8,128)} %pad_maximum_fusion.1), calls=%async_computation | async-start | bytes 786432 | tf_op jit(solution)/shard_map/all_to_all | solution.py:406
  12.7 0.1 collective-permute-start
  12.8 0.0 collective-permute-done.1.refs_6_
  12.8 2.3 %collective-permute-start.2 = (bf16[4,512,128]{2,1,0:T(8,128)(2,1)S(1)}, bf16[4,512,128]{2,1,0:T(8,128)(2,1)S(1)}, u32[]{:S(2)}, u32[]{:S(2)}) collective-permute-start(bf16[4,512,128]{2,1,0:T(8,128)(2,1)S(1)} %collective-permute-done.1.refs_6_), channel_id=1, source_target_pairs={{0,1},{1,0},{2,3},{3,2},{4,5},{5,4},{6,7},{7,6},{8,9},{9,8},{10,11... | collective-permute-start | bytes 1572872 | tf_op jit(solution)/shard_map/ppermute | solution.py:39
  15.1 0.8 add_select_fusion
  15.9 3.4 %all-to-all-done.got.inverse = f32[4,192,128]{2,1,0:T(8,128)S(1)} async-done(((f32[4,192,128]{2,1,0:T(8,128)}), f32[4,192,128]{2,1,0:T(8,128)S(1)}, u32[]{:S(2)}, u32[]{:S(2)}) %all-to-all-start) | async-done | bytes 393248 | tf_op jit(solution)/shard_map/all_to_all | solution.py:406
  19.3 1.1 shard_map.65
  20.4 13.8 %all-to-all-start.1 = ((bf16[64,16,128]{2,1,0:T(8,128)(2,1)}), bf16[64,16,128]{2,1,0:T(8,128)(2,1)S(1)}, u32[]{:S(2)}, u32[]{:S(2)}) async-start(bf16[64,16,128]{2,1,0:T(8,128)(2,1)} %bitcast.3), calls=%async_computation.1 | async-start | bytes 524288 | tf_op jit(solution)/shard_map/all_to_all | solution.py:389
  34.1 0.1 convert_reduce_fusion.2
  34.2 0.6 compare_select_fusion
  34.8 0.0 collective-permute-done.refs_5_
  34.9 0.7 copy-done.12
  35.6 0.2 copy-done.13
  35.8 7.4 %shard_map.64 = (f32[16,128,128]{2,1,0:T(8,128)}, bf16[8,192,128]{2,1,0:T(8,128)(2,1)}, bf16[8,192,128]{2,1,0:T(8,128)(2,1)}) custom-call(s32[4,4]{1,0:T(4,128)} %get-tuple-element.50.refs_0_.after, s32[4,4]{1,0:T(4,128)} %get-tuple-element.49.refs_1_.before, f32[4,16]{1,0:T(4,128)} %copy-done.14, bf16[4,512,2048]{2,1,0:T(8,128)(2,1)} %refs_0_.1, ...), custom_call_target="tpu_custom_call" | custom-call | flops 1000 | bytes 1000 | tf_op jit(solution)/shard_map/pallas_call | solution.py:158
  43.2 2.6 %collective-permute-start.3 = (bf16[8,192,128]{2,1,0:T(8,128)(2,1)}, bf16[8,192,128]{2,1,0:T(8,128)(2,1)S(1)}, u32[]{:S(2)}, u32[]{:S(2)}) collective-permute-start(bf16[8,192,128]{2,1,0:T(8,128)(2,1)} %get-tuple-element.23), channel_id=1, source_target_pairs={{0,4},{4,8},{8,12},{12,16},{16,20},{20,24},{24,28},{28,32},{32,36}... | collective-permute-start | bytes 1179656 | tf_op jit(solution)/shard_map/ppermute | solution.py:34
  45.8 4.7 %collective-permute-start.4 = (bf16[8,192,128]{2,1,0:T(8,128)(2,1)}, bf16[8,192,128]{2,1,0:T(8,128)(2,1)S(1)}, u32[]{:S(2)}, u32[]{:S(2)}) collective-permute-start(bf16[8,192,128]{2,1,0:T(8,128)(2,1)} %get-tuple-element.24), channel_id=1, source_target_pairs={{0,252},{4,0},{8,4},{12,8},{16,12},{20,16},{24,20},{28,24},{32,28}... | collective-permute-start | bytes 1179656 | tf_op jit(solution)/shard_map/ppermute | solution.py:34
  50.5 0.1 convert_reduce_fusion.1.r1
  50.6 2.9 %collective-permute-start.6 = (f32[16,128]{1,0:T(8,128)S(1)}, f32[16,128]{1,0:T(8,128)S(1)}, u32[]{:S(2)}, u32[]{:S(2)}) collective-permute-start(f32[16,128]{1,0:T(8,128)S(1)} %convert_reduce_fusion.1.r1), channel_id=1, source_target_pairs={{0,252},{4,0},{8,4},{12,8},{16,12},{20,16},{24,20},{28,24},{32,28}... | collective-permute-start | bytes 24584 | tf_op jit(solution)/shard_map/ppermute | solution.py:34
  53.5 0.2 collective-permute-start.5
  53.6 9.9 %collective-permute-done.6.r2 = f32[16,128]{1,0:T(8,128)S(1)} collective-permute-done((f32[16,128]{1,0:T(8,128)S(1)}, f32[16,128]{1,0:T(8,128)S(1)}, u32[]{:S(2)}, u32[]{:S(2)}) %collective-permute-start.6) | collective-permute-done | bytes 8224 | tf_op jit(solution)/shard_map/ppermute | solution.py:34
  63.6 0.9 copy-done.2
  64.5 1.2 copy-done.5
  65.7 2.6 %shard_map.66 = (f32[16,128,128]{2,1,0:T(8,128)S(1)}, bf16[16,192,128]{2,1,0:T(8,128)(2,1)S(1)}, f32[208,128]{1,0:T(8,128)S(1)}) custom-call(s32[4,4]{1,0:T(4,128)S(1)} %get-tuple-element.53.kind, s32[4,4]{1,0:T(4,128)S(1)} %get-tuple-element.51.index, f32[16,128]{1,0:T(8,128)S(1)} %collective-permute-done.5.r0, f32[16,128]{1,0:T(8,128)S(1)} %convert_reduce_fusion.1.r1, ...), custom_call_target="tpu_custom_call" | custom-call | flops 100000000 | bytes 3000000 | tf_op jit(solution)/shard_map/pallas_call | solution.py:272
  68.3 8.5 %all-gather = f32[832,128]{1,0:T(8,128)S(1)} all-gather(f32[208,128]{1,0:T(8,128)S(1)} %get-tuple-element.31), channel_id=2, replica_groups=mesh['sub'=64,'dom'=4] {'dom'}, dimensions={0}, use_global_device_ids=true | all-gather | bytes 532480 | tf_op jit(solution)/shard_map/all_gather | solution.py:416
  76.8 1.3 %shard_map.67 = (bf16[16,128,128]{2,1,0:T(8,128)(2,1)S(1)}, bf16[1024,128]{1,0:T(8,128)(2,1)}) custom-call(f32[4,208,128]{2,1,0:T(8,128)S(1)} %bitcast.17, f32[16,128,128]{2,1,0:T(8,128)S(1)} %get-tuple-element.32.delta, bf16[16,192,128]{2,1,0:T(8,128)(2,1)S(1)} %get-tuple-element.33.spread, f32[4,192,128]{2,1,0:T(8,128)S(1)} %all-to-all-done.got.inverse), custom_call_target="tpu_custom_call" | custom-call | flops 100000000 | bytes 3000000 | tf_op jit(solution)/shard_map/pallas_call | solution.py:311
  78.1 0.7 collective-permute-start.8
  78.8 0.4 collective-permute-start.7
  79.2 12.2 %all-to-all-start.2 = ((bf16[64,16,128]{2,1,0:T(8,128)(2,1)}), bf16[64,16,128]{2,1,0:T(8,128)(2,1)S(1)}, u32[]{:S(2)}, u32[]{:S(2)}) async-start(bf16[64,16,128]{2,1,0:T(8,128)(2,1)} %bitcast.5), calls=%async_computation.2 | async-start | bytes 524288 | tf_op jit(solution)/shard_map/all_to_all | solution.py:389
  91.4 0.1 collective-permute-done.8.refs_3_
  91.5 1.1 collective-permute-start.9
  92.6 0.1 collective-permute-start.12
  92.7 0.4 collective-permute-start.11
  93.1 0.1 collective-permute-start.10
  93.2 0.4 collective-permute-done.9
  93.6 0.4 collective-permute-done.12
  94.0 0.2 collective-permute-done.11
  94.1 0.3 collective-permute-done.10
  94.5 0.9 pad_maximum_fusion.refs_4_
  95.4 0.8 copy-done.11
  96.1 6.7 %shard_map.68.direct_in = f32[16,128,128]{2,1,0:T(8,128)} custom-call(bf16[4,512,2048]{2,1,0:T(8,128)(2,1)} %refs_0_.1, bf16[4,512,128]{2,1,0:T(8,128)(2,1)} %bitcast.20, bf16[4,512,128]{2,1,0:T(8,128)(2,1)} %copy-done.11, bf16[4,512,128]{2,1,0:T(8,128)(2,1)} %copy-done.9, bf16[4,512,128]{2,1,0:T(8,128)(2,1)} %pad_maximum_fusion.refs_4_), custom_call_target="tpu_custom_call" | custom-call | flops 1000 | bytes 1000 | tf_op jit(solution)/shard_map/pallas_call | solution.py:158
  102.9 1.5 %all-to-all-done.2 = bf16[64,16,128]{2,1,0:T(8,128)(2,1)S(1)} async-done(((bf16[64,16,128]{2,1,0:T(8,128)(2,1)}), bf16[64,16,128]{2,1,0:T(8,128)(2,1)S(1)}, u32[]{:S(2)}, u32[]{:S(2)}) %all-to-all-start.2) | async-done | bytes 262176 | tf_op jit(solution)/shard_map/all_to_all | solution.py:389
  104.4 0.1 convert_reduce_fusion.r0
  104.5 2.2 %collective-permute-start.15 = (f32[16,128]{1,0:T(8,128)S(1)}, f32[16,128]{1,0:T(8,128)S(1)}, u32[]{:S(2)}, u32[]{:S(2)}) collective-permute-start(f32[16,128]{1,0:T(8,128)S(1)} %convert_reduce_fusion.r0), channel_id=1, source_target_pairs={{0,3},{1,2},{2,1},{3,0},{4,7},{5,6},{6,5},{7,4},{8,11},{9,10},{10,... | collective-permute-start | bytes 24584 | tf_op jit(solution)/shard_map/ppermute | solution.py:39
  106.6 1.3 collective-permute-start.14
  107.9 0.1 collective-permute-done.15.r3
  108.0 1.3 collective-permute-done.14.r2
  109.3 1.2 copy-done.4
  110.5 1.4 %shard_map.69 = (bf16[16,128,128]{2,1,0:T(8,128)(2,1)S(1)}, bf16[8,128,128]{2,1,0:T(8,128)(2,1)S(1)}, bf16[8,128,128]{2,1,0:T(8,128)(2,1)S(1)}) custom-call(s32[4,4]{1,0:T(4,128)S(1)} %copy-done.8, s32[4,4]{1,0:T(4,128)S(1)} %copy-done.7, f32[16,128]{1,0:T(8,128)S(1)} %convert_reduce_fusion.r0, f32[16,128]{1,0:T(8,128)S(1)} %collective-permute-done.13.r1, ...), custom_call_target="tpu_custom_call" | custom-call | flops 100000000 | bytes 3000000 | tf_op jit(solution)/shard_map/pallas_call | solution.py:195
  111.9 2.2 %collective-permute-start.16 = (bf16[8,128,128]{2,1,0:T(8,128)(2,1)S(1)}, bf16[8,128,128]{2,1,0:T(8,128)(2,1)S(1)}, u32[]{:S(2)}, u32[]{:S(2)}) collective-permute-start(bf16[8,128,128]{2,1,0:T(8,128)(2,1)S(1)} %get-tuple-element.39), channel_id=1, source_target_pairs={{0,4},{4,8},{8,12},{12,16},{16,20},{20,24},{24,28},{28,32},{32,36}... | collective-permute-start | bytes 786440 | tf_op jit(solution)/shard_map/ppermute | solution.py:34
  114.1 5.0 %collective-permute-start.17 = (bf16[8,128,128]{2,1,0:T(8,128)(2,1)S(1)}, bf16[8,128,128]{2,1,0:T(8,128)(2,1)S(1)}, u32[]{:S(2)}, u32[]{:S(2)}) collective-permute-start(bf16[8,128,128]{2,1,0:T(8,128)(2,1)S(1)} %get-tuple-element.40), channel_id=1, source_target_pairs={{0,252},{4,0},{8,4},{12,8},{16,12},{20,16},{24,20},{28,24},{32,28}... | collective-permute-start | bytes 786440 | tf_op jit(solution)/shard_map/ppermute | solution.py:34
  119.2 5.3 %collective-permute-done.16.from_before = bf16[8,128,128]{2,1,0:T(8,128)(2,1)S(1)} collective-permute-done((bf16[8,128,128]{2,1,0:T(8,128)(2,1)S(1)}, bf16[8,128,128]{2,1,0:T(8,128)(2,1)S(1)}, u32[]{:S(2)}, u32[]{:S(2)}) %collective-permute-start.16) | collective-permute-done | bytes 262176 | tf_op jit(solution)/shard_map/ppermute | solution.py:34
  124.5 1.7 %collective-permute-done.17.from_after = bf16[8,128,128]{2,1,0:T(8,128)(2,1)S(1)} collective-permute-done((bf16[8,128,128]{2,1,0:T(8,128)(2,1)S(1)}, bf16[8,128,128]{2,1,0:T(8,128)(2,1)S(1)}, u32[]{:S(2)}, u32[]{:S(2)}) %collective-permute-start.17) | collective-permute-done | bytes 262176 | tf_op jit(solution)/shard_map/ppermute | solution.py:34
  126.2 1.7 %shard_map.70 = bf16[16,128,128]{2,1,0:T(8,128)(2,1)} custom-call(s32[4,4]{1,0:T(4,128)S(1)} %get-tuple-element.53.kind, s32[4,4]{1,0:T(4,128)S(1)} %get-tuple-element.51.index, f32[4,4]{1,0:T(4,128)S(1)} %get-tuple-element.44.signs, bf16[16,128,128]{2,1,0:T(8,128)(2,1)S(1)} %get-tuple-element.38.w, ...), custom_call_target="tpu_custom_call" | custom-call | flops 10000000 | bytes 3000000 | tf_op jit(solution)/shard_map/pallas_call | solution.py:343
  (37 shorter events, 0.1 us)
Async XLA Ops:
  0.0 5.5 %copy-start = (bf16[4,24,512]{2,1,0:T(8,128)(2,1)S(1)}, bf16[4,24,512]{2,1,0:T(8,128)(2,1)}, u32[]{:S(2)}) copy-start(bf16[4,24,512]{2,1,0:T(8,128)(2,1)} %param.8) | copy-start | bytes 294916
  0.0 12.8 %collective-permute-start.1 = (bf16[4,512,128]{2,1,0:T(8,128)(2,1)}, bf16[4,512,128]{2,1,0:T(8,128)(2,1)S(1)}, u32[]{:S(2)}, u32[]{:S(2)}) collective-permute-start(bf16[4,512,128]{2,1,0:T(8,128)(2,1)} %refs_4_.1), channel_id=1, source_target_pairs={{0,2},{1,3},{2,0},{3,1},{4,6},{5,7},{6,4},{7,5},{8,10},{9,11},{10,... | collective-permute-start | bytes 1572872 | tf_op jit(solution)/shard_map/ppermute | solution.py:39
  2.8 32.1 %copy-start.14 = (f32[4,16]{1,0:T(4,128)}, f32[4,16]{1,0:T(4,128)S(1)}, u32[]{:S(2)}) copy-start(f32[4,16]{1,0:T(4,128)S(1)} %compare_select_fusion.2.refs_2_) | copy-start | bytes 772
  5.9 29.0 %copy-start.1 = (bf16[4,64,512]{2,1,0:T(8,128)(2,1)}, bf16[4,64,512]{2,1,0:T(8,128)(2,1)S(1)}, u32[]{:S(2)}) copy-start(bf16[4,64,512]{2,1,0:T(8,128)(2,1)S(1)} %convolution_convert_fusion.refs_8_.coupling) | copy-start | bytes 786436
  8.0 11.2 %all-to-all-start = ((f32[4,192,128]{2,1,0:T(8,128)}), f32[4,192,128]{2,1,0:T(8,128)S(1)}, u32[]{:S(2)}, u32[]{:S(2)}) async-start(f32[4,192,128]{2,1,0:T(8,128)} %pad_maximum_fusion.1), calls=%async_computation | async-start | bytes 786432 | tf_op jit(solution)/shard_map/all_to_all | solution.py:406
  12.7 22.2 %collective-permute-start = (bf16[4,512,128]{2,1,0:T(8,128)(2,1)}, bf16[4,512,128]{2,1,0:T(8,128)(2,1)S(1)}, u32[]{:S(2)}, u32[]{:S(2)}) collective-permute-start(bf16[4,512,128]{2,1,0:T(8,128)(2,1)} %refs_4_.1), channel_id=1, source_target_pairs={{0,1},{1,0},{2,3},{3,2},{4,5},{5,4},{6,7},{7,6},{8,9},{9,8},{10,11... | collective-permute-start | bytes 1572872 | tf_op jit(solution)/shard_map/ppermute | solution.py:39
  12.8 22.1 %copy-start.10 = (bf16[4,512,128]{2,1,0:T(8,128)(2,1)}, bf16[4,512,128]{2,1,0:T(8,128)(2,1)S(1)}, u32[]{:S(2)}) copy-start(bf16[4,512,128]{2,1,0:T(8,128)(2,1)S(1)} %collective-permute-done.1.refs_6_) | copy-start | bytes 1572868
  12.8 22.0 %collective-permute-start.2 = (bf16[4,512,128]{2,1,0:T(8,128)(2,1)S(1)}, bf16[4,512,128]{2,1,0:T(8,128)(2,1)S(1)}, u32[]{:S(2)}, u32[]{:S(2)}) collective-permute-start(bf16[4,512,128]{2,1,0:T(8,128)(2,1)S(1)} %collective-permute-done.1.refs_6_), channel_id=1, source_target_pairs={{0,1},{1,0},{2,3},{3,2},{4,5},{5,4},{6,7},{7,6},{8,9},{9,8},{10,11... | collective-permute-start | bytes 1572872 | tf_op jit(solution)/shard_map/ppermute | solution.py:39
  20.4 30.1 %all-to-all-start.1 = ((bf16[64,16,128]{2,1,0:T(8,128)(2,1)}), bf16[64,16,128]{2,1,0:T(8,128)(2,1)S(1)}, u32[]{:S(2)}, u32[]{:S(2)}) async-start(bf16[64,16,128]{2,1,0:T(8,128)(2,1)} %bitcast.3), calls=%async_computation.1 | async-start | bytes 524288 | tf_op jit(solution)/shard_map/all_to_all | solution.py:389
  34.8 0.8 copy-start.12
  34.9 1.0 copy-start.13
  43.2 20.3 %collective-permute-start.3 = (bf16[8,192,128]{2,1,0:T(8,128)(2,1)}, bf16[8,192,128]{2,1,0:T(8,128)(2,1)S(1)}, u32[]{:S(2)}, u32[]{:S(2)}) collective-permute-start(bf16[8,192,128]{2,1,0:T(8,128)(2,1)} %get-tuple-element.23), channel_id=1, source_target_pairs={{0,4},{4,8},{8,12},{12,16},{16,20},{20,24},{24,28},{28,32},{32,36}... | collective-permute-start | bytes 1179656 | tf_op jit(solution)/shard_map/ppermute | solution.py:34
  45.8 17.7 %collective-permute-start.4 = (bf16[8,192,128]{2,1,0:T(8,128)(2,1)}, bf16[8,192,128]{2,1,0:T(8,128)(2,1)S(1)}, u32[]{:S(2)}, u32[]{:S(2)}) collective-permute-start(bf16[8,192,128]{2,1,0:T(8,128)(2,1)} %get-tuple-element.24), channel_id=1, source_target_pairs={{0,252},{4,0},{8,4},{12,8},{16,12},{20,16},{24,20},{28,24},{32,28}... | collective-permute-start | bytes 1179656 | tf_op jit(solution)/shard_map/ppermute | solution.py:34
  50.6 13.0 %collective-permute-start.6 = (f32[16,128]{1,0:T(8,128)S(1)}, f32[16,128]{1,0:T(8,128)S(1)}, u32[]{:S(2)}, u32[]{:S(2)}) collective-permute-start(f32[16,128]{1,0:T(8,128)S(1)} %convert_reduce_fusion.1.r1), channel_id=1, source_target_pairs={{0,252},{4,0},{8,4},{12,8},{16,12},{20,16},{24,20},{28,24},{32,28}... | collective-permute-start | bytes 24584 | tf_op jit(solution)/shard_map/ppermute | solution.py:34
  53.5 10.1 %collective-permute-start.5 = (f32[16,128]{1,0:T(8,128)S(1)}, f32[16,128]{1,0:T(8,128)S(1)}, u32[]{:S(2)}, u32[]{:S(2)}) collective-permute-start(f32[16,128]{1,0:T(8,128)S(1)} %convert_reduce_fusion.1.r1), channel_id=1, source_target_pairs={{0,4},{4,8},{8,12},{12,16},{16,20},{20,24},{24,28},{28,32},{32,36}... | collective-permute-start | bytes 24584 | tf_op jit(solution)/shard_map/ppermute | solution.py:34
  63.6 1.0 copy-start.2
  64.5 1.2 copy-start.5
  76.8 32.4 %copy-start.3 = (bf16[4,64,512]{2,1,0:T(8,128)(2,1)S(1)}, bf16[4,64,512]{2,1,0:T(8,128)(2,1)}, u32[]{:S(2)}) copy-start(bf16[4,64,512]{2,1,0:T(8,128)(2,1)} %copy-done.1) | copy-start | bytes 786436
  76.8 32.4 %copy-start.7 = (s32[4,4]{1,0:T(4,128)S(1)}, s32[4,4]{1,0:T(4,128)}, u32[]{:S(2)}) copy-start(s32[4,4]{1,0:T(4,128)} %get-tuple-element.49.refs_1_.before) | copy-start | bytes 196
  76.8 32.4 %copy-start.8 = (s32[4,4]{1,0:T(4,128)S(1)}, s32[4,4]{1,0:T(4,128)}, u32[]{:S(2)}) copy-start(s32[4,4]{1,0:T(4,128)} %get-tuple-element.50.refs_0_.after) | copy-start | bytes 196
  78.1 17.2 %copy-start.6 = (bf16[16,128,128]{2,1,0:T(8,128)(2,1)}, bf16[16,128,128]{2,1,0:T(8,128)(2,1)S(1)}, u32[]{:S(2)}) copy-start(bf16[16,128,128]{2,1,0:T(8,128)(2,1)S(1)} %get-tuple-element.35) | copy-start | bytes 1572868
  78.1 13.4 %collective-permute-start.8 = (bf16[4,512,128]{2,1,0:T(8,128)(2,1)S(1)}, bf16[4,512,128]{2,1,0:T(8,128)(2,1)S(1)}, u32[]{:S(2)}, u32[]{:S(2)}) collective-permute-start(bf16[4,512,128]{2,1,0:T(8,128)(2,1)S(1)} %bitcast.18), channel_id=1, source_target_pairs={{0,2},{1,3},{2,0},{3,1},{4,6},{5,7},{6,4},{7,5},{8,10},{9,11},{10,... | collective-permute-start | bytes 1572872 | tf_op jit(solution)/shard_map/ppermute | solution.py:39
  78.8 16.6 %collective-permute-start.7 = (bf16[4,512,128]{2,1,0:T(8,128)(2,1)S(1)}, bf16[4,512,128]{2,1,0:T(8,128)(2,1)S(1)}, u32[]{:S(2)}, u32[]{:S(2)}) collective-permute-start(bf16[4,512,128]{2,1,0:T(8,128)(2,1)S(1)} %bitcast.19), channel_id=1, source_target_pairs={{0,1},{1,0},{2,3},{3,2},{4,5},{5,4},{6,7},{7,6},{8,9},{9,8},{10,11... | collective-permute-start | bytes 1572872 | tf_op jit(solution)/shard_map/ppermute | solution.py:39
  79.2 25.1 %all-to-all-start.2 = ((bf16[64,16,128]{2,1,0:T(8,128)(2,1)}), bf16[64,16,128]{2,1,0:T(8,128)(2,1)S(1)}, u32[]{:S(2)}, u32[]{:S(2)}) async-start(bf16[64,16,128]{2,1,0:T(8,128)(2,1)} %bitcast.5), calls=%async_computation.2 | async-start | bytes 524288 | tf_op jit(solution)/shard_map/all_to_all | solution.py:389
  91.5 3.8 %copy-start.9 = (bf16[4,512,128]{2,1,0:T(8,128)(2,1)}, bf16[4,512,128]{2,1,0:T(8,128)(2,1)S(1)}, u32[]{:S(2)}) copy-start(bf16[4,512,128]{2,1,0:T(8,128)(2,1)S(1)} %collective-permute-done.8.refs_3_) | copy-start | bytes 1572868
  91.5 2.0 %collective-permute-start.9 = (bf16[1,512,128]{2,1,0:T(8,128)(2,1)S(1)}, bf16[1,512,128]{2,1,0:T(8,128)(2,1)S(1)}, u32[]{:S(2)}, u32[]{:S(2)}) collective-permute-start(bf16[1,512,128]{2,1,0:T(8,128)(2,1)S(1)} %get-tuple-element.45), channel_id=1, source_target_pairs={{0,1},{1,0},{2,3},{3,2},{4,5},{5,4},{6,7},{7,6},{8,9},{9,8},{10,11... | collective-permute-start | bytes 393224 | tf_op jit(solution)/shard_map/ppermute | solution.py:39
  92.6 1.3 %collective-permute-start.12 = (bf16[1,512,128]{2,1,0:T(8,128)(2,1)S(1)}, bf16[1,512,128]{2,1,0:T(8,128)(2,1)S(1)}, u32[]{:S(2)}, u32[]{:S(2)}) collective-permute-start(bf16[1,512,128]{2,1,0:T(8,128)(2,1)S(1)} %get-tuple-element.46), channel_id=1, source_target_pairs={{0,1},{1,0},{2,3},{3,2},{4,5},{5,4},{6,7},{7,6},{8,9},{9,8},{10,11... | collective-permute-start | bytes 393224 | tf_op jit(solution)/shard_map/ppermute | solution.py:39
  92.7 1.4 %collective-permute-start.11 = (bf16[1,512,128]{2,1,0:T(8,128)(2,1)S(1)}, bf16[1,512,128]{2,1,0:T(8,128)(2,1)S(1)}, u32[]{:S(2)}, u32[]{:S(2)}) collective-permute-start(bf16[1,512,128]{2,1,0:T(8,128)(2,1)S(1)} %get-tuple-element.47), channel_id=1, source_target_pairs={{0,1},{1,0},{2,3},{3,2},{4,5},{5,4},{6,7},{7,6},{8,9},{9,8},{10,11... | collective-permute-start | bytes 393224 | tf_op jit(solution)/shard_map/ppermute | solution.py:39
  93.1 1.3 %collective-permute-start.10 = (bf16[1,512,128]{2,1,0:T(8,128)(2,1)S(1)}, bf16[1,512,128]{2,1,0:T(8,128)(2,1)S(1)}, u32[]{:S(2)}, u32[]{:S(2)}) collective-permute-start(bf16[1,512,128]{2,1,0:T(8,128)(2,1)S(1)} %get-tuple-element.48), channel_id=1, source_target_pairs={{0,1},{1,0},{2,3},{3,2},{4,5},{5,4},{6,7},{7,6},{8,9},{9,8},{10,11... | collective-permute-start | bytes 393224 | tf_op jit(solution)/shard_map/ppermute | solution.py:39
  95.4 0.8 copy-start.11
  104.5 3.5 %collective-permute-start.15 = (f32[16,128]{1,0:T(8,128)S(1)}, f32[16,128]{1,0:T(8,128)S(1)}, u32[]{:S(2)}, u32[]{:S(2)}) collective-permute-start(f32[16,128]{1,0:T(8,128)S(1)} %convert_reduce_fusion.r0), channel_id=1, source_target_pairs={{0,3},{1,2},{2,1},{3,0},{4,7},{5,6},{6,5},{7,4},{8,11},{9,10},{10,... | collective-permute-start | bytes 24584 | tf_op jit(solution)/shard_map/ppermute | solution.py:39
  106.6 2.6 %collective-permute-start.14 = (f32[16,128]{1,0:T(8,128)S(1)}, f32[16,128]{1,0:T(8,128)S(1)}, u32[]{:S(2)}, u32[]{:S(2)}) collective-permute-start(f32[16,128]{1,0:T(8,128)S(1)} %convert_reduce_fusion.r0), channel_id=1, source_target_pairs={{0,2},{1,3},{2,0},{3,1},{4,6},{5,7},{6,4},{7,5},{8,10},{9,11},{10,... | collective-permute-start | bytes 24584 | tf_op jit(solution)/shard_map/ppermute | solution.py:39
  107.9 1.3 %collective-permute-start.13 = (f32[16,128]{1,0:T(8,128)S(1)}, f32[16,128]{1,0:T(8,128)S(1)}, u32[]{:S(2)}, u32[]{:S(2)}) collective-permute-start(f32[16,128]{1,0:T(8,128)S(1)} %convert_reduce_fusion.r0), channel_id=1, source_target_pairs={{0,1},{1,0},{2,3},{3,2},{4,5},{5,4},{6,7},{7,6},{8,9},{9,8},{10,11... | collective-permute-start | bytes 24584 | tf_op jit(solution)/shard_map/ppermute | solution.py:39
  109.3 1.2 copy-start.4
  111.9 12.6 %collective-permute-start.16 = (bf16[8,128,128]{2,1,0:T(8,128)(2,1)S(1)}, bf16[8,128,128]{2,1,0:T(8,128)(2,1)S(1)}, u32[]{:S(2)}, u32[]{:S(2)}) collective-permute-start(bf16[8,128,128]{2,1,0:T(8,128)(2,1)S(1)} %get-tuple-element.39), channel_id=1, source_target_pairs={{0,4},{4,8},{8,12},{12,16},{16,20},{20,24},{24,28},{28,32},{32,36}... | collective-permute-start | bytes 786440 | tf_op jit(solution)/shard_map/ppermute | solution.py:34
  114.1 12.1 %collective-permute-start.17 = (bf16[8,128,128]{2,1,0:T(8,128)(2,1)S(1)}, bf16[8,128,128]{2,1,0:T(8,128)(2,1)S(1)}, u32[]{:S(2)}, u32[]{:S(2)}) collective-permute-start(bf16[8,128,128]{2,1,0:T(8,128)(2,1)S(1)} %get-tuple-element.40), channel_id=1, source_target_pairs={{0,252},{4,0},{8,4},{12,8},{16,12},{20,16},{24,20},{28,24},{32,28}... | collective-permute-start | bytes 786440 | tf_op jit(solution)/shard_map/ppermute | solution.py:34
